TPU v7x, 128 devices: a whole 4x4x4 slice. The times are simulated.
128 devices in a mesh: dp: 16 (over y, x_hi, core), row: 4 (over z), col: 2 (over x_lo).
Axes of the slice: x: 4 (x_hi: 2, x_lo: 2; x = x_hi * 2 + x_lo), y: 4, z: 4, core: 2. Of those that a mesh axis runs over, the one named last changes fastest.
Arguments:
- inputs: bfloat16 [12288, 2048], P('dp', 'col')
- segments: int32 [12288], P('dp'), may hold values from 0 to 2, as said below
- w_query: bfloat16 [2048, 2048], P('col', 'row')
- w_key: bfloat16 [2048, 2048], P('col', 'row')
- w_value: bfloat16 [2048, 2048], P('col', 'row'), may hold values from -0.125 to 0.125
- w_mix: bfloat16 [2048, 2048], P('row', 'col')
- w_gate: bfloat16 [2048, 8192], P('col', 'row'), may hold values from -0.125 to 0.125
- w_up: bfloat16 [2048, 8192], P('col', 'row'), may hold values from -0.125 to 0.125
- w_down: bfloat16 [8192, 2048], P('row', 'col')
- attn_gain: float32 [2048], P('col'), may hold values from 0.25 to 1.75
- ffn_gain: float32 [2048], P('col'), may hold values from 0.25 to 1.75
- query_gain: float32 [2048], P(('row', 'col')), may hold values from 0.25 to 1.75
- key_gain: float32 [2048], P(('row', 'col')), may hold values from 0.25 to 1.75
- out_grad: bfloat16 [12288, 2048], P('dp', 'col'), may hold values from -6 to 6
Outputs:
- block_out: bfloat16 [12288, 2048], P('dp', 'col')
- input_grad: float32 [12288, 2048], P('dp', 'col')
- query_grad: float32 [2048, 2048], P(('col', 'dp'), 'row')
- key_grad: float32 [2048, 2048], P(('col', 'dp'), 'row')
- value_grad: float32 [2048, 2048], P(('col', 'dp'), 'row')
- mix_grad: float32 [2048, 2048], P('row', ('col', 'dp'))
- gate_grad: float32 [2048, 8192], P(('col', 'dp'), 'row')
- up_grad: float32 [2048, 8192], P(('col', 'dp'), 'row')
- down_grad: float32 [8192, 2048], P('row', ('col', 'dp'))
- attn_gain_grad: float32 [2048], P(('col', 'dp'))
- ffn_gain_grad: float32 [2048], P(('col', 'dp'))
- query_gain_grad: float32 [2048], P(('row', 'col', 'dp'))
- key_gain_grad: float32 [2048], P(('row', 'col', 'dp'))
Inputs may be any that keep to these rules, and one draw needn't show every extreme that they name: `segments`: within each sequence of 768 tokens the segment numbers start at 0 and never fall; every document holds at least 200 tokens; in every draw one sequence is a single document and another holds 3 documents.
All inputs are finite; a program needn't handle non-finite values.
Results may differ from a plain program's by a relative error of at most 0.028.
Values may be sent and summed in bfloat16 or wider, within the bound.
No kernel may reach another device: no remote copies, remote signals or barrier semaphores. Data moves between devices by JAX's collectives and lax.ppermute only.
A program may use at most 192 MiB of HBM per device.

v0:
```python
import functools

import jax
import jax.numpy as jnp
from jax import lax
from jax.experimental import pallas as pl
from jax.experimental.pallas import tpu as pltpu
from jax.sharding import Mesh, PartitionSpec as P

D = 2048
HEAD = 128
SEQ = 768
NEAR = D // 2
OWN = SEQ // 2
RING = 4
BLOCK = SEQ // 8
EPSILON = 1e-06
ROPE_BASE = 500000.0
MASKED = -1e30
LOW = jnp.bfloat16
F32 = jnp.float32
FREE = pl.CostEstimate(flops=0, bytes_accessed=0, transcendentals=0)
PARAMS = pltpu.CompilerParams(vmem_limit_bytes=24 * 1024 * 1024)
EARLY = pltpu.CompilerParams(vmem_limit_bytes=60 * 1024 * 1024)


def dot(a, b, dims=((1,), (0,))):
    return lax.dot_general(a, b, (dims, ((), ())), preferred_element_type=F32)


NT = ((1,), (1,))
TN = ((0,), (0,))


def after(value, *earlier):
    return lax.optimization_barrier((value, earlier))[0]


def ring_shift(a, axes, step):
    return lax.ppermute(a, axes, [(i, (i + step) % RING) for i in range(RING)])


def z_shift(a, step):
    return ring_shift(a, "z", step)


def plane_shift(a, step, swapped):
    pairs = []
    for y in range(4):
        for x in range(4):
            for c in range(2):
                there = ((y + step) % 4, x) if (c == 0) != swapped else (y, (x + step) % 4)
                xh, xl = x // 2, x % 2
                source = ((y * 2 + xh) * 2 + c) * 2 + xl
                pairs.append((source, ((there[0] * 2 + there[1] // 2) * 2 + c) * 2 + there[1] % 2))
    return lax.ppermute(a, ("y", "xh", "core", "xl"), pairs)


def core_swap(a):
    return lax.ppermute(a, "core", [(0, 1), (1, 0)])


def pair_swap(a):
    return lax.ppermute(a, "xl", [(0, 1), (1, 0)])


def wrap_swap(a):
    return lax.ppermute(a, ("xh", "xl"), [(0, 3), (3, 0), (1, 2), (2, 1)])


def pick(blocks, index, axis=0):
    return lax.dynamic_index_in_dim(blocks, index, axis, keepdims=False)


class Place:
    def __init__(self):
        self.s = lax.axis_index("xl")
        self.xh = lax.axis_index("xh")
        self.x = self.xh * 2 + self.s
        self.y = lax.axis_index("y")
        self.c = lax.axis_index("core")
        self.z = lax.axis_index("z")
        self.home = self.c == self.s
        self.z_scalar = self.z.reshape(1).astype(jnp.int32)
        steps = jnp.arange(RING, dtype=jnp.int32)
        self.back = (self.z - steps) % RING
        self.rows = jnp.concatenate([self.c * 4 + self.back, (1 - self.c) * 4 + self.back])
        first, second = steps[:, None], steps[None, :]
        dx = jnp.where(self.c == 0, second, first)
        dy = jnp.where(self.c == 0, first, second)
        self.columns = (
            (dx % 2) * 8 + ((self.y + dy) % 4) * 2 + ((self.x + dx) % 4) // 2
        ).reshape(-1)
        y, x = first, second
        self.plain = (((x % 2) ^ self.s) * 8 + y * 2 + x // 2).reshape(-1)


def place_kernel(plan, sources, table, *refs):
    ins, outs, sems = refs[:sources], refs[sources:-1], refs[-1]
    copies = []
    for i, (source, there) in enumerate(plan(table, ins, outs)):
        copies.append(pltpu.make_async_copy(source, there, sems.at[i]))
        copies[-1].start()
    for copy in copies:
        copy.wait()


def place(plan, count, shapes, table, *sources, params=PARAMS):
    return pl.pallas_call(
        functools.partial(place_kernel, plan, len(sources)),
        in_specs=[pl.BlockSpec(memory_space=pltpu.SMEM)]
        + [pl.BlockSpec(memory_space=pltpu.HBM)] * len(sources),
        out_specs=tuple(pl.BlockSpec(memory_space=pltpu.VMEM) for _ in shapes),
        out_shape=tuple(jax.ShapeDtypeStruct(shape, LOW) for shape in shapes),
        scratch_shapes=[pltpu.SemaphoreType.DMA((count,))],
        compiler_params=params,
        cost_estimate=FREE,
    )(jnp.stack(table).astype(jnp.int32), *sources)


def at_block(index, size):
    return pl.ds(pl.multiple_of(index * size, size), size)


def first_hop(a):
    return lax.ppermute(a, ("core", "xl"), [(0, 2), (3, 1), (2, 3), (1, 0)])


def second_hop(first):
    return lax.ppermute(first, ("core", "xl"), [(0, 2), (3, 1)])


def sequence_kernel(count, table, a_ref, first_ref, second_ref, out_ref, sems):
    def move(near, far):
        copies = []
        for i in range(count):
            block = at_block(table[i], BLOCK)
            there = pl.ds(i * BLOCK, BLOCK)
            for source, lo in ((near.at[block], 0), (far.at[block], NEAR)):
                copies.append(
                    pltpu.make_async_copy(
                        source, out_ref.at[there, pl.ds(lo, NEAR)], sems.at[len(copies)]
                    )
                )
        for copy in copies:
            copy.start()
        for copy in copies:
            copy.wait()

    pl.when(table[count] == 1)(functools.partial(move, a_ref, first_ref))
    pl.when(table[count] == 0)(functools.partial(move, first_ref, second_ref))


def to_sequence(at, a, first, second, count=8):
    table = jnp.concatenate([at.rows[:count], at.home[None].astype(jnp.int32)])
    return pl.pallas_call(
        functools.partial(sequence_kernel, count),
        in_specs=[pl.BlockSpec(memory_space=pltpu.SMEM)]
        + [pl.BlockSpec(memory_space=pltpu.HBM)] * 3,
        out_specs=pl.BlockSpec(memory_space=pltpu.VMEM),
        out_shape=jax.ShapeDtypeStruct((count * BLOCK, D), LOW),
        scratch_shapes=[pltpu.SemaphoreType.DMA((2 * count,))],
        compiler_params=PARAMS,
        cost_estimate=FREE,
    )(table.astype(jnp.int32), a, first, second)


def order_rows(at, sources, index, which):
    joined = jnp.concatenate(sources) if len(sources) > 1 else sources[0]
    rows = sources[0].shape[0] // BLOCK

    def plan(table, ins, outs):
        return [
            (ins[0].at[at_block(table[i], BLOCK)], outs[0].at[pl.ds(i * BLOCK, BLOCK)])
            for i in range(8)
        ]

    table = index + rows * which if len(sources) > 1 else index * 2 + which
    return place(plan, 8, [(SEQ, joined.shape[1])], list(table), joined)[0]


def cut_columns(at, heights, *weights):
    width = weights[0].shape[1] // 2
    starts = [sum(heights[:i]) for i in range(len(heights))]

    def plan(table, ins, outs):
        return [
            (
                ref.at[pl.ds(start, height), at_block(table[0], width)],
                out.at[:, pl.ds(width * i, width)],
            )
            for i, ref in enumerate(ins)
            for start, height, out in zip(starts, heights, outs)
        ]

    shapes = [(height, width * len(weights)) for height in heights]
    return place(plan, len(heights) * len(weights), shapes, [at.c], *weights, params=EARLY)


PIECES = (
    (("gate", 0),), (("gate", 1),),
    (("gate", 2), ("up", 0)), (("gate", 3), ("up", 1)),
    (("up", 2), ("down", 0)), (("up", 3), ("down", 1)),
    (("down", 2),), (("down", 3),),
)
PART = 256


def cut_pieces(at, w_gate, w_up, w_down):
    def plan(table, ins, outs):
        named = dict(zip(("gate", "up", "down"), ins))
        copies = []
        for out, piece in zip(outs, PIECES):
            for i, (name, part) in enumerate(piece):
                if name == "down":
                    rows = pl.ds(pl.multiple_of(table[0] * NEAR + PART * part, PART), PART)
                    source = named[name].at[rows]
                else:
                    source = named[name].at[pl.ds(PART * part, PART), at_block(table[0], NEAR)]
                copies.append((source, out.at[pl.ds(PART * i, PART)]))
        return copies

    shapes = [(PART * len(piece), NEAR) for piece in PIECES]
    return place(plan, 12, shapes, [at.c], w_gate, w_up, w_down, params=EARLY)


def pieces_with(name):
    return [k for k, piece in enumerate(PIECES) if name in dict(piece)]


def views(name, refs):
    out = []
    for ref, k in zip(refs, pieces_with(name)):
        for i, (found, _) in enumerate(PIECES[k]):
            if found == name:
                out.append(ref.at[pl.ds(PART * i, PART)])
    return out


def join_columns(parts):
    starts = [sum(part.shape[1] for part in parts[:i]) for i in range(len(parts) + 1)]

    def plan(table, ins, outs):
        return [
            (ref, outs[0].at[:, pl.ds(starts[i], parts[i].shape[1])]) for i, ref in enumerate(ins)
        ]

    return place(plan, len(parts), [(D, starts[-1])], [0], *parts)[0]


def fetch(first, second):
    return pair_swap(first), wrap_swap(second)


def scatter_z(parts):
    total = parts[0]
    for i in range(1, RING):
        total = total + z_shift(parts[i], -i).astype(F32)
    return total


def gather_z(rows):
    return [rows] + [z_shift(rows, i) for i in range(1, RING)]


def all_stats(pair):
    theirs = core_swap(pair)
    pair = pair + jnp.concatenate([theirs[:, OWN:], theirs[:, :OWN]], axis=1)
    total = pair
    for i in range(1, RING):
        came, cut = z_shift(pair, i), OWN - i * BLOCK
        total = total + jnp.concatenate(
            [came[:, cut:OWN], came[:, :cut], came[:, OWN + cut :], came[:, OWN : OWN + cut]],
            axis=1,
        )
    return total


def plane_sum(own, came):
    total = own.astype(F32) + came[0].astype(F32) + came[1].astype(F32) + came[2].astype(F32)
    total = lax.optimization_barrier(total.astype(LOW))
    height = own.shape[0] // RING
    return [total[height * i : height * (i + 1)] for i in range(RING)]


def share_kernel(core, p0, p1, p2, p3, own_ref, sent_ref):
    total = p0[...].astype(F32) + p1[...].astype(F32) + p2[...].astype(F32) + p3[...].astype(F32)
    flip = core[0] == 1
    for i in range(total.shape[0] // 128):
        at = slice(64 * i, 64 * (i + 1))
        low, high = total[128 * i : 128 * i + 64, :], total[128 * i + 64 : 128 * (i + 1), :]
        own_ref[at, :] = jnp.where(flip, high, low)
        sent_ref[at, :] = jnp.where(flip, low, high).astype(LOW)
    rest = total.shape[0] % 128
    if rest:
        own_ref[-rest:, :] = total[-rest:, :]
        sent_ref[-rest:, :] = total[-rest:, :].astype(LOW)


def wide_kernel(plan, core, own_ref, came_ref, *outs):
    first = core[0] == 0
    own, came = own_ref[...], came_ref[...].astype(F32)
    sides = jnp.where(first, own, came), jnp.where(first, came, own)
    for i, (out, pieces) in enumerate(zip(outs, plan)):
        at = 0
        for side in sides:
            for rows, start, width in pieces:
                value = side[64 * rows : 64 * (rows + 1), start : start + width]
                if i == len(plan) - 1:
                    out[at : at + width, :] = value.T
                else:
                    out[:, at : at + width] = value
                at += width
    if len(outs) > len(plan):
        width_ref, heads_ref = outs[len(plan) :]
        zero, one = (side[-16:-8, :128] for side in sides)
        width_ref[...] = zero + one
        heads_ref[0:8, :] = zero
        heads_ref[8:16, :] = one


def share_cores(at, own, came, plan, extra=()):
    height, width = own.shape
    shape = (height // 128 * 64 + height % 128, width)
    core = at.c.reshape(1).astype(jnp.int32)
    own, sent = call(share_kernel, [(shape, F32), (shape, LOW)], core, own, *came, scalars=1)
    widths = [2 * sum(piece[2] for piece in pieces) for pieces in plan]
    shapes = [((64, width), F32) for width in widths[:-1]] + [((widths[-1], 64), F32)]
    shapes += [(shape, F32) for shape in extra]
    return call(functools.partial(wide_kernel, plan), shapes, core, own, core_swap(sent), scalars=1)


def call(kernel, shapes, *args, scratch=(), scalars=0):
    return pl.pallas_call(
        kernel,
        in_specs=[
            pl.BlockSpec(memory_space=pltpu.SMEM if i < scalars else pltpu.VMEM)
            for i in range(len(args))
        ],
        out_shape=tuple(jax.ShapeDtypeStruct(shape, dtype) for shape, dtype in shapes),
        scratch_shapes=list(scratch),
        compiler_params=PARAMS,
        cost_estimate=FREE,
    )(*args)


def row_dot(rows, refs, at):
    value = 0.0
    start = 0
    for ref in refs:
        height = ref.shape[0]
        value += dot(rows[:, start : start + height], ref[:, at])
        start += height
    return value


def strips(width, size):
    return [slice(i, i + size) for i in range(0, width, size)]


def as_rows(first, second):
    return jnp.concatenate([first, second, jnp.zeros((SEQ, 6), F32)], axis=1).T


def qkv_kernel(states_ref, *refs):
    *blocks, qkv_ref, sums_ref = refs
    sums = []
    for at in strips(SEQ, 256):
        value = row_dot(states_ref, blocks, at)
        qkv_ref[:, at] = value
        sums.append(jnp.sum(value * value, axis=1, keepdims=True))
    sums_ref[...] = as_rows(*sums[:2])


def product_kernel(body, *refs):
    *refs, out_ref = refs
    for at, value in body(refs):
        out_ref[:, at] = value.astype(out_ref.dtype)


def product(body, dtype, *args):
    return call(functools.partial(product_kernel, body), [((OWN, D), dtype)], *args)[0]


def half_rows(ref, half):
    return ref[OWN * half : OWN * (half + 1), :]


def mix(left, half, near, far, dtype):
    def body(refs):
        left, near, far = refs
        left = half_rows(left, half)
        for at in strips(NEAR, 512):
            yield at, dot(left, near[:, at])
            yield slice(NEAR + at.start, NEAR + at.stop), dot(left, far[:, at])

    return product(body, dtype, left, near, far)


def down(units, pieces, dtype):
    count = len(pieces) // 2

    def body(refs):
        units, *w = refs
        for i in range(2):
            blocks = views("down", w[count * i : count * (i + 1)])
            for at in strips(NEAR, 512):
                yield slice(NEAR * i + at.start, NEAR * i + at.stop), row_dot(units, blocks, at)

    return product(body, dtype, units, *pieces)


def pair_down(gate_back, up_back, gates, ups, dtype):
    def body(refs):
        gate_back, up_back, *w = refs
        for i in range(2):
            n, m = len(gates) // 2, len(ups) // 2
            gate = views("gate", w[n * i : n * (i + 1)])
            up = views("up", w[2 * n + m * i : 2 * n + m * (i + 1)])
            for k in range(4):
                value = dot(gate_back[...], gate[k][...], NT) + dot(up_back[...], up[k][...], NT)
                yield slice(NEAR * i + PART * k, NEAR * i + PART * (k + 1)), value

    return product(body, dtype, gate_back, up_back, *gates, *ups)


def qkv_down(back, half, blocks, dtype):
    def body(refs):
        back, *w = refs
        back = half_rows(back, half)
        start = 0
        for ref in w:
            for at in strips(ref.shape[0], 256):
                yield slice(start + at.start, start + at.stop), dot(back, ref[at, :], NT)
            start += ref.shape[0]

    return product(body, dtype, back, *blocks)


def settle_kernel(own_ref, came_ref, *outs):
    for i, ref in enumerate(outs):
        at = slice(i * BLOCK, (i + 1) * BLOCK)
        ref[...] = (own_ref[at, :] + came_ref[at, :].astype(F32)).astype(ref.dtype)


def settle(own, came):
    return call(
        settle_kernel, [((BLOCK, D), F32)] + [((BLOCK, D), LOW)] * 3, own, came
    )


def z_rows(z, i):
    return pl.ds(pl.multiple_of(lax.rem(z + RING - i, RING) * BLOCK, BLOCK), BLOCK)


def settle_ordered_kernel(z_ref, own_ref, came_ref, out_ref):
    for i in range(RING):
        at = slice(i * BLOCK, (i + 1) * BLOCK)
        value = own_ref[at, :] + came_ref[at, :].astype(F32)
        out_ref[z_rows(z_ref[0], i), :] = value.astype(LOW)


def settle_ordered(at, own, came):
    return call(settle_ordered_kernel, [((OWN, D), LOW)], at.z_scalar, own, came, scalars=1)[0]


def units_kernel(n, m, rows_ref, *refs):
    gate_ref, up_ref, units_ref = refs[-3:]
    gates = views("gate", refs[:n]) + views("gate", refs[n : 2 * n])
    ups = views("up", refs[2 * n : 2 * n + m]) + views("up", refs[2 * n + m : 2 * n + 2 * m])
    for at in strips(1024, 512):
        gate, up = row_dot(rows_ref, gates, at), row_dot(rows_ref, ups, at)
        gate_ref[:, at] = gate.astype(LOW)
        up_ref[:, at] = up.astype(LOW)
        units_ref[:, at] = (gate * jax.nn.sigmoid(gate) * up).astype(LOW)


def units_of(rows, gates, ups):
    kernel = functools.partial(units_kernel, len(gates) // 2, len(ups) // 2)
    return call(kernel, [((OWN, 1024), LOW)] * 3, rows, *gates, *ups)


def units_back_kernel(branch_ref, *refs):
    *w, gate_ref, up_ref, gate_back_ref, up_back_ref = refs
    count = len(w) // 2
    near, far = views("down", w[:count]), views("down", w[count:])
    for k in range(4):
        at = slice(PART * k, PART * (k + 1))
        grad = dot(branch_ref[:, :NEAR], near[k][...], NT)
        grad += dot(branch_ref[:, NEAR:], far[k][...], NT)
        gate, up = gate_ref[:, at].astype(F32), up_ref[:, at].astype(F32)
        sigmoid = jax.nn.sigmoid(gate)
        gate_back_ref[:, at] = (grad * up * sigmoid * (1.0 + gate * (1.0 - sigmoid))).astype(LOW)
        up_back_ref[:, at] = (grad * gate * sigmoid).astype(LOW)


def units_back(branch, pieces, gate, up):
    return call(units_back_kernel, [((OWN, 1024), LOW)] * 2, branch, *pieces, gate, up)


def grad_kernel(plan, count, extras, cut, *refs):
    table, ins = refs[0], refs[1 : 1 + count]
    extra, outs = refs[1 + count : 1 + count + extras], refs[1 + count + extras :]
    if cut:
        outs = [(outs[0],), outs[1:3], (outs[3],), outs[4:6]]
    for d in range(RING):
        blocks = [table[4 * d + e] for e in range(RING)]
        places = [at_block(block, 128) for block in blocks]
        start = 0
        for lo, width, terms in plan:
            value = 0.0
            for left, right, row in terms:
                left, right = ins[left], ins[right]
                chosen = jnp.concatenate([left[:, place] for place in places], axis=1)
                value += dot(chosen, right[row : row + left.shape[0], lo : lo + width], TN)
            value = value.astype(LOW)
            at = slice(start, start + width)
            if cut:
                put_columns(outs[d], start, value)
            elif not extras:
                outs[d][:, at] = value
            else:
                for e in range(RING):
                    outs[d][144 * e : 144 * e + 128, at] = value[128 * e : 128 * (e + 1)]
            start += width
        if extras:
            attn_ref, ffn_ref, heads_ref = extra
            for e in range(RING):
                block = lax.rem(blocks[e], 8)
                rows = [attn_ref[0:1, places[e]], ffn_ref[0:1, places[e]]]
                rows += [heads_ref[pl.ds(block + 8 * i, 1), :] for i in range(2)]
                rows = jnp.concatenate([*rows, jnp.zeros((12, 128), F32)])
                at = slice(144 * e + 128, 144 * (e + 1))
                outs[d][at, :128] = rows.astype(LOW)
                outs[d][at, 128:] = jnp.zeros((16, start - 128), LOW)


def put_columns(outs, start, value):
    at = 0
    for out in outs:
        lo, hi = max(start, at), min(start + value.shape[1], at + out.shape[1])
        if lo < hi:
            out[:, lo - at : hi - at] = value[:, lo - start : hi - start]
        at += out.shape[1]


def weight_grad(table, arrays, plan, extra=(), cut=False):
    width = sum(span[1] for span in plan)
    height = 576 if extra else 512
    kernel = functools.partial(grad_kernel, plan, len(arrays), len(extra), cut)
    widths = [width, width // 2, width // 2, width, width // 2, width // 2] if cut else [width] * RING
    outs = [((height, w), LOW) for w in widths]
    return call(kernel, outs, table.astype(jnp.int32), *arrays, *extra, scalars=1)


def turn(v, cosines, sines):
    return v * cosines + pltpu.roll(v, HEAD // 2, 1) * sines


def turn_back(v, cosines, sines):
    return v * cosines - pltpu.roll(v, HEAD // 2, 1) * sines


TILE = 256


def seen(table_ref, row_ref, lo):
    here = table_ref[lo : lo + TILE, 2 * HEAD : 3 * HEAD]
    there = row_ref[0:1, :]
    return (there <= here[:, 0:1]) & (there >= here[:, 1:2])


def attend_kernel(
    qkv_ref, sums_ref, gain_ref, table_ref, row_ref, mixed_ref, low_ref, scale_ref
):
    cosines, sines = table_ref[:, :HEAD], table_ref[:, HEAD : 2 * HEAD]
    scale_ref[...] = lax.rsqrt(sums_ref[...] * (1.0 / D) + EPSILON).T
    for h in range(2):
        at = slice(h * HEAD, (h + 1) * HEAD)
        k_at = slice(256 + h * HEAD, 256 + (h + 1) * HEAD)
        q = qkv_ref[:, at] * scale_ref[:, 0:1] * gain_ref[0:1, at]
        k = qkv_ref[:, k_at] * scale_ref[:, 1:2] * gain_ref[1:2, at]
        low_ref[:, at] = turn(q, cosines, sines).astype(LOW)
        k = turn(k, cosines, sines).astype(LOW)
        v = qkv_ref[:, 512 + h * HEAD : 512 + (h + 1) * HEAD].astype(LOW)
        low_ref[:, k_at] = k
        low_ref[:, 512 + h * HEAD : 512 + (h + 1) * HEAD] = v
        for lo in range(0, SEQ, TILE):
            q = low_ref[lo : lo + TILE, at]
            scores = dot(q, k, NT) * HEAD**-0.5
            scores = jnp.where(seen(table_ref, row_ref, lo), scores, MASKED)
            peak = jnp.max(scores, axis=1, keepdims=True)
            weights = jnp.exp(scores - peak)
            total = jnp.sum(weights, axis=1, keepdims=True)
            weights = (weights * (1.0 / total)).astype(LOW)
            mixed_ref[lo : lo + TILE, at] = dot(weights, v).astype(LOW)
            scale_ref[lo : lo + TILE, 2 + h : 3 + h] = peak + jnp.log(total)


def attend_back_kernel(
    qkv_ref, scale_ref, gain_ref, table_ref, row_ref, low_ref,
    own_ref, other_ref, near_ref, far_ref,
    hat_ref, value_ref, dots_ref, part_ref, dk_ref, dv_ref, grad_ref,
):
    cosines, sines = table_ref[:, :HEAD], table_ref[:, HEAD : 2 * HEAD]
    for i, ref in enumerate((own_ref, other_ref)):
        grad = dot(ref[:, :NEAR], near_ref[...], NT) + dot(ref[:, NEAR:], far_ref[...], NT)
        grad_ref[OWN * i : OWN * (i + 1), :] = grad.astype(LOW)
    for h in range(2):
        at = slice(h * HEAD, (h + 1) * HEAD)
        k_at = slice(256 + h * HEAD, 256 + (h + 1) * HEAD)
        k = low_ref[:, k_at]
        v = low_ref[:, 512 + h * HEAD : 512 + (h + 1) * HEAD]
        for lo in range(0, SEQ, TILE):
            q = low_ref[lo : lo + TILE, at]
            grad = grad_ref[lo : lo + TILE, at]
            scores = dot(q, k, NT) * HEAD**-0.5
            weights = jnp.exp(scores - scale_ref[lo : lo + TILE, 2 + h : 3 + h])
            weights = jnp.where(seen(table_ref, row_ref, lo), weights, 0.0)
            weight_grad = dot(grad, v, NT)
            centre = jnp.sum(weights * weight_grad, axis=1, keepdims=True)
            score_grad = (weights * (weight_grad - centre)).astype(LOW)
            hat_ref[lo : lo + TILE, at] = dot(score_grad, k) * HEAD**-0.5
            value_part = dot(weights.astype(LOW), grad, TN)
            key_part = dot(score_grad, q, TN)
            if lo == 0:
                dv_ref[...] = value_part
                dk_ref[...] = key_part
            else:
                dv_ref[...] += value_part
                dk_ref[...] += key_part
        value_ref[:, at] = dv_ref[...].astype(LOW)
        q_grad = turn_back(hat_ref[:, at], cosines, sines)
        k_grad = turn_back(dk_ref[...] * HEAD**-0.5, cosines, sines)
        q, k = qkv_ref[:, at], qkv_ref[:, k_at]
        part_ref[0:1, at] = jnp.sum(q_grad * q * scale_ref[:, 0:1], axis=0, keepdims=True)
        part_ref[1:2, at] = jnp.sum(k_grad * k * scale_ref[:, 1:2], axis=0, keepdims=True)
        hat_ref[:, at] = q_grad * gain_ref[0:1, at]
        hat_ref[:, k_at] = k_grad * gain_ref[1:2, at]
    dots_ref[...] = as_rows(
        jnp.sum(hat_ref[:, :256] * qkv_ref[:, :256], axis=1, keepdims=True),
        jnp.sum(hat_ref[:, 256:] * qkv_ref[:, 256:512], axis=1, keepdims=True),
    )


def qkv_back_kernel(hat_ref, qkv_ref, rms_ref, dots_ref, value_ref, out_ref):
    dots = dots_ref[...].T
    for i in range(2):
        at = slice(i * 256, (i + 1) * 256)
        rms = rms_ref[:, i : i + 1]
        coefficient = rms * rms * rms * dots[:, i : i + 1] * (1.0 / D)
        out_ref[:, at] = (rms * hat_ref[:, at] - qkv_ref[:, at] * coefficient).astype(LOW)
    out_ref[:, 512:] = value_ref[...]


def widen_kernel(table, rows_ref, out_ref):
    for i in range(8):
        block = pl.ds(pl.multiple_of(table[i] * BLOCK, BLOCK), BLOCK)
        out_ref[i * BLOCK : (i + 1) * BLOCK, :] = rows_ref[block, :].astype(F32)


def blocks_of(ref):
    return [slice(i * BLOCK, (i + 1) * BLOCK) for i in range(ref.shape[0] // BLOCK)]


def hidden_kernel(b0, b1, b2, b3, states_ref, gain_ref, low_ref, rms_ref):
    for at, ref in zip(blocks_of(low_ref), (b0, b1, b2, b3)):
        branch = ref[...].astype(F32)
        rms = lax.rsqrt(jnp.mean(branch * branch, axis=1, keepdims=True) + EPSILON)
        hidden = states_ref[at, :].astype(F32) + gain_ref[...] * branch * rms
        low_ref[at, :] = hidden.astype(LOW)
        rms_ref[at, :] = rms


def back_of(upstream, branch, rms, gain):
    part = jnp.sum(upstream * branch * rms, axis=0, keepdims=True)
    scaled = upstream * gain
    inner = jnp.sum(scaled * branch, axis=1, keepdims=True)
    return rms * scaled - branch * (rms * rms * rms * inner * (1.0 / D)), part


def ffn_back_kernel(b0, b1, b2, b3, upstream_ref, gain_ref, back_ref, rms_ref, part_ref):
    for i, (at, ref) in enumerate(zip(blocks_of(back_ref), (b0, b1, b2, b3))):
        branch = ref[...].astype(F32)
        rms = lax.rsqrt(jnp.mean(branch * branch, axis=1, keepdims=True) + EPSILON)
        back, part = back_of(upstream_ref[at, :].astype(F32), branch, rms, gain_ref[...])
        back_ref[at, :] = back.astype(LOW)
        rms_ref[at, :] = rms
        part_ref[...] = part if i == 0 else part_ref[...] + part


def attn_back_kernel(
    g0, g1, g2, g3, b0, b1, b2, b3, upstream_ref, rms_ref, gain_ref, back_ref, part_ref
):
    pairs = zip(blocks_of(back_ref), (g0, g1, g2, g3), (b0, b1, b2, b3))
    for i, (at, grad_ref, ref) in enumerate(pairs):
        grad = grad_ref[...].astype(F32) + upstream_ref[at, :].astype(F32)
        back, part = back_of(grad, ref[...].astype(F32), rms_ref[at, :], gain_ref[...])
        back_ref[at, :] = back.astype(LOW)
        part_ref[...] = part if i == 0 else part_ref[...] + part


def out_kernel(
    core_ref, a0, a1, a2, a3, b0, b1, b2, b3, states_ref, attn_rms_ref, ffn_rms_ref,
    attn_gain_ref, ffn_gain_ref, sent0_ref, sent1_ref,
):
    pairs = zip(blocks_of(states_ref), (a0, a1, a2, a3), (b0, b1, b2, b3))
    flip = core_ref[0] == 1
    for at, a_ref, b_ref in pairs:
        value = (
            states_ref[at, :].astype(F32)
            + attn_gain_ref[...] * a_ref[...].astype(F32) * attn_rms_ref[at, :]
            + ffn_gain_ref[...] * b_ref[...].astype(F32) * ffn_rms_ref[at, :]
        ).astype(LOW)
        near, far = value[:, :NEAR], value[:, NEAR:]
        sent0_ref[at, :] = jnp.where(flip, far, near)
        sent1_ref[at, :] = jnp.where(flip, near, far)


def shuffle(sent):
    out = []
    for k in range(2):
        perm = [(c * 2 + s, s * 2 + (s ^ c ^ k)) for s in range(2) for c in range(2)]
        out.append(lax.ppermute(sent[k], ("core", "xl"), [p for p in perm if p[0] != p[1]]))
    return out


def shuffled_of(at, sent, came):
    return [jnp.where((at.s == k) & (at.c == k), sent[k], came[k]) for k in range(2)]


def local(
    inputs, segments, w_query, w_key, w_value, w_mix, w_gate, w_up, w_down,
    attn_gain, ffn_gain, query_gain, key_gain, out_grad,
):
    at = Place()
    first = first_hop(inputs)
    near_qkv = cut_columns(at, (768, 256), w_query, w_key, w_value)
    far_qkv = [wrap_swap(near_qkv[0]), pair_swap(near_qkv[1])]
    near_mix = lax.dynamic_slice_in_dim(w_mix, at.c * 256, 256, 0)
    near = cut_pieces(at, after(w_gate, near_qkv), w_up, w_down)

    gains = jnp.concatenate([attn_gain, ffn_gain, query_gain, key_gain])
    their_gains = pair_swap(gains)
    attn_gains = jnp.concatenate([attn_gain, their_gains[:NEAR]])[None]
    ffn_gains = jnp.concatenate([ffn_gain, their_gains[NEAR:D]])[None]
    head_gains = jnp.where(at.home, gains[D:], their_gains[D:]).reshape(2, 256)

    segment_ids = jnp.where(at.home, segments, core_swap(segments))
    step_index = jnp.arange(SEQ, dtype=jnp.int32)
    earlier = jnp.concatenate([segment_ids[:1] - 1, segment_ids[:-1]])
    begins = lax.cummax(jnp.where(segment_ids != earlier, step_index, 0))
    chosen = at.rows[:, None, None] == jnp.arange(8, dtype=jnp.int32)[None, :, None]
    begins = jnp.sum(jnp.where(chosen, begins.reshape(1, 8, BLOCK), 0), axis=1).reshape(-1)
    index = (at.rows[:, None] * BLOCK + jnp.arange(BLOCK, dtype=jnp.int32)[None]).reshape(-1)
    frequency = ROPE_BASE ** (-2.0 * jnp.arange(HEAD // 2, dtype=F32) / HEAD)
    angles = (index - begins).astype(F32)[:, None] * frequency
    cosines, sines = jnp.cos(angles), jnp.sin(angles)
    place_columns = jnp.stack([index, begins], axis=1).astype(F32)
    table = jnp.concatenate(
        [cosines, cosines, -sines, sines, jnp.pad(place_columns, ((0, 0), (0, 126)))], axis=1
    )
    tables = (table, index[None].astype(F32))

    tables, head_gains, attn_gains, ffn_gains, at.columns, at.plain, at.rows, near, first = (
        lax.optimization_barrier(
            (tables, head_gains, attn_gains, ffn_gains, at.columns, at.plain, at.rows, near, first)
        )
    )
    states = to_sequence(at, inputs, first, second_hop(after(first, far_qkv)))
    states, far_qkv = lax.optimization_barrier((states, far_qkv))
    qkv_blocks = [*near_qkv, *far_qkv]
    qkv, squares = call(qkv_kernel, [((SEQ, SEQ), F32), ((8, SEQ), F32)], states, *qkv_blocks)
    far = fetch(*after(near[:2], far_qkv))
    both_mix = lax.all_gather(after(near_mix, far_qkv), "xl")
    squares = all_stats(squares)
    squares, far = lax.optimization_barrier((squares, far))
    far_mix = jnp.where(at.s == 0, both_mix[1], both_mix[0])
    mixed, low, scales = call(
        attend_kernel,
        [((SEQ, 256), LOW), ((SEQ, SEQ), LOW), ((SEQ, 8), F32)],
        qkv, squares, head_gains, *tables,
    )
    came = core_swap(mix(mixed, 1, near_mix, far_mix, LOW))
    mix_parts = settle(mix(mixed, 0, near_mix, far_mix, F32), came)
    mix_parts = lax.optimization_barrier(mix_parts)
    far = [*far, *fetch(*after(near[2:4], mix_parts))]
    attn_sum = scatter_z(mix_parts).astype(LOW)
    attn_sum, far = lax.optimization_barrier((attn_sum, far))
    far = [*far, *fetch(*after(near[4:6], attn_sum))]
    attn_blocks = gather_z(attn_sum)
    own_states = after(states, attn_sum)[:OWN]
    attn_blocks, far, own_states = lax.optimization_barrier((attn_blocks, far, own_states))
    far = [*far, *fetch(*after(near[6:], attn_blocks))]
    hidden_own, attn_rms = call(
        hidden_kernel,
        [((OWN, D), LOW), ((OWN, 1), F32)],
        *attn_blocks, own_states, attn_gains,
    )
    hidden_other = core_swap(hidden_own)

    gates, ups, downs = (
        [side[k] for side in (near, far) for k in pieces_with(name)]
        for name in ("gate", "up", "down")
    )
    gate_own, up_own, units_own = units_of(hidden_own, gates, ups)
    hidden_other = after(hidden_other, units_own)
    gate_other, up_other, units_other = units_of(hidden_other, gates, ups)
    came = core_swap(down(units_other, downs, LOW))
    ffn_parts = settle(down(after(units_own, units_other), downs, F32), came)
    ffn_parts = lax.optimization_barrier(ffn_parts)
    grad_first = first_hop(after(out_grad, ffn_parts))
    ffn_sum = scatter_z(ffn_parts).astype(LOW)
    ffn_sum, grad_first = lax.optimization_barrier((ffn_sum, grad_first))
    ffn_blocks = gather_z(ffn_sum)
    upstream = to_sequence(at, out_grad, grad_first, second_hop(grad_first), RING)
    ffn_blocks, upstream = lax.optimization_barrier((ffn_blocks, upstream))
    branch_own, ffn_rms, ffn_gain_part = call(
        ffn_back_kernel,
        [((OWN, D), LOW), ((OWN, 1), F32), ((1, D), F32)],
        *ffn_blocks, upstream, ffn_gains,
    )
    branch_other = core_swap(branch_own)
    gate_back_own, up_back_own = units_back(branch_own, downs, gate_own, up_own)
    sent = call(
        out_kernel,
        [((OWN, NEAR), LOW)] * 2,
        at.c.reshape(1).astype(jnp.int32), *attn_blocks, *ffn_blocks,
        own_states, attn_rms, after(ffn_rms, gate_back_own), attn_gains, ffn_gains,
        scalars=1,
    )
    branch_other = after(branch_other, gate_back_own, sent)
    gate_back_other, up_back_other = units_back(branch_other, downs, gate_other, up_other)
    came = core_swap(pair_down(gate_back_other, up_back_other, gates, ups, LOW))
    pair_parts = pair_down(after(gate_back_own, gate_back_other), up_back_own, gates, ups, F32)
    pair_parts = settle(pair_parts, came)

    hidden_sum = scatter_z(pair_parts)
    hidden_rows = hidden_sum + upstream[:BLOCK].astype(F32)
    branch_own, hidden_own, pair_parts = lax.optimization_barrier(
        (branch_own, hidden_own, pair_parts)
    )
    shuffled = shuffle(after(sent, pair_parts))
    gate_args = [hidden_own, hidden_other, gate_back_own, gate_back_other]
    up_args = [hidden_own, hidden_other, up_back_own, up_back_other]
    down_args = [branch_own, branch_other, units_own, units_other]
    terms = [(0, 2, 0), (1, 3, 0)]
    grads0 = weight_grad(
        at.columns,
        [*gate_args, *up_args[2:]],
        [(0, 1024, terms), (0, 512, [(0, 4, 0), (1, 5, 0)])],
    )
    hidden_sum, grads0, shuffled, up_args, down_args = lax.optimization_barrier(
        (hidden_sum.astype(LOW), grads0, shuffled, up_args, down_args)
    )

    hidden_blocks = gather_z(hidden_sum)
    came0 = {i: plane_shift(after(grads0[i], hidden_sum), i, False) for i in (1, 3)}
    grads1 = weight_grad(
        at.columns,
        [*up_args, *down_args],
        [(512, 512, terms), (0, 1024, [(4, 6, 0), (5, 7, 0)])],
        cut=True,
    )
    hidden_blocks, came0, grads1 = lax.optimization_barrier((hidden_blocks, came0, grads1))
    mix_own, attn_gain_part = call(
        attn_back_kernel,
        [((OWN, D), LOW), ((1, D), F32)],
        *hidden_blocks, *attn_blocks, upstream, attn_rms, attn_gains,
    )
    mix_other = core_swap(mix_own)

    keep1, up0, up1, far1, down0, down1 = after(grads1, hidden_blocks)
    came1a = [plane_shift(up0, 1, False), plane_shift(down0, 3, False)]
    hat, value_back, dots, head_parts = call(
        attend_back_kernel,
        [((SEQ, 512), F32), ((SEQ, 256), LOW), ((8, SEQ), F32), ((2, 256), F32)],
        qkv, scales, head_gains, *tables, low, mix_own, mix_other, near_mix, far_mix,
        scratch=[pltpu.VMEM((SEQ, HEAD), F32)] * 2 + [pltpu.VMEM((SEQ, 256), LOW)],
    )
    hat, dots, came1a, up1, down1 = lax.optimization_barrier((hat, dots, came1a, up1, down1))
    came1b = [plane_shift(up1, 1, False), plane_shift(down1, 3, False)]
    dots, came1b, far1 = lax.optimization_barrier((all_stats(dots), came1b, far1))
    came0[2] = plane_shift(after(grads0[2], dots), 2, False)
    came1 = plane_shift(far1, 2, False)
    (qkv_back,) = call(
        qkv_back_kernel, [((SEQ, SEQ), LOW)], hat, qkv, scales, dots, value_back
    )
    came = core_swap(qkv_down(qkv_back, 1, qkv_blocks, LOW))
    input_parts = settle_ordered(at, qkv_down(qkv_back, 0, qkv_blocks, F32), came)
    input_parts, qkv_back = lax.optimization_barrier((input_parts, qkv_back))

    input_sum = lax.psum_scatter(input_parts, "z", scatter_dimension=0, tiled=True)
    attn_grads = weight_grad(
        at.columns,
        [states, qkv_back, mix_own, mix_other, mixed],
        [(0, SEQ, [(0, 1, 0)]), (0, 256, [(2, 4, 0), (3, 4, OWN)])],
        [attn_gain_part, ffn_gain_part, jnp.pad(head_parts.reshape(16, 32), ((0, 0), (0, 96)))],
    )
    input_sum, attn_grads = lax.optimization_barrier((input_sum, attn_grads))
    input_low = (input_sum.astype(F32) + hidden_rows).astype(LOW)
    near, far = input_low[:, :NEAR], input_low[:, NEAR:]
    flip = at.c == 1
    input_sent = [jnp.where(flip, far, near), jnp.where(flip, near, far)]
    input_rows = shuffled_of(at, input_sent, shuffle(input_sent))
    input_rows, attn_grads, came0, came1 = lax.optimization_barrier(
        (jnp.concatenate(input_rows), attn_grads, came0, came1)
    )
    input_rows = lax.all_gather(input_rows, "z", axis=0, tiled=True)
    attn_came = [plane_shift(attn_grads[i], i, False) for i in range(1, RING)]
    steps = jnp.arange(8, dtype=jnp.int32)
    from_part = at.s ^ at.c ^ (steps // RING)
    from_z = (at.z - steps) % RING
    block_out = order_rows(
        at, shuffled_of(at, sent, after(shuffled, input_low)), from_z, from_part
    )
    (input_grad,) = call(
        widen_kernel, [((SEQ, NEAR), F32)],
        (steps % RING * 2 + from_part).astype(jnp.int32), input_rows,
        scalars=1,
    )

    block_out, came0, came1, came1a, came1b = lax.optimization_barrier(
        (block_out, came0, came1, came1a, came1b)
    )
    rows0 = plane_sum(grads0[0], [came0[i] for i in (1, 2, 3)])
    came1b = [jnp.concatenate(halves, axis=1) for halves in zip(came1a, came1b)]
    rows1 = plane_sum(keep1, [*came1b, came1])
    attn_came, rows0, rows1 = lax.optimization_barrier((attn_came, rows0, rows1))
    ffn_rows = [jnp.concatenate(rows) for rows in zip(rows0, rows1)]
    ffn_came = [plane_shift(ffn_rows[i], i, True) for i in range(1, RING)]
    attn_rows = plane_sum(attn_grads[0], attn_came)
    attn_came = [plane_shift(attn_rows[i], i, True) for i in range(1, RING)]
    attn_came, ffn_came, input_grad = lax.optimization_barrier((attn_came, ffn_came, input_grad))
    gate_out, up_out, down_out = share_cores(
        at,
        ffn_rows[0],
        ffn_came,
        [[(0, 0, 1024)], [(0, 1024, 512), (1, 0, 512)], [(1, 512, 1024)]],
    )
    query, key, value, mix_out, width, heads = share_cores(
        at, attn_rows[0], attn_came, [[(0, i, 256)] for i in range(0, 1024, 256)],
        [(8, 128), (16, 128)],
    )
    width = jnp.where(flip, width[:2, 64:], width[:2, :64])
    heads = jnp.where(at.s == 0, heads[2:4, :32], heads[10:12, :32])
    heads = jnp.where(flip, heads[:, 16:], heads[:, :16])

    return (
        block_out, input_grad, query, key, value, mix_out, gate_out, up_out, down_out,
        width[0], width[1], heads[0], heads[1],
    )


def solution(mesh):
    fine = Mesh(mesh.devices.reshape(4, 2, 2, 4, 2), ("y", "xh", "core", "z", "xl"))
    dp = ("y", "xh", "core")
    row, col = "z", "xl"
    return jax.shard_map(
        local,
        mesh=fine,
        in_specs=(
            P(dp, col), P(dp), P(col, row), P(col, row), P(col, row), P(row, col),
            P(col, row), P(col, row), P(row, col), P(col), P(col), P((row, col)),
            P((row, col)), P(dp, col),
        ),
        out_specs=(
            P(dp, col), P(dp, col),
            P((col,) + dp, row), P((col,) + dp, row), P((col,) + dp, row), P(row, (col,) + dp),
            P((col,) + dp, row), P((col,) + dp, row), P(row, (col,) + dp),
            P((col,) + dp), P((col,) + dp), P((row, col) + dp), P((row, col) + dp),
        ),
        check_vma=False,
    )
```

profile of v0, /device:TPU:1, one launch (start us, length us, event | category | flops | bytes accessed | tf_op | source)
XLA Modules:
  0.0 453.6 jit_solution(13784904356520355968)
XLA Ops:
  11.0 2.5 shard_map.237
  17.0 5.6 %shard_map.238 = (bf16[256,1024]{1,0:T(8,128)(2,1)}, bf16[256,1024]{1,0:T(8,128)(2,1)}, bf16[512,1024]{1,0:T(8,128)(2,1)}, bf16[512,1024]{1,0:T(8,128)(2,1)}, bf...) custom-call(s32[1]{0:T(128)} %bitcast.table.core_ref.core, ...), custom_call_target="tpu_custom_call" | custom-call | tf_op jit(solution)/shard_map/pallas_call | solution.py:109
  33.0 4.2 collective-permute-done.4.refs_3_.refs_4_
  38.0 4.3 collective-permute-done.3.refs_2_.refs_3_
  44.7 4.2 collective-permute-done.5.second_ref
  52.5 2.8 shard_map.240
  56.6 4.0 collective-permute-start.9
  65.6 3.5 collective-permute-done.7
  69.3 7.4 %collective-permute-done.10.refs_4_.refs_6_ = bf16[256,1024]{1,0:T(8,128)(2,1)S(1)} collective-permute-done((bf16[256,1024]{1,0:T(8,128)(2,1)}, bf16[256,1024]{1,0:T(8,128)(2,1)S(1)}, u32[]{:S(2)}, u32[]{:S(2)}) %collective-permute-start.10) | collective-permute-done | bytes 524320 | tf_op jit(solution)/shard_map/ppermute | solution.py:64
  79.6 6.1 %shard_map.241 = (bf16[768,256]{1,0:T(8,128)(2,1)S(1)}, bf16[768,768]{1,0:T(8,128)(2,1)S(1)}, f32[768,8]{1,0:T(8,128)S(1)}) custom-call(f32[768,768]{1,0:T(8,128)S(1)} %get-tuple-element.265.qkv_ref, f32[8,768]{1,0:T(8,128)S(1)} %fusion.3.sums_ref, f32[2,256]{1,0:T(2,128)S(1)} %select_n.189.gain_ref, f32[768,384]{1,0:T(8,128)S(1)} %copy-done.15, ...), custom_call_target="tpu_custom_call" | custom-call | tf_op jit(solution)/shard_map/pallas_call | solution.py:334
  89.6 3.0 collective-permute-start.12
  97.1 2.7 collective-permute-start.17
  101.3 8.5 %collective-permute-done.13 = bf16[96,2048]{1,0:T(8,128)(2,1)S(1)} collective-permute-done((bf16[96,2048]{1,0:T(8,128)(2,1)S(1)}, bf16[96,2048]{1,0:T(8,128)(2,1)S(1)}, u32[]{:S(2)}, u32[]{:S(2)}) %collective-permute-start.13) | collective-permute-done | bytes 393248 | tf_op jit(solution)/shard_map/ppermute | solution.py:40
  111.4 9.4 %collective-permute-done.15 = bf16[96,2048]{1,0:T(8,128)(2,1)S(1)} collective-permute-done((bf16[96,2048]{1,0:T(8,128)(2,1)S(1)}, bf16[96,2048]{1,0:T(8,128)(2,1)S(1)}, u32[]{:S(2)}, u32[]{:S(2)}) %collective-permute-start.15) | collective-permute-done | bytes 393248 | tf_op jit(solution)/shard_map/ppermute | solution.py:40
  125.5 2.7 collective-permute-start.20
  128.3 15.6 %collective-permute-done.18.b1.a1 = bf16[96,2048]{1,0:T(8,128)(2,1)S(1)} collective-permute-done((bf16[96,2048]{1,0:T(8,128)(2,1)S(1)}, bf16[96,2048]{1,0:T(8,128)(2,1)S(1)}, u32[]{:S(2)}, u32[]{:S(2)}) %collective-permute-start.18) | collective-permute-done | bytes 393248 | tf_op jit(solution)/shard_map/ppermute | solution.py:40
  149.1 2.5 collective-permute-start.23
  153.9 3.4 shard_map.246
  157.4 3.4 shard_map.247
  160.8 4.2 collective-permute-done.24.refs_7_.refs_6_
  174.3 8.9 %collective-permute-done.27 = bf16[96,2048]{1,0:T(8,128)(2,1)S(1)} collective-permute-done((bf16[96,2048]{1,0:T(8,128)(2,1)S(1)}, bf16[96,2048]{1,0:T(8,128)(2,1)S(1)}, u32[]{:S(2)}, u32[]{:S(2)}) %collective-permute-start.27) | collective-permute-done | bytes 393248 | tf_op jit(solution)/shard_map/ppermute | solution.py:40
  184.7 9.1 %collective-permute-done.29 = bf16[96,2048]{1,0:T(8,128)(2,1)S(1)} collective-permute-done((bf16[96,2048]{1,0:T(8,128)(2,1)S(1)}, bf16[96,2048]{1,0:T(8,128)(2,1)S(1)}, u32[]{:S(2)}, u32[]{:S(2)}) %collective-permute-start.29) | collective-permute-done | bytes 393248 | tf_op jit(solution)/shard_map/ppermute | solution.py:40
  200.4 6.9 %collective-permute-done.31.b1 = bf16[96,2048]{1,0:T(8,128)(2,1)S(1)} collective-permute-done((bf16[96,2048]{1,0:T(8,128)(2,1)S(1)}, bf16[96,2048]{1,0:T(8,128)(2,1)S(1)}, u32[]{:S(2)}, u32[]{:S(2)}) %collective-permute-start.31) | collective-permute-done | bytes 393248 | tf_op jit(solution)/shard_map/ppermute | solution.py:40
  207.3 5.7 %collective-permute-done.32.b2 = bf16[96,2048]{1,0:T(8,128)(2,1)S(1)} collective-permute-done((bf16[96,2048]{1,0:T(8,128)(2,1)S(1)}, bf16[96,2048]{1,0:T(8,128)(2,1)S(1)}, u32[]{:S(2)}, u32[]{:S(2)}) %collective-permute-start.32) | collective-permute-done | bytes 393248 | tf_op jit(solution)/shard_map/ppermute | solution.py:40
  226.3 3.4 shard_map.257
  230.3 3.4 shard_map.256.own_ref
  236.8 4.4 collective-permute-start.40
  243.1 7.3 %shard_map.259 = (bf16[512,1536]{1,0:T(8,128)(2,1)S(1)}, bf16[512,1536]{1,0:T(8,128)(2,1)S(1)}, bf16[512,1536]{1,0:T(8,128)(2,1)S(1)}, bf16[512,1536]{1,0:T(8,128)(2,1)S(1)}) custom-call(s32[16]{0:T(128)S(1)} %copy-done.81, bf16[384,2048]{1,0:T(8,128)(2,1)S(1)} %get-tuple-element.369.rows_ref.refs_1_, ...), custom_call_target="tpu_custom_call" | custom-call | tf_op jit(solution)/shard_map/pallas_call | solution.py:334
  251.7 4.8 %collective-permute-done.39 = bf16[96,2048]{1,0:T(8,128)(2,1)S(1)} collective-permute-done((bf16[96,2048]{1,0:T(8,128)(2,1)S(1)}, bf16[96,2048]{1,0:T(8,128)(2,1)S(1)}, u32[]{:S(2)}, u32[]{:S(2)}) %collective-permute-start.39) | collective-permute-done | bytes 393248 | tf_op jit(solution)/shard_map/ppermute | solution.py:40
  264.5 7.3 %shard_map.260 = (bf16[512,1536]{1,0:T(8,128)(2,1)S(1)}, bf16[512,768]{1,0:T(8,128)(2,1)S(1)}, bf16[512,768]{1,0:T(8,128)(2,1)S(1)}, bf16[512,1536]{1,0:T(8,128)...) custom-call(s32[16]{0:T(128)S(1)} %copy-done.81, ...), custom_call_target="tpu_custom_call" | custom-call | tf_op jit(solution)/shard_map/pallas_call | solution.py:334
  273.0 4.8 %collective-permute-done.43.g2 = bf16[96,2048]{1,0:T(8,128)(2,1)S(1)} collective-permute-done((bf16[96,2048]{1,0:T(8,128)(2,1)S(1)}, bf16[96,2048]{1,0:T(8,128)(2,1)S(1)}, u32[]{:S(2)}, u32[]{:S(2)}) %collective-permute-start.43) | collective-permute-done | bytes 393248 | tf_op jit(solution)/shard_map/ppermute | solution.py:40
  277.8 2.8 collective-permute-done.44.g3
  283.5 2.5 collective-permute-start.47
  290.3 7.7 %shard_map.262 = (f32[768,512]{1,0:T(8,128)S(1)}, bf16[768,256]{1,0:T(8,128)(2,1)S(1)}, f32[8,768]{1,0:T(8,128)S(1)}, f32[2,256]{1,0:T(2,128)S(1)}) custom-call(f32[768,768]{1,0:T(8,128)S(1)} %copy-done.9, f32[768,8]{1,0:T(8,128)S(1)} %copy-done.55, f32[2,256]{1,0:T(2,128)S(1)} %copy-done.78, f32[768,384]{1,0:T(8,128)S(1)} %copy-done.16, ...), custom_call_target="tpu_custom_call" | custom-call | tf_op jit(solution)/shard_map/pallas_call | solution.py:334
  308.4 4.1 collective-permute-done.51
  312.8 3.2 collective-permute-done.54
  327.4 3.2 collective-permute-start.59
  335.5 4.4 shard_map.267
  344.0 7.5 %reduce-scatter.2.cloned.1.call-done = bf16[96,2048]{1,0:T(8,128)(2,1)} async-done(((bf16[384,2048]{1,0:T(8,128)(2,1)}), bf16[96,2048]{1,0:T(8,128)(2,1)}) %reduce-scatter.2.cloned.1.call-update) | async-done | bytes 393232 | tf_op jit(solution)/shard_map/reduce_scatter | solution.py:893
  353.8 4.5 collective-permute-start.57
  361.1 3.8 shard_map.268
  364.9 6.3 %collective-permute-done.57 = bf16[96,1024]{1,0:T(8,128)(2,1)S(1)} collective-permute-done((bf16[96,1024]{1,0:T(8,128)(2,1)S(1)}, bf16[96,1024]{1,0:T(8,128)(2,1)S(1)}, u32[]{:S(2)}, u32[]{:S(2)}) %collective-permute-start.57) | collective-permute-done | bytes 196640 | tf_op jit(solution)/shard_map/ppermute | solution.py:724
  375.3 4.3 add_convert_fusion.1
  384.3 17.4 %collective-permute-done.61 = bf16[576,1024]{1,0:T(8,128)(2,1)} collective-permute-done((bf16[576,1024]{1,0:T(8,128)(2,1)}, bf16[576,1024]{1,0:T(8,128)(2,1)}, u32[]{:S(2)}, u32[]{:S(2)}) %collective-permute-start.61) | collective-permute-done | bytes 1179680 | tf_op jit(solution)/shard_map/ppermute | solution.py:56
  403.2 3.1 collective-permute-start.69
  409.3 3.0 add_convert_fusion.2
  416.3 15.4 %collective-permute-done.64.p1 = bf16[144,1024]{1,0:T(8,128)(2,1)S(1)} collective-permute-done((bf16[144,1024]{1,0:T(8,128)(2,1)S(1)}, bf16[144,1024]{1,0:T(8,128)(2,1)S(1)}, u32[]{:S(2)}, u32[]{:S(2)}) %collective-permute-start.64) | collective-permute-done | bytes 294944 | tf_op jit(solution)/shard_map/ppermute | solution.py:56
  433.7 2.4 shard_map.269
  (465 shorter events, 175.3 us)
Async XLA Ops:
  7.2 80.3 %all-gather.6.cloned.1.call-start = ((), (), s32[]{:S(2)}) async-start(), calls=%async_computation.3 | async-start | bytes 1572864 | tf_op jit(solution)/shard_map/all_gather | solution.py:775
  7.2 15.4 %collective-permute-start = (s32[768]{0:T(1024)}, s32[768]{0:T(1024)S(1)}, u32[]{:S(2)}, u32[]{:S(2)}) collective-permute-start(s32[768]{0:T(1024)} %param.15), channel_id=1, source_target_pairs={{0,8},{8,0},{1,9},{9,1},{2,10},{10,2},{3,11},{11,3},{4,12},{12,4},... | collective-permute-start | bytes 9224 | tf_op jit(solution)/shard_map/ppermute | solution.py:60
  9.5 23.0 %collective-permute-start.1 = (f32[2560]{0:T(1024)S(1)}, f32[2560]{0:T(1024)S(1)}, u32[]{:S(2)}, u32[]{:S(2)}) collective-permute-start(f32[2560]{0:T(1024)S(1)} %pad_maximum_fusion.6), channel_id=1, source_target_pairs={{0,1},{1,0},{2,3},{3,2},{4,5},{5,4},{6,7},{7,6},{8,9},{9,8},{10,11... | collective-permute-start | bytes 30728 | tf_op jit(solution)/shard_map/ppermute | solution.py:64
  10.8 22.2 %collective-permute-start.2 = (bf16[768,1024]{1,0:T(8,128)(2,1)}, bf16[768,1024]{1,0:T(8,128)(2,1)}, u32[]{:S(2)}, u32[]{:S(2)}) collective-permute-start(bf16[768,1024]{1,0:T(8,128)(2,1)} %a_ref.2), channel_id=1, source_target_pairs={{0,8},{9,1},{8,9},{1,0},{2,10},{11,3},{10,11},{3,2},{4,12},{13,5},... | collective-permute-start | bytes 4718600 | tf_op jit(solution)/shard_map/ppermute | solution.py:126
  13.5 28.7 %collective-permute-start.3 = (bf16[768,768]{1,0:T(8,128)(2,1)}, bf16[768,768]{1,0:T(8,128)(2,1)S(1)}, u32[]{:S(2)}, u32[]{:S(2)}) collective-permute-start(bf16[768,768]{1,0:T(8,128)(2,1)} %get-tuple-element.248.refs_0_.refs_1_), channel_id=1, source_target_pairs={{0,17},{17,0},{1,16},{16,1},{2,19},{19,2},{3,18},{18,3},{4,21},{21... | collective-permute-start | bytes 3538952 | tf_op jit(solution)/shard_map/ppermute | solution.py:68
  15.6 21.6 %collective-permute-start.4 = (bf16[256,768]{1,0:T(8,128)(2,1)}, bf16[256,768]{1,0:T(8,128)(2,1)S(1)}, u32[]{:S(2)}, u32[]{:S(2)}) collective-permute-start(bf16[256,768]{1,0:T(8,128)(2,1)} %get-tuple-element.249.refs_1_.refs_2_), channel_id=1, source_target_pairs={{0,1},{1,0},{2,3},{3,2},{4,5},{5,4},{6,7},{7,6},{8,9},{9,8},{10,11... | collective-permute-start | bytes 1179656 | tf_op jit(solution)/shard_map/ppermute | solution.py:64
  61.4 290.1 %reduce-scatter.2.cloned.1.call-start = ((), (), s32[]{:S(2)}) async-start(), calls=%async_computation.1 | async-start | bytes 1966080 | tf_op jit(solution)/shard_map/reduce_scatter | solution.py:893
  61.5 15.2 %collective-permute-start.10 = (bf16[256,1024]{1,0:T(8,128)(2,1)}, bf16[256,1024]{1,0:T(8,128)(2,1)S(1)}, u32[]{:S(2)}, u32[]{:S(2)}) collective-permute-start(bf16[256,1024]{1,0:T(8,128)(2,1)} %get-tuple-element.269.refs_0_.refs_2_), channel_id=1, source_target_pairs={{0,1},{1,0},{2,3},{3,2},{4,5},{5,4},{6,7},{7,6},{8,9},{9,8},{10,11... | collective-permute-start | bytes 1572872 | tf_op jit(solution)/shard_map/ppermute | solution.py:64
  62.0 15.5 %collective-permute-start.11 = (bf16[256,1024]{1,0:T(8,128)(2,1)}, bf16[256,1024]{1,0:T(8,128)(2,1)S(1)}, u32[]{:S(2)}, u32[]{:S(2)}) collective-permute-start(bf16[256,1024]{1,0:T(8,128)(2,1)} %get-tuple-element.270.refs_1_.refs_3_), channel_id=1, source_target_pairs={{0,17},{17,0},{1,16},{16,1},{2,19},{19,2},{3,18},{18,3},{4,21},{21... | collective-permute-start | bytes 1572872 | tf_op jit(solution)/shard_map/ppermute | solution.py:68
  95.9 25.1 %collective-permute-start.16 = (bf16[512,1024]{1,0:T(8,128)(2,1)S(1)}, bf16[512,1024]{1,0:T(8,128)(2,1)S(1)}, u32[]{:S(2)}, u32[]{:S(2)}) collective-permute-start(bf16[512,1024]{1,0:T(8,128)(2,1)S(1)} %copy-done.2), channel_id=1, source_target_pairs={{0,1},{1,0},{2,3},{3,2},{4,5},{5,4},{6,7},{7,6},{8,9},{9,8},{10,11... | collective-permute-start | bytes 3145736 | tf_op jit(solution)/shard_map/ppermute | solution.py:64
  97.1 25.3 %collective-permute-start.17 = (bf16[512,1024]{1,0:T(8,128)(2,1)S(1)}, bf16[512,1024]{1,0:T(8,128)(2,1)S(1)}, u32[]{:S(2)}, u32[]{:S(2)}) collective-permute-start(bf16[512,1024]{1,0:T(8,128)(2,1)S(1)} %copy-done.3), channel_id=1, source_target_pairs={{0,17},{17,0},{1,16},{16,1},{2,19},{19,2},{3,18},{18,3},{4,21},{21... | collective-permute-start | bytes 3145736 | tf_op jit(solution)/shard_map/ppermute | solution.py:68
  99.8 21.0 %collective-permute-start.15 = (bf16[96,2048]{1,0:T(8,128)(2,1)S(1)}, bf16[96,2048]{1,0:T(8,128)(2,1)S(1)}, u32[]{:S(2)}, u32[]{:S(2)}) collective-permute-start(bf16[96,2048]{1,0:T(8,128)(2,1)S(1)} %get-tuple-element.280), channel_id=1, source_target_pairs={{0,2},{2,4},{4,6},{6,0},{1,3},{3,5},{5,7},{7,1},{8,10},{10,12},{12... | collective-permute-start | bytes 1179656 | tf_op jit(solution)/shard_map/ppermute | solution.py:40
  122.4 23.1 %collective-permute-start.21 = (bf16[512,1024]{1,0:T(8,128)(2,1)S(1)}, bf16[512,1024]{1,0:T(8,128)(2,1)S(1)}, u32[]{:S(2)}, u32[]{:S(2)}) collective-permute-start(bf16[512,1024]{1,0:T(8,128)(2,1)S(1)} %copy-done.4), channel_id=1, source_target_pairs={{0,1},{1,0},{2,3},{3,2},{4,5},{5,4},{6,7},{7,6},{8,9},{9,8},{10,11... | collective-permute-start | bytes 3145736 | tf_op jit(solution)/shard_map/ppermute | solution.py:64
  123.5 24.4 %collective-permute-start.22 = (bf16[512,1024]{1,0:T(8,128)(2,1)S(1)}, bf16[512,1024]{1,0:T(8,128)(2,1)S(1)}, u32[]{:S(2)}, u32[]{:S(2)}) collective-permute-start(bf16[512,1024]{1,0:T(8,128)(2,1)S(1)} %copy-done.5), channel_id=1, source_target_pairs={{0,17},{17,0},{1,16},{16,1},{2,19},{19,2},{3,18},{18,3},{4,21},{21... | collective-permute-start | bytes 3145736 | tf_op jit(solution)/shard_map/ppermute | solution.py:68
  125.5 18.5 %collective-permute-start.18 = (bf16[96,2048]{1,0:T(8,128)(2,1)S(1)}, bf16[96,2048]{1,0:T(8,128)(2,1)S(1)}, u32[]{:S(2)}, u32[]{:S(2)}) collective-permute-start(bf16[96,2048]{1,0:T(8,128)(2,1)S(1)} %add_convert_fusion.5.b0.a0), channel_id=1, source_target_pairs={{0,2},{2,4},{4,6},{6,0},{1,3},{3,5},{5,7},{7,1},{8,10},{10,12},{12... | collective-permute-start | bytes 1179656 | tf_op jit(solution)/shard_map/ppermute | solution.py:40
  125.5 18.5 %collective-permute-start.19 = (bf16[96,2048]{1,0:T(8,128)(2,1)S(1)}, bf16[96,2048]{1,0:T(8,128)(2,1)S(1)}, u32[]{:S(2)}, u32[]{:S(2)}) collective-permute-start(bf16[96,2048]{1,0:T(8,128)(2,1)S(1)} %add_convert_fusion.5.b0.a0), channel_id=1, source_target_pairs={{0,4},{2,6},{4,0},{6,2},{1,5},{3,7},{5,1},{7,3},{8,12},{10,14},{12... | collective-permute-start | bytes 1179656 | tf_op jit(solution)/shard_map/ppermute | solution.py:40
  125.5 19.6 %collective-permute-start.20 = (bf16[96,2048]{1,0:T(8,128)(2,1)S(1)}, bf16[96,2048]{1,0:T(8,128)(2,1)S(1)}, u32[]{:S(2)}, u32[]{:S(2)}) collective-permute-start(bf16[96,2048]{1,0:T(8,128)(2,1)S(1)} %add_convert_fusion.5.b0.a0), channel_id=1, source_target_pairs={{0,6},{2,0},{4,2},{6,4},{1,7},{3,1},{5,3},{7,5},{8,14},{10,8},{12,... | collective-permute-start | bytes 1179656 | tf_op jit(solution)/shard_map/ppermute | solution.py:40
  151.5 13.5 %collective-permute-start.24 = (bf16[256,1024]{1,0:T(8,128)(2,1)S(1)}, bf16[256,1024]{1,0:T(8,128)(2,1)S(1)}, u32[]{:S(2)}, u32[]{:S(2)}) collective-permute-start(bf16[256,1024]{1,0:T(8,128)(2,1)S(1)} %copy-done.24), channel_id=1, source_target_pairs={{0,1},{1,0},{2,3},{3,2},{4,5},{5,4},{6,7},{7,6},{8,9},{9,8},{10,11... | collective-permute-start | bytes 1572872 | tf_op jit(solution)/shard_map/ppermute | solution.py:64
  151.7 14.5 %collective-permute-start.25 = (bf16[256,1024]{1,0:T(8,128)(2,1)S(1)}, bf16[256,1024]{1,0:T(8,128)(2,1)S(1)}, u32[]{:S(2)}, u32[]{:S(2)}) collective-permute-start(bf16[256,1024]{1,0:T(8,128)(2,1)S(1)} %copy-done.25), channel_id=1, source_target_pairs={{0,17},{17,0},{1,16},{16,1},{2,19},{19,2},{3,18},{18,3},{4,21},{21... | collective-permute-start | bytes 1572872 | tf_op jit(solution)/shard_map/ppermute | solution.py:68
  172.6 21.4 %collective-permute-start.30 = (bf16[768,1024]{1,0:T(8,128)(2,1)S(1)}, bf16[768,1024]{1,0:T(8,128)(2,1)S(1)}, u32[]{:S(2)}, u32[]{:S(2)}) collective-permute-start(bf16[768,1024]{1,0:T(8,128)(2,1)S(1)} %copy-done.57), channel_id=1, source_target_pairs={{0,8},{9,1},{8,9},{1,0},{2,10},{11,3},{10,11},{3,2},{4,12},{13,5},... | collective-permute-start | bytes 4718600 | tf_op jit(solution)/shard_map/ppermute | solution.py:126
  172.8 21.0 %collective-permute-start.29 = (bf16[96,2048]{1,0:T(8,128)(2,1)S(1)}, bf16[96,2048]{1,0:T(8,128)(2,1)S(1)}, u32[]{:S(2)}, u32[]{:S(2)}) collective-permute-start(bf16[96,2048]{1,0:T(8,128)(2,1)S(1)} %get-tuple-element.321), channel_id=1, source_target_pairs={{0,2},{2,4},{4,6},{6,0},{1,3},{3,5},{5,7},{7,1},{8,10},{10,12},{12... | collective-permute-start | bytes 1179656 | tf_op jit(solution)/shard_map/ppermute | solution.py:40
  195.4 17.7 %collective-permute-start.32 = (bf16[96,2048]{1,0:T(8,128)(2,1)S(1)}, bf16[96,2048]{1,0:T(8,128)(2,1)S(1)}, u32[]{:S(2)}, u32[]{:S(2)}) collective-permute-start(bf16[96,2048]{1,0:T(8,128)(2,1)S(1)} %add_convert_fusion.4.b0), channel_id=1, source_target_pairs={{0,4},{2,6},{4,0},{6,2},{1,5},{3,7},{5,1},{7,3},{8,12},{10,14},{12... | collective-permute-start | bytes 1179656 | tf_op jit(solution)/shard_map/ppermute | solution.py:40
  196.7 18.2 %collective-permute-start.33 = (bf16[96,2048]{1,0:T(8,128)(2,1)S(1)}, bf16[96,2048]{1,0:T(8,128)(2,1)S(1)}, u32[]{:S(2)}, u32[]{:S(2)}) collective-permute-start(bf16[96,2048]{1,0:T(8,128)(2,1)S(1)} %add_convert_fusion.4.b0), channel_id=1, source_target_pairs={{0,6},{2,0},{4,2},{6,4},{1,7},{3,1},{5,3},{7,5},{8,14},{10,8},{12,... | collective-permute-start | bytes 1179656 | tf_op jit(solution)/shard_map/ppermute | solution.py:40
  234.0 17.6 %collective-permute-start.37 = (bf16[96,2048]{1,0:T(8,128)(2,1)S(1)}, bf16[96,2048]{1,0:T(8,128)(2,1)S(1)}, u32[]{:S(2)}, u32[]{:S(2)}) collective-permute-start(bf16[96,2048]{1,0:T(8,128)(2,1)S(1)} %get-tuple-element.348), channel_id=1, source_target_pairs={{0,6},{2,0},{4,2},{6,4},{1,7},{3,1},{5,3},{7,5},{8,14},{10,8},{12,... | collective-permute-start | bytes 1179656 | tf_op jit(solution)/shard_map/ppermute | solution.py:40
  236.1 15.5 %collective-permute-start.38 = (bf16[96,2048]{1,0:T(8,128)(2,1)S(1)}, bf16[96,2048]{1,0:T(8,128)(2,1)S(1)}, u32[]{:S(2)}, u32[]{:S(2)}) collective-permute-start(bf16[96,2048]{1,0:T(8,128)(2,1)S(1)} %get-tuple-element.349), channel_id=1, source_target_pairs={{0,4},{2,6},{4,0},{6,2},{1,5},{3,7},{5,1},{7,3},{8,12},{10,14},{12... | collective-permute-start | bytes 1179656 | tf_op jit(solution)/shard_map/ppermute | solution.py:40
  236.1 20.4 %collective-permute-start.39 = (bf16[96,2048]{1,0:T(8,128)(2,1)S(1)}, bf16[96,2048]{1,0:T(8,128)(2,1)S(1)}, u32[]{:S(2)}, u32[]{:S(2)}) collective-permute-start(bf16[96,2048]{1,0:T(8,128)(2,1)S(1)} %get-tuple-element.350), channel_id=1, source_target_pairs={{0,2},{2,4},{4,6},{6,0},{1,3},{3,5},{5,7},{7,1},{8,10},{10,12},{12... | collective-permute-start | bytes 1179656 | tf_op jit(solution)/shard_map/ppermute | solution.py:40
  236.8 19.9 %collective-permute-start.40 = (bf16[384,1024]{1,0:T(8,128)(2,1)}, bf16[384,1024]{1,0:T(8,128)(2,1)S(1)}, u32[]{:S(2)}, u32[]{:S(2)}) collective-permute-start(bf16[384,1024]{1,0:T(8,128)(2,1)} %get-tuple-element.357), channel_id=1, source_target_pairs={{8,1},{1,9},{9,8},{10,3},{3,11},{11,10},{12,5},{5,13},{13,12},{14,... | collective-permute-start | bytes 2359304 | tf_op jit(solution)/shard_map/ppermute | solution.py:724
  241.2 17.1 %collective-permute-start.41 = (bf16[384,1024]{1,0:T(8,128)(2,1)}, bf16[384,1024]{1,0:T(8,128)(2,1)S(1)}, u32[]{:S(2)}, u32[]{:S(2)}) collective-permute-start(bf16[384,1024]{1,0:T(8,128)(2,1)} %get-tuple-element.358), channel_id=1, source_target_pairs={{0,1},{8,0},{1,8},{2,3},{10,2},{3,10},{4,5},{12,4},{5,12},{6,7},{1... | collective-permute-start | bytes 2359304 | tf_op jit(solution)/shard_map/ppermute | solution.py:724
  258.3 22.3 %collective-permute-start.46 = (bf16[512,1536]{1,0:T(8,128)(2,1)S(1)}, bf16[512,1536]{1,0:T(8,128)(2,1)S(1)}, u32[]{:S(2)}, u32[]{:S(2)}) collective-permute-start(bf16[512,1536]{1,0:T(8,128)(2,1)S(1)} %get-tuple-element.368), channel_id=1, source_target_pairs={{0,96},{8,25},{1,97},{9,8},{16,112},{24,9},{17,113},{25,24},{32,0}... | collective-permute-start | bytes 4718600 | tf_op jit(solution)/shard_map/ppermute | solution.py:56
  260.4 20.8 %collective-permute-start.45 = (bf16[512,1536]{1,0:T(8,128)(2,1)S(1)}, bf16[512,1536]{1,0:T(8,128)(2,1)S(1)}, u32[]{:S(2)}, u32[]{:S(2)}) collective-permute-start(bf16[512,1536]{1,0:T(8,128)(2,1)S(1)} %get-tuple-element.366), channel_id=1, source_target_pairs={{0,32},{8,9},{1,33},{9,24},{16,48},{24,25},{17,49},{25,8},{32,64},... | collective-permute-start | bytes 4718600 | tf_op jit(solution)/shard_map/ppermute | solution.py:56
  260.4 12.6 %collective-permute-start.42 = (bf16[96,2048]{1,0:T(8,128)(2,1)S(1)}, bf16[96,2048]{1,0:T(8,128)(2,1)S(1)}, u32[]{:S(2)}, u32[]{:S(2)}) collective-permute-start(bf16[96,2048]{1,0:T(8,128)(2,1)S(1)} %fusion.1.g0), channel_id=1, source_target_pairs={{0,2},{2,4},{4,6},{6,0},{1,3},{3,5},{5,7},{7,1},{8,10},{10,12},{12... | collective-permute-start | bytes 1179656 | tf_op jit(solution)/shard_map/ppermute | solution.py:40
  261.9 16.0 %collective-permute-start.43 = (bf16[96,2048]{1,0:T(8,128)(2,1)S(1)}, bf16[96,2048]{1,0:T(8,128)(2,1)S(1)}, u32[]{:S(2)}, u32[]{:S(2)}) collective-permute-start(bf16[96,2048]{1,0:T(8,128)(2,1)S(1)} %fusion.1.g0), channel_id=1, source_target_pairs={{0,4},{2,6},{4,0},{6,2},{1,5},{3,7},{5,1},{7,3},{8,12},{10,14},{12... | collective-permute-start | bytes 1179656 | tf_op jit(solution)/shard_map/ppermute | solution.py:40
  263.1 17.6 %collective-permute-start.44 = (bf16[96,2048]{1,0:T(8,128)(2,1)S(1)}, bf16[96,2048]{1,0:T(8,128)(2,1)S(1)}, u32[]{:S(2)}, u32[]{:S(2)}) collective-permute-start(bf16[96,2048]{1,0:T(8,128)(2,1)S(1)} %fusion.1.g0), channel_id=1, source_target_pairs={{0,6},{2,0},{4,2},{6,4},{1,7},{3,1},{5,3},{7,5},{8,14},{10,8},{12,... | collective-permute-start | bytes 1179656 | tf_op jit(solution)/shard_map/ppermute | solution.py:40
  286.0 13.4 %collective-permute-start.48 = (bf16[512,768]{1,0:T(8,128)(2,1)S(1)}, bf16[512,768]{1,0:T(8,128)(2,1)S(1)}, u32[]{:S(2)}, u32[]{:S(2)}) collective-permute-start(bf16[512,768]{1,0:T(8,128)(2,1)S(1)} %get-tuple-element.396), channel_id=1, source_target_pairs={{0,32},{8,9},{1,33},{9,24},{16,48},{24,25},{17,49},{25,8},{32,64},... | collective-permute-start | bytes 2359304 | tf_op jit(solution)/shard_map/ppermute | solution.py:56
  302.8 13.2 %collective-permute-start.54 = (bf16[512,768]{1,0:T(8,128)(2,1)S(1)}, bf16[512,768]{1,0:T(8,128)(2,1)S(1)}, u32[]{:S(2)}, u32[]{:S(2)}) collective-permute-start(bf16[512,768]{1,0:T(8,128)(2,1)S(1)} %get-tuple-element.402), channel_id=1, source_target_pairs={{0,32},{8,9},{1,33},{9,24},{16,48},{24,25},{17,49},{25,8},{32,64},... | collective-permute-start | bytes 2359304 | tf_op jit(solution)/shard_map/ppermute | solution.py:56
  324.8 107.5 %all-gather.4.cloned.1.call-start = ((), (), s32[]{:S(2)}) async-start(), calls=%async_computation.2 | async-start | bytes 1966080 | tf_op jit(solution)/shard_map/all_gather | solution.py:909
  327.4 44.6 %collective-permute-start.59 = (bf16[512,1536]{1,0:T(8,128)(2,1)}, bf16[512,1536]{1,0:T(8,128)(2,1)}, u32[]{:S(2)}, u32[]{:S(2)}) collective-permute-start(bf16[512,1536]{1,0:T(8,128)(2,1)} %copy-done.85), channel_id=1, source_target_pairs={{0,64},{8,24},{1,65},{9,25},{16,80},{24,8},{17,81},{25,9},{32,96},... | collective-permute-start | bytes 4718600 | tf_op jit(solution)/shard_map/ppermute | solution.py:56
  330.6 41.5 %collective-permute-start.60 = (bf16[512,1536]{1,0:T(8,128)(2,1)}, bf16[512,1536]{1,0:T(8,128)(2,1)}, u32[]{:S(2)}, u32[]{:S(2)}) collective-permute-start(bf16[512,1536]{1,0:T(8,128)(2,1)} %copy-done.86), channel_id=1, source_target_pairs={{0,64},{8,24},{1,65},{9,25},{16,80},{24,8},{17,81},{25,9},{32,96},... | collective-permute-start | bytes 4718600 | tf_op jit(solution)/shard_map/ppermute | solution.py:56
  353.8 17.5 %collective-permute-start.57 = (bf16[96,1024]{1,0:T(8,128)(2,1)S(1)}, bf16[96,1024]{1,0:T(8,128)(2,1)S(1)}, u32[]{:S(2)}, u32[]{:S(2)}) collective-permute-start(bf16[96,1024]{1,0:T(8,128)(2,1)S(1)} %get-tuple-element.562), channel_id=1, source_target_pairs={{8,1},{1,9},{9,8},{10,3},{3,11},{11,10},{12,5},{5,13},{13,12},{14,... | collective-permute-start | bytes 589832 | tf_op jit(solution)/shard_map/ppermute | solution.py:724
  358.3 12.9 %collective-permute-start.58 = (bf16[96,1024]{1,0:T(8,128)(2,1)S(1)}, bf16[96,1024]{1,0:T(8,128)(2,1)S(1)}, u32[]{:S(2)}, u32[]{:S(2)}) collective-permute-start(bf16[96,1024]{1,0:T(8,128)(2,1)S(1)} %get-tuple-element.563), channel_id=1, source_target_pairs={{0,1},{8,0},{1,8},{2,3},{10,2},{3,10},{4,5},{12,4},{5,12},{6,7},{1... | collective-permute-start | bytes 589832 | tf_op jit(solution)/shard_map/ppermute | solution.py:724
  372.1 29.6 %collective-permute-start.61 = (bf16[576,1024]{1,0:T(8,128)(2,1)}, bf16[576,1024]{1,0:T(8,128)(2,1)}, u32[]{:S(2)}, u32[]{:S(2)}) collective-permute-start(bf16[576,1024]{1,0:T(8,128)(2,1)} %copy-done.90), channel_id=1, source_target_pairs={{0,32},{8,9},{1,33},{9,24},{16,48},{24,25},{17,49},{25,8},{32,64},... | collective-permute-start | bytes 3538952 | tf_op jit(solution)/shard_map/ppermute | solution.py:56
  372.2 29.5 %collective-permute-start.62 = (bf16[576,1024]{1,0:T(8,128)(2,1)}, bf16[576,1024]{1,0:T(8,128)(2,1)}, u32[]{:S(2)}, u32[]{:S(2)}) collective-permute-start(bf16[576,1024]{1,0:T(8,128)(2,1)} %copy-done.89), channel_id=1, source_target_pairs={{0,64},{8,24},{1,65},{9,25},{16,80},{24,8},{17,81},{25,9},{32,96},... | collective-permute-start | bytes 3538952 | tf_op jit(solution)/shard_map/ppermute | solution.py:56
  373.4 29.0 %collective-permute-start.63 = (bf16[576,1024]{1,0:T(8,128)(2,1)S(1)}, bf16[576,1024]{1,0:T(8,128)(2,1)}, u32[]{:S(2)}, u32[]{:S(2)}) collective-permute-start(bf16[576,1024]{1,0:T(8,128)(2,1)S(1)} %copy-done.88), channel_id=1, source_target_pairs={{0,96},{8,25},{1,97},{9,8},{16,112},{24,9},{17,113},{25,24},{32,0}... | collective-permute-start | bytes 3538952 | tf_op jit(solution)/shard_map/ppermute | solution.py:56
  403.2 34.5 %collective-permute-start.69 = (bf16[256,1536]{1,0:T(8,128)(2,1)}, bf16[256,1536]{1,0:T(8,128)(2,1)S(1)}, u32[]{:S(2)}, u32[]{:S(2)}) collective-permute-start(bf16[256,1536]{1,0:T(8,128)(2,1)} %pad_maximum_fusion.3), channel_id=1, source_target_pairs={{0,17},{8,104},{1,0},{9,105},{16,1},{24,120},{17,16},{25,121},{32,... | collective-permute-start | bytes 2359304 | tf_op jit(solution)/shard_map/ppermute | solution.py:56
  407.3 30.5 %collective-permute-start.68 = (bf16[256,1536]{1,0:T(8,128)(2,1)}, bf16[256,1536]{1,0:T(8,128)(2,1)S(1)}, u32[]{:S(2)}, u32[]{:S(2)}) collective-permute-start(bf16[256,1536]{1,0:T(8,128)(2,1)} %pad_maximum_fusion.2), channel_id=1, source_target_pairs={{0,16},{8,72},{1,17},{9,73},{16,0},{24,88},{17,1},{25,89},{32,48},... | collective-permute-start | bytes 2359304 | tf_op jit(solution)/shard_map/ppermute | solution.py:56
  408.5 29.3 %collective-permute-start.67 = (bf16[256,1536]{1,0:T(8,128)(2,1)}, bf16[256,1536]{1,0:T(8,128)(2,1)S(1)}, u32[]{:S(2)}, u32[]{:S(2)}) collective-permute-start(bf16[256,1536]{1,0:T(8,128)(2,1)} %pad_maximum_fusion.1), channel_id=1, source_target_pairs={{0,1},{8,40},{1,16},{9,41},{16,17},{24,56},{17,0},{25,57},{32,33},... | collective-permute-start | bytes 2359304 | tf_op jit(solution)/shard_map/ppermute | solution.py:56
  413.3 18.4 %collective-permute-start.64 = (bf16[144,1024]{1,0:T(8,128)(2,1)S(1)}, bf16[144,1024]{1,0:T(8,128)(2,1)S(1)}, u32[]{:S(2)}, u32[]{:S(2)}) collective-permute-start(bf16[144,1024]{1,0:T(8,128)(2,1)S(1)} %get-tuple-element.561), channel_id=1, source_target_pairs={{0,1},{8,40},{1,16},{9,41},{16,17},{24,56},{17,0},{25,57},{32,33},... | collective-permute-start | bytes 884744 | tf_op jit(solution)/shard_map/ppermute | solution.py:56
  414.8 21.3 %collective-permute-start.65 = (bf16[144,1024]{1,0:T(8,128)(2,1)}, bf16[144,1024]{1,0:T(8,128)(2,1)S(1)}, u32[]{:S(2)}, u32[]{:S(2)}) collective-permute-start(bf16[144,1024]{1,0:T(8,128)(2,1)} %get-tuple-element.560), channel_id=1, source_target_pairs={{0,16},{8,72},{1,17},{9,73},{16,0},{24,88},{17,1},{25,89},{32,48},... | collective-permute-start | bytes 884744 | tf_op jit(solution)/shard_map/ppermute | solution.py:56
  (145 other events, 1681.0 us)
Sparse Core Ops, SparseCore 0:
  61.6 25.5 all-gather.5
  324.9 26.6 reduce-scatter.1
  382.0 26.4 all-gather.3
where the time goes:
time: 460 us; the launch traced here: 454 us
  waiting for transfers between devices  184 us (40%)
  starting transfers between devices  95.7 us (21%)
  Pallas kernels  91.5 us (20%)
  local copies, waits for them, and re-layouts  43 us (9%)
  other arithmetic  23.2 us (5%)
  between operations  16.3 us (4%)
    ppermute x24, waiting for transfers between devices, ring_shift(): return lax.ppermute(a, axes, [(i, (i + step) % RING) for i in range(RING)])  90.4 us
    pallas_call x32, Pallas kernels, call(): pl.pallas_call(kernel, in_specs=[pl.BlockSpec(memory_space=pltpu.SMEM if...  76.3 us
    ppermute x17, waiting for transfers between devices, plane_shift(): return lax.ppermute(a, ('y', 'xh', 'core', 'xl'), pairs)  40.2 us
    unnamed x238, local copies, waits for them, and re-layouts  29.7 us
    ppermute x24, starting transfers between devices, ring_shift(): return lax.ppermute(a, axes, [(i, (i + step) % RING) for i in range(RING)])  24.6 us
    ppermute x17, starting transfers between devices, plane_shift(): return lax.ppermute(a, ('y', 'xh', 'core', 'xl'), pairs)  24 us
    ppermute x6, waiting for transfers between devices, pair_swap(): return lax.ppermute(a, 'xl', [(0, 1), (1, 0)])  16.3 us
    ppermute x12, starting transfers between devices, core_swap(): return lax.ppermute(a, 'core', [(0, 1), (1, 0)])  15.2 us
  transfers between devices with their start and end apart: 75, of which 42 were waited for; matrix products, arithmetic and copies ran while one was open for 8% of the time, Pallas kernels for 15%

commit v1 on v0

--- a/solution.py
+++ b/solution.py
@@ -198,7 +198,7 @@
 
 
 PIECES = (
-    (("gate", 0),), (("gate", 1),),
+    (("gate", 0), ("mix", 0)), (("gate", 1), ("mix", 1)),
     (("gate", 2), ("up", 0)), (("gate", 3), ("up", 1)),
     (("up", 2), ("down", 0)), (("up", 3), ("down", 1)),
     (("down", 2),), (("down", 3),),
@@ -206,22 +206,35 @@
 PART = 256
 
 
-def cut_pieces(at, w_gate, w_up, w_down):
+def part_height(name):
+    return 128 if name == "mix" else PART
+
+
+def part_starts(piece):
+    heights = [part_height(name) for name, _ in piece]
+    return [sum(heights[:i]) for i in range(len(heights) + 1)]
+
+
+def cut_pieces(at, w_gate, w_up, w_down, w_mix):
     def plan(table, ins, outs):
-        named = dict(zip(("gate", "up", "down"), ins))
+        named = dict(zip(("gate", "up", "down", "mix"), ins))
         copies = []
         for out, piece in zip(outs, PIECES):
-            for i, (name, part) in enumerate(piece):
-                if name == "down":
-                    rows = pl.ds(pl.multiple_of(table[0] * NEAR + PART * part, PART), PART)
-                    source = named[name].at[rows]
+            for start, (name, part) in zip(part_starts(piece), piece):
+                height = part_height(name)
+                if name in ("down", "mix"):
+                    half = named[name].shape[0] // 2
+                    first = pl.multiple_of(table[0] * half + height * part, height)
+                    source = named[name].at[pl.ds(first, height)]
                 else:
-                    source = named[name].at[pl.ds(PART * part, PART), at_block(table[0], NEAR)]
-                copies.append((source, out.at[pl.ds(PART * i, PART)]))
+                    rows = pl.ds(height * part, height)
+                    source = named[name].at[rows, at_block(table[0], NEAR)]
+                copies.append((source, out.at[pl.ds(start, height)]))
         return copies
 
-    shapes = [(PART * len(piece), NEAR) for piece in PIECES]
-    return place(plan, 12, shapes, [at.c], w_gate, w_up, w_down, params=EARLY)
+    shapes = [(part_starts(piece)[-1], NEAR) for piece in PIECES]
+    count = sum(len(piece) for piece in PIECES)
+    return place(plan, count, shapes, [at.c], w_gate, w_up, w_down, w_mix, params=EARLY)
 
 
 def pieces_with(name):
@@ -231,9 +244,9 @@
 def views(name, refs):
     out = []
     for ref, k in zip(refs, pieces_with(name)):
-        for i, (found, _) in enumerate(PIECES[k]):
+        for start, (found, _) in zip(part_starts(PIECES[k]), PIECES[k]):
             if found == name:
-                out.append(ref.at[pl.ds(PART * i, PART)])
+                out.append(ref.at[pl.ds(start, part_height(name))])
     return out
 
 
@@ -281,6 +294,17 @@
     total = lax.optimization_barrier(total.astype(LOW))
     height = own.shape[0] // RING
     return [total[height * i : height * (i + 1)] for i in range(RING)]
+
+
+def sum_kernel(p0, p1, p2, p3, *outs):
+    for i, out in enumerate(outs):
+        at = slice(128 * i, 128 * (i + 1))
+        total = p0[at, :].astype(F32) + p1[at, :].astype(F32)
+        out[...] = (total + p2[at, :].astype(F32) + p3[at, :].astype(F32)).astype(LOW)
+
+
+def plane_parts(own, came):
+    return call(sum_kernel, [((128, own.shape[1]), LOW)] * RING, own, *came)
 
 
 def share_kernel(core, p0, p1, p2, p3, own_ref, sent_ref):
@@ -301,15 +325,12 @@
     first = core[0] == 0
     own, came = own_ref[...], came_ref[...].astype(F32)
     sides = jnp.where(first, own, came), jnp.where(first, came, own)
-    for i, (out, pieces) in enumerate(zip(outs, plan)):
+    for out, pieces in zip(outs, plan):
         at = 0
         for side in sides:
             for rows, start, width in pieces:
                 value = side[64 * rows : 64 * (rows + 1), start : start + width]
-                if i == len(plan) - 1:
-                    out[at : at + width, :] = value.T
-                else:
-                    out[:, at : at + width] = value
+                out[:, at : at + width] = value
                 at += width
     if len(outs) > len(plan):
         width_ref, heads_ref = outs[len(plan) :]
@@ -325,7 +346,7 @@
     core = at.c.reshape(1).astype(jnp.int32)
     own, sent = call(share_kernel, [(shape, F32), (shape, LOW)], core, own, *came, scalars=1)
     widths = [2 * sum(piece[2] for piece in pieces) for pieces in plan]
-    shapes = [((64, width), F32) for width in widths[:-1]] + [((widths[-1], 64), F32)]
+    shapes = [((64, width), F32) for width in widths]
     shapes += [(shape, F32) for shape in extra]
     return call(functools.partial(wide_kernel, plan), shapes, core, own, core_swap(sent), scalars=1)
 
@@ -386,15 +407,18 @@
     return ref[OWN * half : OWN * (half + 1), :]
 
 
-def mix(left, half, near, far, dtype):
+def mix(left, half, pieces, dtype):
+    count = len(pieces) // 2
+
     def body(refs):
-        left, near, far = refs
+        left, *w = refs
         left = half_rows(left, half)
-        for at in strips(NEAR, 512):
-            yield at, dot(left, near[:, at])
-            yield slice(NEAR + at.start, NEAR + at.stop), dot(left, far[:, at])
-
-    return product(body, dtype, left, near, far)
+        for i in range(2):
+            blocks = views("mix", w[count * i : count * (i + 1)])
+            for at in strips(NEAR, 512):
+                yield slice(NEAR * i + at.start, NEAR * i + at.stop), row_dot(left, blocks, at)
+
+    return product(body, dtype, left, *pieces)
 
 
 def down(units, pieces, dtype):
@@ -561,7 +585,7 @@
     return v * cosines - pltpu.roll(v, HEAD // 2, 1) * sines
 
 
-TILE = 256
+TILE = 384
 
 
 def seen(table_ref, row_ref, lo):
@@ -599,13 +623,15 @@
 
 def attend_back_kernel(
     qkv_ref, scale_ref, gain_ref, table_ref, row_ref, low_ref,
-    own_ref, other_ref, near_ref, far_ref,
+    own_ref, other_ref, near0, near1, far0, far1,
     hat_ref, value_ref, dots_ref, part_ref, dk_ref, dv_ref, grad_ref,
 ):
     cosines, sines = table_ref[:, :HEAD], table_ref[:, HEAD : 2 * HEAD]
     for i, ref in enumerate((own_ref, other_ref)):
-        grad = dot(ref[:, :NEAR], near_ref[...], NT) + dot(ref[:, NEAR:], far_ref[...], NT)
-        grad_ref[OWN * i : OWN * (i + 1), :] = grad.astype(LOW)
+        pairs = zip(views("mix", (near0, near1)), views("mix", (far0, far1)))
+        for k, (near, far) in enumerate(pairs):
+            grad = dot(ref[:, :NEAR], near[...], NT) + dot(ref[:, NEAR:], far[...], NT)
+            grad_ref[OWN * i : OWN * (i + 1), 128 * k : 128 * (k + 1)] = grad.astype(LOW)
     for h in range(2):
         at = slice(h * HEAD, (h + 1) * HEAD)
         k_at = slice(256 + h * HEAD, 256 + (h + 1) * HEAD)
@@ -737,8 +763,7 @@
     first = first_hop(inputs)
     near_qkv = cut_columns(at, (768, 256), w_query, w_key, w_value)
     far_qkv = [wrap_swap(near_qkv[0]), pair_swap(near_qkv[1])]
-    near_mix = lax.dynamic_slice_in_dim(w_mix, at.c * 256, 256, 0)
-    near = cut_pieces(at, after(w_gate, near_qkv), w_up, w_down)
+    near = cut_pieces(at, after(w_gate, near_qkv), w_up, w_down, w_mix)
 
     gains = jnp.concatenate([attn_gain, ffn_gain, query_gain, key_gain])
     their_gains = pair_swap(gains)
@@ -772,17 +797,17 @@
     qkv_blocks = [*near_qkv, *far_qkv]
     qkv, squares = call(qkv_kernel, [((SEQ, SEQ), F32), ((8, SEQ), F32)], states, *qkv_blocks)
     far = fetch(*after(near[:2], far_qkv))
-    both_mix = lax.all_gather(after(near_mix, far_qkv), "xl")
     squares = all_stats(squares)
-    squares, far = lax.optimization_barrier((squares, far))
-    far_mix = jnp.where(at.s == 0, both_mix[1], both_mix[0])
+    squares = lax.optimization_barrier(squares)
     mixed, low, scales = call(
         attend_kernel,
         [((SEQ, 256), LOW), ((SEQ, SEQ), LOW), ((SEQ, 8), F32)],
         qkv, squares, head_gains, *tables,
     )
-    came = core_swap(mix(mixed, 1, near_mix, far_mix, LOW))
-    mix_parts = settle(mix(mixed, 0, near_mix, far_mix, F32), came)
+    mixed, far = lax.optimization_barrier((mixed, far))
+    mixes = [*near[:2], *far[:2]]
+    came = core_swap(mix(mixed, 1, mixes, LOW))
+    mix_parts = settle(mix(mixed, 0, mixes, F32), came)
     mix_parts = lax.optimization_barrier(mix_parts)
     far = [*far, *fetch(*after(near[2:4], mix_parts))]
     attn_sum = scatter_z(mix_parts).astype(LOW)
@@ -875,7 +900,7 @@
     hat, value_back, dots, head_parts = call(
         attend_back_kernel,
         [((SEQ, 512), F32), ((SEQ, 256), LOW), ((8, SEQ), F32), ((2, 256), F32)],
-        qkv, scales, head_gains, *tables, low, mix_own, mix_other, near_mix, far_mix,
+        qkv, scales, head_gains, *tables, low, mix_own, mix_other, *mixes,
         scratch=[pltpu.VMEM((SEQ, HEAD), F32)] * 2 + [pltpu.VMEM((SEQ, 256), LOW)],
     )
     hat, dots, came1a, up1, down1 = lax.optimization_barrier((hat, dots, came1a, up1, down1))
@@ -923,19 +948,20 @@
     block_out, came0, came1, came1a, came1b = lax.optimization_barrier(
         (block_out, came0, came1, came1a, came1b)
     )
-    rows0 = plane_sum(grads0[0], [came0[i] for i in (1, 2, 3)])
+    rows0 = plane_parts(grads0[0], [came0[i] for i in (1, 2, 3)])
     came1b = [jnp.concatenate(halves, axis=1) for halves in zip(came1a, came1b)]
-    rows1 = plane_sum(keep1, [*came1b, came1])
-    attn_came, rows0, rows1 = lax.optimization_barrier((attn_came, rows0, rows1))
+    rows1 = plane_parts(keep1, [*came1b, came1])
     ffn_rows = [jnp.concatenate(rows) for rows in zip(rows0, rows1)]
-    ffn_came = [plane_shift(ffn_rows[i], i, True) for i in range(1, RING)]
+    ffn_came = {i: plane_shift(ffn_rows[i], i, True) for i in (1, 3)}
+    attn_came, ffn_came = lax.optimization_barrier((attn_came, ffn_came))
+    ffn_came[2] = plane_shift(after(ffn_rows[2], ffn_came), 2, True)
     attn_rows = plane_sum(attn_grads[0], attn_came)
     attn_came = [plane_shift(attn_rows[i], i, True) for i in range(1, RING)]
-    attn_came, ffn_came, input_grad = lax.optimization_barrier((attn_came, ffn_came, input_grad))
+    attn_came, input_grad = lax.optimization_barrier((attn_came, input_grad))
     gate_out, up_out, down_out = share_cores(
         at,
         ffn_rows[0],
-        ffn_came,
+        [ffn_came[i] for i in (1, 2, 3)],
         [[(0, 0, 1024)], [(0, 1024, 512), (1, 0, 512)], [(1, 512, 1024)]],
     )
     query, key, value, mix_out, width, heads = share_cores(
@@ -947,7 +973,7 @@
     heads = jnp.where(flip, heads[:, 16:], heads[:, :16])
 
     return (
-        block_out, input_grad, query, key, value, mix_out, gate_out, up_out, down_out,
+        block_out, input_grad, query, key, value, mix_out.T, gate_out, up_out, down_out.T,
         width[0], width[1], heads[0], heads[1],
     )
 

time: 460 us -> 442 us (0.961)
  waiting for transfers between devices: 184 us -> 168 us
  Pallas kernels: 91.5 us -> 102 us
  other arithmetic: 23.2 us -> 17.5 us
  local copies, waits for them, and re-layouts: 43 us -> 37.8 us
    pallas_call x32 -> x34, Pallas kernels: 76.3 us -> 86.6 us  [call(): pl.pallas_call(kernel, in_specs=[pl.BlockSpec(memory_space=pltpu.SMEM if...]
    ppermute x17, waiting for transfers between devices: 40.2 us -> 32.1 us  [plane_shift(): return lax.ppermute(a, ('y', 'xh', 'core', 'xl'), pairs)]
    convert_element_type x3 -> x1, other arithmetic: 9.52 us -> 3.03 us  [plane_sum(): total = lax.optimization_barrier(total.astype(LOW))]
    unnamed x238 -> x174, local copies, waits for them, and re-layouts: 29.7 us -> 24.2 us
    ppermute x6, waiting for transfers between devices: 16.3 us -> 10.8 us  [pair_swap(): return lax.ppermute(a, 'xl', [(0, 1), (1, 0)])]
  transfers between devices with their start and end apart: 75 -> 74, of which waited for: 42 -> 45; matrix products, arithmetic and copies ran while one was open for 8% -> 7% of each run, Pallas kernels for 15% -> 18%
where the time goes in v1:
time: 442 us; the launch traced here: 435 us
  waiting for transfers between devices  168 us (38%)
  Pallas kernels  102 us (23%)
  starting transfers between devices  93.3 us (21%)
  local copies, waits for them, and re-layouts  37.8 us (9%)
  other arithmetic  17.5 us (4%)
  between operations  16.4 us (4%)
    ppermute x24, waiting for transfers between devices, ring_shift(): return lax.ppermute(a, axes, [(i, (i + step) % RING) for i in range(RING)])  89.7 us
    pallas_call x34, Pallas kernels, call(): pl.pallas_call(kernel, in_specs=[pl.BlockSpec(memory_space=pltpu.SMEM if...  86.6 us
    ppermute x17, waiting for transfers between devices, plane_shift(): return lax.ppermute(a, ('y', 'xh', 'core', 'xl'), pairs)  32.1 us
    ppermute x17, starting transfers between devices, plane_shift(): return lax.ppermute(a, ('y', 'xh', 'core', 'xl'), pairs)  25.5 us
    unnamed x174, local copies, waits for them, and re-layouts  24.2 us
    ppermute x24, starting transfers between devices, ring_shift(): return lax.ppermute(a, axes, [(i, (i + step) % RING) for i in range(RING)])  24.1 us
    ppermute x12, starting transfers between devices, core_swap(): return lax.ppermute(a, 'core', [(0, 1), (1, 0)])  14.5 us
    ppermute x4, starting transfers between devices, shuffle(): lax.ppermute(sent[k], ('core', 'xl'), [p for p in perm if p[0] != p[1]])  12.8 us
  transfers between devices with their start and end apart: 74, of which 45 were waited for; matrix products, arithmetic and copies ran while one was open for 7% of the time, Pallas kernels for 18%

profile of v1, /device:TPU:1, one launch (start us, length us, event | category | flops | bytes accessed | tf_op | source)
XLA Modules:
  0.0 435.4 jit_solution(4285424780125245949)
XLA Ops:
  11.5 2.5 shard_map.237
  18.5 5.9 %shard_map.238 = (bf16[384,1024]{1,0:T(8,128)(2,1)}, bf16[384,1024]{1,0:T(8,128)(2,1)}, bf16[512,1024]{1,0:T(8,128)(2,1)}, bf16[512,1024]{1,0:T(8,128)(2,1)}, bf...) custom-call(s32[1]{0:T(128)} %bitcast.table.core_ref.core, ...), custom_call_target="tpu_custom_call" | custom-call | tf_op jit(solution)/shard_map/pallas_call | solution.py:109
  27.3 3.1 multiply_sine_fusion
  34.5 2.4 concatenate.81.table_ref
  39.6 3.2 collective-permute-done.3.refs_2_.refs_3_
  54.4 2.8 shard_map.240
  58.5 4.0 collective-permute-start.9
  66.4 3.5 collective-permute-done.7
  70.1 5.7 %shard_map.241 = (bf16[768,256]{1,0:T(8,128)(2,1)S(1)}, bf16[768,768]{1,0:T(8,128)(2,1)S(1)}, f32[768,8]{1,0:T(8,128)S(1)}) custom-call(f32[768,768]{1,0:T(8,128)S(1)} %get-tuple-element.264.qkv_ref, f32[8,768]{1,0:T(8,128)S(1)} %fusion.3.sums_ref, f32[2,256]{1,0:T(2,128)S(1)} %copy-done.58, f32[768,384]{1,0:T(8,128)S(1)} %copy-done.9, f32[1,768]{1,0:T(1,128)S(1)} %copy-done.57), custom_call_target="tpu_custom_call" | custom-call | tf_op jit(solution)/shard_map/pallas_call | solution.py:355
  75.9 5.3 %collective-permute-done.10.refs_3_.refs_4_.refs_6_.far0 = bf16[384,1024]{1,0:T(8,128)(2,1)S(1)} collective-permute-done((bf16[384,1024]{1,0:T(8,128)(2,1)S(1)}, bf16[384,1024]{1,0:T(8,128)(2,1)S(1)}, u32[]{:S(2)}, u32[]{:S(2)}) %collective-permute-start.10) | collective-permute-done | bytes 786464 | tf_op jit(solution)/shard_map/ppermute | solution.py:64
  92.4 8.2 %collective-permute-done.13 = bf16[96,2048]{1,0:T(8,128)(2,1)S(1)} collective-permute-done((bf16[96,2048]{1,0:T(8,128)(2,1)S(1)}, bf16[96,2048]{1,0:T(8,128)(2,1)S(1)}, u32[]{:S(2)}, u32[]{:S(2)}) %collective-permute-start.13) | collective-permute-done | bytes 393248 | tf_op jit(solution)/shard_map/ppermute | solution.py:40
  102.0 10.0 %collective-permute-done.15 = bf16[96,2048]{1,0:T(8,128)(2,1)S(1)} collective-permute-done((bf16[96,2048]{1,0:T(8,128)(2,1)S(1)}, bf16[96,2048]{1,0:T(8,128)(2,1)S(1)}, u32[]{:S(2)}, u32[]{:S(2)}) %collective-permute-start.15) | collective-permute-done | bytes 393248 | tf_op jit(solution)/shard_map/ppermute | solution.py:40
  119.1 8.2 %collective-permute-done.18.b1.a1 = bf16[96,2048]{1,0:T(8,128)(2,1)S(1)} collective-permute-done((bf16[96,2048]{1,0:T(8,128)(2,1)S(1)}, bf16[96,2048]{1,0:T(8,128)(2,1)S(1)}, u32[]{:S(2)}, u32[]{:S(2)}) %collective-permute-start.18) | collective-permute-done | bytes 393248 | tf_op jit(solution)/shard_map/ppermute | solution.py:40
  127.4 5.7 %collective-permute-done.19.b2.a2 = bf16[96,2048]{1,0:T(8,128)(2,1)S(1)} collective-permute-done((bf16[96,2048]{1,0:T(8,128)(2,1)S(1)}, bf16[96,2048]{1,0:T(8,128)(2,1)S(1)}, u32[]{:S(2)}, u32[]{:S(2)}) %collective-permute-start.19) | collective-permute-done | bytes 393248 | tf_op jit(solution)/shard_map/ppermute | solution.py:40
  133.1 2.8 collective-permute-done.20.b3.a3
  139.8 2.7 collective-permute-start.23
  144.7 3.4 shard_map.246
  149.0 3.4 shard_map.247
  152.5 3.4 collective-permute-done.24.refs_7_.refs_6_
  165.3 8.9 %collective-permute-done.27 = bf16[96,2048]{1,0:T(8,128)(2,1)S(1)} collective-permute-done((bf16[96,2048]{1,0:T(8,128)(2,1)S(1)}, bf16[96,2048]{1,0:T(8,128)(2,1)S(1)}, u32[]{:S(2)}, u32[]{:S(2)}) %collective-permute-start.27) | collective-permute-done | bytes 393248 | tf_op jit(solution)/shard_map/ppermute | solution.py:40
  175.5 9.4 %collective-permute-done.29 = bf16[96,2048]{1,0:T(8,128)(2,1)S(1)} collective-permute-done((bf16[96,2048]{1,0:T(8,128)(2,1)S(1)}, bf16[96,2048]{1,0:T(8,128)(2,1)S(1)}, u32[]{:S(2)}, u32[]{:S(2)}) %collective-permute-start.29) | collective-permute-done | bytes 393248 | tf_op jit(solution)/shard_map/ppermute | solution.py:40
  191.5 6.9 %collective-permute-done.31.b1 = bf16[96,2048]{1,0:T(8,128)(2,1)S(1)} collective-permute-done((bf16[96,2048]{1,0:T(8,128)(2,1)S(1)}, bf16[96,2048]{1,0:T(8,128)(2,1)S(1)}, u32[]{:S(2)}, u32[]{:S(2)}) %collective-permute-start.31) | collective-permute-done | bytes 393248 | tf_op jit(solution)/shard_map/ppermute | solution.py:40
  198.5 5.7 %collective-permute-done.32.b2 = bf16[96,2048]{1,0:T(8,128)(2,1)S(1)} collective-permute-done((bf16[96,2048]{1,0:T(8,128)(2,1)S(1)}, bf16[96,2048]{1,0:T(8,128)(2,1)S(1)}, u32[]{:S(2)}, u32[]{:S(2)}) %collective-permute-start.32) | collective-permute-done | bytes 393248 | tf_op jit(solution)/shard_map/ppermute | solution.py:40
  219.1 3.4 shard_map.257
  223.1 3.4 shard_map.256.own_ref
  231.2 4.4 %collective-permute-start.40 = (bf16[384,1024]{1,0:T(8,128)(2,1)}, bf16[384,1024]{1,0:T(8,128)(2,1)S(1)}, u32[]{:S(2)}, u32[]{:S(2)}) collective-permute-start(bf16[384,1024]{1,0:T(8,128)(2,1)} %get-tuple-element.355), channel_id=1, source_target_pairs={{8,1},{1,9},{9,8},{10,3},{3,11},{11,10},{12,5},{5,13},{13,12},{14,... | collective-permute-start | bytes 2359304 | tf_op jit(solution)/shard_map/ppermute | solution.py:750
  237.5 8.5 %shard_map.259 = (bf16[512,1536]{1,0:T(8,128)(2,1)S(1)}, bf16[512,1536]{1,0:T(8,128)(2,1)S(1)}, bf16[512,1536]{1,0:T(8,128)(2,1)S(1)}, bf16[512,1536]{1,0:T(8,128)(2,1)}) custom-call(s32[16]{0:T(128)S(1)} %copy-done.61, bf16[384,2048]{1,0:T(8,128)(2,1)S(1)} %get-tuple-element.367.rows_ref.refs_1_, ...), custom_call_target="tpu_custom_call" | custom-call | tf_op jit(solution)/shard_map/pallas_call | solution.py:355
  247.2 3.7 collective-permute-done.39
  258.8 7.3 %shard_map.260 = (bf16[512,1536]{1,0:T(8,128)(2,1)S(1)}, bf16[512,768]{1,0:T(8,128)(2,1)S(1)}, bf16[512,768]{1,0:T(8,128)(2,1)S(1)}, bf16[512,1536]{1,0:T(8,128)...) custom-call(s32[16]{0:T(128)S(1)} %copy-done.61, ...), custom_call_target="tpu_custom_call" | custom-call | tf_op jit(solution)/shard_map/pallas_call | solution.py:355
  267.2 5.4 %collective-permute-done.43.g2 = bf16[96,2048]{1,0:T(8,128)(2,1)S(1)} collective-permute-done((bf16[96,2048]{1,0:T(8,128)(2,1)S(1)}, bf16[96,2048]{1,0:T(8,128)(2,1)S(1)}, u32[]{:S(2)}, u32[]{:S(2)}) %collective-permute-start.43) | collective-permute-done | bytes 393248 | tf_op jit(solution)/shard_map/ppermute | solution.py:40
  272.7 2.6 collective-permute-done.44.g3
  277.5 2.4 collective-permute-start.47
  284.2 7.9 %shard_map.262 = (f32[768,512]{1,0:T(8,128)S(1)}, bf16[768,256]{1,0:T(8,128)(2,1)S(1)}, f32[8,768]{1,0:T(8,128)S(1)}, f32[2,256]{1,0:T(2,128)S(1)}) custom-call(f32[768,768]{1,0:T(8,128)S(1)} %get-tuple-element.264.qkv_ref, f32[768,8]{1,0:T(8,128)S(1)} %get-tuple-element.360.scale_ref.rms_ref, f32[2,256]{1,0:T(2,128)S(1)} %copy-done.58, ...), custom_call_target="tpu_custom_call" | custom-call | tf_op jit(solution)/shard_map/pallas_call | solution.py:355
  302.4 4.1 collective-permute-done.51
  306.7 3.2 collective-permute-done.54
  320.4 2.8 collective-permute-start.59
  328.1 6.2 %shard_map.267 = (bf16[576,1024]{1,0:T(8,128)(2,1)S(1)}, bf16[576,1024]{1,0:T(8,128)(2,1)}, bf16[576,1024]{1,0:T(8,128)(2,1)}, bf16[576,1024]{1,0:T(8,128)(2,1)}) custom-call(s32[16]{0:T(128)S(1)} %copy-done.62, bf16[768,2048]{1,0:T(8,128)(2,1)S(1)} %shard_map.239.states_ref.refs_1_, bf16[768,768]{1,0:T(8,128)(2,1)S(1)} %copy-done.7, ...), custom_call_target="tpu_custom_call" | custom-call | tf_op jit(solution)/shard_map/pallas_call | solution.py:355
  335.4 9.2 %reduce-scatter.2.cloned.1.call-done = bf16[96,2048]{1,0:T(8,128)(2,1)} async-done(((bf16[384,2048]{1,0:T(8,128)(2,1)}), bf16[96,2048]{1,0:T(8,128)(2,1)}) %reduce-scatter.2.cloned.1.call-update) | async-done | bytes 393232 | tf_op jit(solution)/shard_map/reduce_scatter | solution.py:918
  346.7 4.6 %collective-permute-start.57 = (bf16[96,1024]{1,0:T(8,128)(2,1)S(1)}, bf16[96,1024]{1,0:T(8,128)(2,1)S(1)}, u32[]{:S(2)}, u32[]{:S(2)}) collective-permute-start(bf16[96,1024]{1,0:T(8,128)(2,1)S(1)} %get-tuple-element.487), channel_id=1, source_target_pairs={{8,1},{1,9},{9,8},{10,3},{3,11},{11,10},{12,5},{5,13},{13,12},{14,... | collective-permute-start | bytes 589832 | tf_op jit(solution)/shard_map/ppermute | solution.py:750
  354.1 3.8 shard_map.268
  357.9 6.0 %collective-permute-done.57 = bf16[96,1024]{1,0:T(8,128)(2,1)S(1)} collective-permute-done((bf16[96,1024]{1,0:T(8,128)(2,1)S(1)}, bf16[96,1024]{1,0:T(8,128)(2,1)S(1)}, u32[]{:S(2)}, u32[]{:S(2)}) %collective-permute-start.57) | collective-permute-done | bytes 196640 | tf_op jit(solution)/shard_map/ppermute | solution.py:750
  376.0 2.7 collective-permute-start.65
  378.9 17.2 %collective-permute-done.65.p3 = bf16[256,1536]{1,0:T(8,128)(2,1)S(1)} collective-permute-done((bf16[256,1536]{1,0:T(8,128)(2,1)S(1)}, bf16[256,1536]{1,0:T(8,128)(2,1)S(1)}, u32[]{:S(2)}, u32[]{:S(2)}) %collective-permute-start.65) | collective-permute-done | bytes 786464 | tf_op jit(solution)/shard_map/ppermute | solution.py:56
  396.1 3.9 collective-permute-done.64.p1
  403.1 3.6 collective-permute-start.70
  406.7 3.0 add_convert_fusion
  413.5 2.8 collective-permute-done.70.p2
  420.5 2.4 shard_map.271
  (396 shorter events, 177.3 us)
Async XLA Ops:
  7.2 337.3 %reduce-scatter.2.cloned.1.call-start = ((), (), s32[]{:S(2)}) async-start(), calls=%async_computation.1 | async-start | bytes 1966080 | tf_op jit(solution)/shard_map/reduce_scatter | solution.py:918
  7.2 17.2 %collective-permute-start = (s32[768]{0:T(1024)}, s32[768]{0:T(1024)S(1)}, u32[]{:S(2)}, u32[]{:S(2)}) collective-permute-start(s32[768]{0:T(1024)} %param.15), channel_id=1, source_target_pairs={{0,8},{8,0},{1,9},{9,1},{2,10},{10,2},{3,11},{11,3},{4,12},{12,4},... | collective-permute-start | bytes 9224 | tf_op jit(solution)/shard_map/ppermute | solution.py:60
  10.1 26.8 %collective-permute-start.1 = (f32[2560]{0:T(1024)}, f32[2560]{0:T(1024)}, u32[]{:S(2)}, u32[]{:S(2)}) collective-permute-start(f32[2560]{0:T(1024)} %pad_maximum_fusion.8), channel_id=1, source_target_pairs={{0,1},{1,0},{2,3},{3,2},{4,5},{5,4},{6,7},{7,6},{8,9},{9,8},{10,11... | collective-permute-start | bytes 30728 | tf_op jit(solution)/shard_map/ppermute | solution.py:64
  11.4 28.2 %collective-permute-start.2 = (bf16[768,1024]{1,0:T(8,128)(2,1)}, bf16[768,1024]{1,0:T(8,128)(2,1)S(1)}, u32[]{:S(2)}, u32[]{:S(2)}) collective-permute-start(bf16[768,1024]{1,0:T(8,128)(2,1)} %a_ref.2), channel_id=1, source_target_pairs={{0,8},{9,1},{8,9},{1,0},{2,10},{11,3},{10,11},{3,2},{4,12},{13,5},... | collective-permute-start | bytes 4718600 | tf_op jit(solution)/shard_map/ppermute | solution.py:126
  14.1 28.7 %collective-permute-start.3 = (bf16[768,768]{1,0:T(8,128)(2,1)}, bf16[768,768]{1,0:T(8,128)(2,1)S(1)}, u32[]{:S(2)}, u32[]{:S(2)}) collective-permute-start(bf16[768,768]{1,0:T(8,128)(2,1)} %get-tuple-element.247.refs_0_.refs_1_), channel_id=1, source_target_pairs={{0,17},{17,0},{1,16},{16,1},{2,19},{19,2},{3,18},{18,3},{4,21},{21... | collective-permute-start | bytes 3538952 | tf_op jit(solution)/shard_map/ppermute | solution.py:68
  16.1 23.5 %collective-permute-start.4 = (bf16[256,768]{1,0:T(8,128)(2,1)}, bf16[256,768]{1,0:T(8,128)(2,1)S(1)}, u32[]{:S(2)}, u32[]{:S(2)}) collective-permute-start(bf16[256,768]{1,0:T(8,128)(2,1)} %get-tuple-element.248.refs_1_.refs_2_), channel_id=1, source_target_pairs={{0,1},{1,0},{2,3},{3,2},{4,5},{5,4},{6,7},{7,6},{8,9},{9,8},{10,11... | collective-permute-start | bytes 1179656 | tf_op jit(solution)/shard_map/ppermute | solution.py:64
  62.5 18.7 %collective-permute-start.10 = (bf16[384,1024]{1,0:T(8,128)(2,1)S(1)}, bf16[384,1024]{1,0:T(8,128)(2,1)S(1)}, u32[]{:S(2)}, u32[]{:S(2)}) collective-permute-start(bf16[384,1024]{1,0:T(8,128)(2,1)S(1)} %copy-done.4), channel_id=1, source_target_pairs={{0,1},{1,0},{2,3},{3,2},{4,5},{5,4},{6,7},{7,6},{8,9},{9,8},{10,11... | collective-permute-start | bytes 2359304 | tf_op jit(solution)/shard_map/ppermute | solution.py:64
  62.9 19.3 %collective-permute-start.11 = (bf16[384,1024]{1,0:T(8,128)(2,1)S(1)}, bf16[384,1024]{1,0:T(8,128)(2,1)S(1)}, u32[]{:S(2)}, u32[]{:S(2)}) collective-permute-start(bf16[384,1024]{1,0:T(8,128)(2,1)S(1)} %copy-done.5), channel_id=1, source_target_pairs={{0,17},{17,0},{1,16},{16,1},{2,19},{19,2},{3,18},{18,3},{4,21},{21... | collective-permute-start | bytes 2359304 | tf_op jit(solution)/shard_map/ppermute | solution.py:68
  88.5 24.5 %collective-permute-start.16 = (bf16[512,1024]{1,0:T(8,128)(2,1)S(1)}, bf16[512,1024]{1,0:T(8,128)(2,1)S(1)}, u32[]{:S(2)}, u32[]{:S(2)}) collective-permute-start(bf16[512,1024]{1,0:T(8,128)(2,1)S(1)} %copy-done), channel_id=1, source_target_pairs={{0,1},{1,0},{2,3},{3,2},{4,5},{5,4},{6,7},{7,6},{8,9},{9,8},{10,11... | collective-permute-start | bytes 3145736 | tf_op jit(solution)/shard_map/ppermute | solution.py:64
  88.8 25.3 %collective-permute-start.17 = (bf16[512,1024]{1,0:T(8,128)(2,1)S(1)}, bf16[512,1024]{1,0:T(8,128)(2,1)S(1)}, u32[]{:S(2)}, u32[]{:S(2)}) collective-permute-start(bf16[512,1024]{1,0:T(8,128)(2,1)S(1)} %copy-done.1), channel_id=1, source_target_pairs={{0,17},{17,0},{1,16},{16,1},{2,19},{19,2},{3,18},{18,3},{4,21},{21... | collective-permute-start | bytes 3145736 | tf_op jit(solution)/shard_map/ppermute | solution.py:68
  91.0 21.0 %collective-permute-start.15 = (bf16[96,2048]{1,0:T(8,128)(2,1)S(1)}, bf16[96,2048]{1,0:T(8,128)(2,1)S(1)}, u32[]{:S(2)}, u32[]{:S(2)}) collective-permute-start(bf16[96,2048]{1,0:T(8,128)(2,1)S(1)} %get-tuple-element.280), channel_id=1, source_target_pairs={{0,2},{2,4},{4,6},{6,0},{1,3},{3,5},{5,7},{7,1},{8,10},{10,12},{12... | collective-permute-start | bytes 1179656 | tf_op jit(solution)/shard_map/ppermute | solution.py:40
  114.1 23.1 %collective-permute-start.21 = (bf16[512,1024]{1,0:T(8,128)(2,1)S(1)}, bf16[512,1024]{1,0:T(8,128)(2,1)S(1)}, u32[]{:S(2)}, u32[]{:S(2)}) collective-permute-start(bf16[512,1024]{1,0:T(8,128)(2,1)S(1)} %copy-done.2), channel_id=1, source_target_pairs={{0,1},{1,0},{2,3},{3,2},{4,5},{5,4},{6,7},{7,6},{8,9},{9,8},{10,11... | collective-permute-start | bytes 3145736 | tf_op jit(solution)/shard_map/ppermute | solution.py:64
  114.4 24.2 %collective-permute-start.22 = (bf16[512,1024]{1,0:T(8,128)(2,1)S(1)}, bf16[512,1024]{1,0:T(8,128)(2,1)S(1)}, u32[]{:S(2)}, u32[]{:S(2)}) collective-permute-start(bf16[512,1024]{1,0:T(8,128)(2,1)S(1)} %copy-done.3), channel_id=1, source_target_pairs={{0,17},{17,0},{1,16},{16,1},{2,19},{19,2},{3,18},{18,3},{4,21},{21... | collective-permute-start | bytes 3145736 | tf_op jit(solution)/shard_map/ppermute | solution.py:68
  116.3 16.8 %collective-permute-start.19 = (bf16[96,2048]{1,0:T(8,128)(2,1)S(1)}, bf16[96,2048]{1,0:T(8,128)(2,1)S(1)}, u32[]{:S(2)}, u32[]{:S(2)}) collective-permute-start(bf16[96,2048]{1,0:T(8,128)(2,1)S(1)} %add_convert_fusion.3.b0.a0), channel_id=1, source_target_pairs={{0,4},{2,6},{4,0},{6,2},{1,5},{3,7},{5,1},{7,3},{8,12},{10,14},{12... | collective-permute-start | bytes 1179656 | tf_op jit(solution)/shard_map/ppermute | solution.py:40
  117.6 18.3 %collective-permute-start.20 = (bf16[96,2048]{1,0:T(8,128)(2,1)S(1)}, bf16[96,2048]{1,0:T(8,128)(2,1)S(1)}, u32[]{:S(2)}, u32[]{:S(2)}) collective-permute-start(bf16[96,2048]{1,0:T(8,128)(2,1)S(1)} %add_convert_fusion.3.b0.a0), channel_id=1, source_target_pairs={{0,6},{2,0},{4,2},{6,4},{1,7},{3,1},{5,3},{7,5},{8,14},{10,8},{12,... | collective-permute-start | bytes 1179656 | tf_op jit(solution)/shard_map/ppermute | solution.py:40
  142.4 13.5 %collective-permute-start.24 = (bf16[256,1024]{1,0:T(8,128)(2,1)S(1)}, bf16[256,1024]{1,0:T(8,128)(2,1)S(1)}, u32[]{:S(2)}, u32[]{:S(2)}) collective-permute-start(bf16[256,1024]{1,0:T(8,128)(2,1)S(1)} %copy-done.13), channel_id=1, source_target_pairs={{0,1},{1,0},{2,3},{3,2},{4,5},{5,4},{6,7},{7,6},{8,9},{9,8},{10,11... | collective-permute-start | bytes 1572872 | tf_op jit(solution)/shard_map/ppermute | solution.py:64
  142.5 14.7 %collective-permute-start.25 = (bf16[256,1024]{1,0:T(8,128)(2,1)S(1)}, bf16[256,1024]{1,0:T(8,128)(2,1)S(1)}, u32[]{:S(2)}, u32[]{:S(2)}) collective-permute-start(bf16[256,1024]{1,0:T(8,128)(2,1)S(1)} %copy-done.14), channel_id=1, source_target_pairs={{0,17},{17,0},{1,16},{16,1},{2,19},{19,2},{3,18},{18,3},{4,21},{21... | collective-permute-start | bytes 1572872 | tf_op jit(solution)/shard_map/ppermute | solution.py:68
  163.6 21.5 %collective-permute-start.30 = (bf16[768,1024]{1,0:T(8,128)(2,1)S(1)}, bf16[768,1024]{1,0:T(8,128)(2,1)S(1)}, u32[]{:S(2)}, u32[]{:S(2)}) collective-permute-start(bf16[768,1024]{1,0:T(8,128)(2,1)S(1)} %copy-done.29), channel_id=1, source_target_pairs={{0,8},{9,1},{8,9},{1,0},{2,10},{11,3},{10,11},{3,2},{4,12},{13,5},... | collective-permute-start | bytes 4718600 | tf_op jit(solution)/shard_map/ppermute | solution.py:126
  163.9 11.6 %collective-permute-start.28 = (bf16[96,2048]{1,0:T(8,128)(2,1)S(1)}, bf16[96,2048]{1,0:T(8,128)(2,1)S(1)}, u32[]{:S(2)}, u32[]{:S(2)}) collective-permute-start(bf16[96,2048]{1,0:T(8,128)(2,1)S(1)} %get-tuple-element.318), channel_id=1, source_target_pairs={{0,4},{2,6},{4,0},{6,2},{1,5},{3,7},{5,1},{7,3},{8,12},{10,14},{12... | collective-permute-start | bytes 1179656 | tf_op jit(solution)/shard_map/ppermute | solution.py:40
  163.9 21.0 %collective-permute-start.29 = (bf16[96,2048]{1,0:T(8,128)(2,1)S(1)}, bf16[96,2048]{1,0:T(8,128)(2,1)S(1)}, u32[]{:S(2)}, u32[]{:S(2)}) collective-permute-start(bf16[96,2048]{1,0:T(8,128)(2,1)S(1)} %get-tuple-element.319), channel_id=1, source_target_pairs={{0,2},{2,4},{4,6},{6,0},{1,3},{3,5},{5,7},{7,1},{8,10},{10,12},{12... | collective-permute-start | bytes 1179656 | tf_op jit(solution)/shard_map/ppermute | solution.py:40
  186.4 12.1 %collective-permute-start.31 = (bf16[96,2048]{1,0:T(8,128)(2,1)S(1)}, bf16[96,2048]{1,0:T(8,128)(2,1)S(1)}, u32[]{:S(2)}, u32[]{:S(2)}) collective-permute-start(bf16[96,2048]{1,0:T(8,128)(2,1)S(1)} %add_convert_fusion.2.b0), channel_id=1, source_target_pairs={{0,2},{2,4},{4,6},{6,0},{1,3},{3,5},{5,7},{7,1},{8,10},{10,12},{12... | collective-permute-start | bytes 1179656 | tf_op jit(solution)/shard_map/ppermute | solution.py:40
  186.5 17.6 %collective-permute-start.32 = (bf16[96,2048]{1,0:T(8,128)(2,1)S(1)}, bf16[96,2048]{1,0:T(8,128)(2,1)S(1)}, u32[]{:S(2)}, u32[]{:S(2)}) collective-permute-start(bf16[96,2048]{1,0:T(8,128)(2,1)S(1)} %add_convert_fusion.2.b0), channel_id=1, source_target_pairs={{0,4},{2,6},{4,0},{6,2},{1,5},{3,7},{5,1},{7,3},{8,12},{10,14},{12... | collective-permute-start | bytes 1179656 | tf_op jit(solution)/shard_map/ppermute | solution.py:40
  187.8 18.3 %collective-permute-start.33 = (bf16[96,2048]{1,0:T(8,128)(2,1)S(1)}, bf16[96,2048]{1,0:T(8,128)(2,1)S(1)}, u32[]{:S(2)}, u32[]{:S(2)}) collective-permute-start(bf16[96,2048]{1,0:T(8,128)(2,1)S(1)} %add_convert_fusion.2.b0), channel_id=1, source_target_pairs={{0,6},{2,0},{4,2},{6,4},{1,7},{3,1},{5,3},{7,5},{8,14},{10,8},{12,... | collective-permute-start | bytes 1179656 | tf_op jit(solution)/shard_map/ppermute | solution.py:40
  228.4 18.8 %collective-permute-start.37 = (bf16[96,2048]{1,0:T(8,128)(2,1)S(1)}, bf16[96,2048]{1,0:T(8,128)(2,1)S(1)}, u32[]{:S(2)}, u32[]{:S(2)}) collective-permute-start(bf16[96,2048]{1,0:T(8,128)(2,1)S(1)} %get-tuple-element.346), channel_id=1, source_target_pairs={{0,6},{2,0},{4,2},{6,4},{1,7},{3,1},{5,3},{7,5},{8,14},{10,8},{12,... | collective-permute-start | bytes 1179656 | tf_op jit(solution)/shard_map/ppermute | solution.py:40
  230.5 16.7 %collective-permute-start.38 = (bf16[96,2048]{1,0:T(8,128)(2,1)S(1)}, bf16[96,2048]{1,0:T(8,128)(2,1)S(1)}, u32[]{:S(2)}, u32[]{:S(2)}) collective-permute-start(bf16[96,2048]{1,0:T(8,128)(2,1)S(1)} %get-tuple-element.347), channel_id=1, source_target_pairs={{0,4},{2,6},{4,0},{6,2},{1,5},{3,7},{5,1},{7,3},{8,12},{10,14},{12... | collective-permute-start | bytes 1179656 | tf_op jit(solution)/shard_map/ppermute | solution.py:40
  230.5 20.4 %collective-permute-start.39 = (bf16[96,2048]{1,0:T(8,128)(2,1)S(1)}, bf16[96,2048]{1,0:T(8,128)(2,1)S(1)}, u32[]{:S(2)}, u32[]{:S(2)}) collective-permute-start(bf16[96,2048]{1,0:T(8,128)(2,1)S(1)} %get-tuple-element.348), channel_id=1, source_target_pairs={{0,2},{2,4},{4,6},{6,0},{1,3},{3,5},{5,7},{7,1},{8,10},{10,12},{12... | collective-permute-start | bytes 1179656 | tf_op jit(solution)/shard_map/ppermute | solution.py:40
  231.2 19.9 %collective-permute-start.40 = (bf16[384,1024]{1,0:T(8,128)(2,1)}, bf16[384,1024]{1,0:T(8,128)(2,1)S(1)}, u32[]{:S(2)}, u32[]{:S(2)}) collective-permute-start(bf16[384,1024]{1,0:T(8,128)(2,1)} %get-tuple-element.355), channel_id=1, source_target_pairs={{8,1},{1,9},{9,8},{10,3},{3,11},{11,10},{12,5},{5,13},{13,12},{14,... | collective-permute-start | bytes 2359304 | tf_op jit(solution)/shard_map/ppermute | solution.py:750
  235.6 17.1 %collective-permute-start.41 = (bf16[384,1024]{1,0:T(8,128)(2,1)S(1)}, bf16[384,1024]{1,0:T(8,128)(2,1)S(1)}, u32[]{:S(2)}, u32[]{:S(2)}) collective-permute-start(bf16[384,1024]{1,0:T(8,128)(2,1)S(1)} %copy-done.47), channel_id=1, source_target_pairs={{0,1},{8,0},{1,8},{2,3},{10,2},{3,10},{4,5},{12,4},{5,12},{6,7},{1... | collective-permute-start | bytes 2359304 | tf_op jit(solution)/shard_map/ppermute | solution.py:750
  252.7 22.6 %collective-permute-start.46 = (bf16[512,1536]{1,0:T(8,128)(2,1)}, bf16[512,1536]{1,0:T(8,128)(2,1)S(1)}, u32[]{:S(2)}, u32[]{:S(2)}) collective-permute-start(bf16[512,1536]{1,0:T(8,128)(2,1)} %get-tuple-element.366), channel_id=1, source_target_pairs={{0,96},{8,25},{1,97},{9,8},{16,112},{24,9},{17,113},{25,24},{32,0}... | collective-permute-start | bytes 4718600 | tf_op jit(solution)/shard_map/ppermute | solution.py:56
  255.0 20.8 %collective-permute-start.45 = (bf16[512,1536]{1,0:T(8,128)(2,1)S(1)}, bf16[512,1536]{1,0:T(8,128)(2,1)S(1)}, u32[]{:S(2)}, u32[]{:S(2)}) collective-permute-start(bf16[512,1536]{1,0:T(8,128)(2,1)S(1)} %get-tuple-element.364), channel_id=1, source_target_pairs={{0,32},{8,9},{1,33},{9,24},{16,48},{24,25},{17,49},{25,8},{32,64},... | collective-permute-start | bytes 4718600 | tf_op jit(solution)/shard_map/ppermute | solution.py:56
  255.1 12.2 %collective-permute-start.42 = (bf16[96,2048]{1,0:T(8,128)(2,1)S(1)}, bf16[96,2048]{1,0:T(8,128)(2,1)S(1)}, u32[]{:S(2)}, u32[]{:S(2)}) collective-permute-start(bf16[96,2048]{1,0:T(8,128)(2,1)S(1)} %fusion.1.g0), channel_id=1, source_target_pairs={{0,2},{2,4},{4,6},{6,0},{1,3},{3,5},{5,7},{7,1},{8,10},{10,12},{12... | collective-permute-start | bytes 1179656 | tf_op jit(solution)/shard_map/ppermute | solution.py:40
  256.2 16.5 %collective-permute-start.43 = (bf16[96,2048]{1,0:T(8,128)(2,1)S(1)}, bf16[96,2048]{1,0:T(8,128)(2,1)S(1)}, u32[]{:S(2)}, u32[]{:S(2)}) collective-permute-start(bf16[96,2048]{1,0:T(8,128)(2,1)S(1)} %fusion.1.g0), channel_id=1, source_target_pairs={{0,4},{2,6},{4,0},{6,2},{1,5},{3,7},{5,1},{7,3},{8,12},{10,14},{12... | collective-permute-start | bytes 1179656 | tf_op jit(solution)/shard_map/ppermute | solution.py:40
  257.4 17.9 %collective-permute-start.44 = (bf16[96,2048]{1,0:T(8,128)(2,1)S(1)}, bf16[96,2048]{1,0:T(8,128)(2,1)S(1)}, u32[]{:S(2)}, u32[]{:S(2)}) collective-permute-start(bf16[96,2048]{1,0:T(8,128)(2,1)S(1)} %fusion.1.g0), channel_id=1, source_target_pairs={{0,6},{2,0},{4,2},{6,4},{1,7},{3,1},{5,3},{7,5},{8,14},{10,8},{12,... | collective-permute-start | bytes 1179656 | tf_op jit(solution)/shard_map/ppermute | solution.py:40
  279.9 13.5 %collective-permute-start.48 = (bf16[512,768]{1,0:T(8,128)(2,1)S(1)}, bf16[512,768]{1,0:T(8,128)(2,1)S(1)}, u32[]{:S(2)}, u32[]{:S(2)}) collective-permute-start(bf16[512,768]{1,0:T(8,128)(2,1)S(1)} %get-tuple-element.394), channel_id=1, source_target_pairs={{0,32},{8,9},{1,33},{9,24},{16,48},{24,25},{17,49},{25,8},{32,64},... | collective-permute-start | bytes 2359304 | tf_op jit(solution)/shard_map/ppermute | solution.py:56
  296.7 13.2 %collective-permute-start.54 = (bf16[512,768]{1,0:T(8,128)(2,1)S(1)}, bf16[512,768]{1,0:T(8,128)(2,1)S(1)}, u32[]{:S(2)}, u32[]{:S(2)}) collective-permute-start(bf16[512,768]{1,0:T(8,128)(2,1)S(1)} %get-tuple-element.400), channel_id=1, source_target_pairs={{0,32},{8,9},{1,33},{9,24},{16,48},{24,25},{17,49},{25,8},{32,64},... | collective-permute-start | bytes 2359304 | tf_op jit(solution)/shard_map/ppermute | solution.py:56
  317.8 101.3 %all-gather.2.cloned.1.call-start = ((), (), s32[]{:S(2)}) async-start(), calls=%async_computation.2 | async-start | bytes 1966080 | tf_op jit(solution)/shard_map/all_gather | solution.py:934
  320.4 44.4 %collective-permute-start.59 = (bf16[512,1536]{1,0:T(8,128)(2,1)}, bf16[512,1536]{1,0:T(8,128)(2,1)}, u32[]{:S(2)}, u32[]{:S(2)}) collective-permute-start(bf16[512,1536]{1,0:T(8,128)(2,1)} %copy-done.65), channel_id=1, source_target_pairs={{0,64},{8,24},{1,65},{9,25},{16,80},{24,8},{17,81},{25,9},{32,96},... | collective-permute-start | bytes 4718600 | tf_op jit(solution)/shard_map/ppermute | solution.py:56
  323.2 41.6 %collective-permute-start.60 = (bf16[512,1536]{1,0:T(8,128)(2,1)}, bf16[512,1536]{1,0:T(8,128)(2,1)}, u32[]{:S(2)}, u32[]{:S(2)}) collective-permute-start(bf16[512,1536]{1,0:T(8,128)(2,1)} %copy-done.66), channel_id=1, source_target_pairs={{0,64},{8,24},{1,65},{9,25},{16,80},{24,8},{17,81},{25,9},{32,96},... | collective-permute-start | bytes 4718600 | tf_op jit(solution)/shard_map/ppermute | solution.py:56
  346.7 17.3 %collective-permute-start.57 = (bf16[96,1024]{1,0:T(8,128)(2,1)S(1)}, bf16[96,1024]{1,0:T(8,128)(2,1)S(1)}, u32[]{:S(2)}, u32[]{:S(2)}) collective-permute-start(bf16[96,1024]{1,0:T(8,128)(2,1)S(1)} %get-tuple-element.487), channel_id=1, source_target_pairs={{8,1},{1,9},{9,8},{10,3},{3,11},{11,10},{12,5},{5,13},{13,12},{14,... | collective-permute-start | bytes 589832 | tf_op jit(solution)/shard_map/ppermute | solution.py:750
  351.3 12.7 %collective-permute-start.58 = (bf16[96,1024]{1,0:T(8,128)(2,1)S(1)}, bf16[96,1024]{1,0:T(8,128)(2,1)S(1)}, u32[]{:S(2)}, u32[]{:S(2)}) collective-permute-start(bf16[96,1024]{1,0:T(8,128)(2,1)S(1)} %get-tuple-element.488), channel_id=1, source_target_pairs={{0,1},{8,0},{1,8},{2,3},{10,2},{3,10},{4,5},{12,4},{5,12},{6,7},{1... | collective-permute-start | bytes 589832 | tf_op jit(solution)/shard_map/ppermute | solution.py:750
  364.8 35.3 %collective-permute-start.61 = (bf16[576,1024]{1,0:T(8,128)(2,1)}, bf16[576,1024]{1,0:T(8,128)(2,1)}, u32[]{:S(2)}, u32[]{:S(2)}) collective-permute-start(bf16[576,1024]{1,0:T(8,128)(2,1)} %get-tuple-element.436), channel_id=1, source_target_pairs={{0,32},{8,9},{1,33},{9,24},{16,48},{24,25},{17,49},{25,8},{32,64},... | collective-permute-start | bytes 3538952 | tf_op jit(solution)/shard_map/ppermute | solution.py:56
  364.8 36.2 %collective-permute-start.62 = (bf16[576,1024]{1,0:T(8,128)(2,1)}, bf16[576,1024]{1,0:T(8,128)(2,1)}, u32[]{:S(2)}, u32[]{:S(2)}) collective-permute-start(bf16[576,1024]{1,0:T(8,128)(2,1)} %get-tuple-element.437), channel_id=1, source_target_pairs={{0,64},{8,24},{1,65},{9,25},{16,80},{24,8},{17,81},{25,9},{32,96},... | collective-permute-start | bytes 3538952 | tf_op jit(solution)/shard_map/ppermute | solution.py:56
  366.1 37.0 %collective-permute-start.63 = (bf16[576,1024]{1,0:T(8,128)(2,1)}, bf16[576,1024]{1,0:T(8,128)(2,1)}, u32[]{:S(2)}, u32[]{:S(2)}) collective-permute-start(bf16[576,1024]{1,0:T(8,128)(2,1)} %get-tuple-element.438), channel_id=1, source_target_pairs={{0,96},{8,25},{1,97},{9,8},{16,112},{24,9},{17,113},{25,24},{32,0}... | collective-permute-start | bytes 3538952 | tf_op jit(solution)/shard_map/ppermute | solution.py:56
  376.0 20.2 %collective-permute-start.65 = (bf16[256,1536]{1,0:T(8,128)(2,1)S(1)}, bf16[256,1536]{1,0:T(8,128)(2,1)S(1)}, u32[]{:S(2)}, u32[]{:S(2)}) collective-permute-start(bf16[256,1536]{1,0:T(8,128)(2,1)S(1)} %pad_maximum_fusion.4), channel_id=1, source_target_pairs={{0,17},{8,104},{1,0},{9,105},{16,1},{24,120},{17,16},{25,121},{32,... | collective-permute-start | bytes 2359304 | tf_op jit(solution)/shard_map/ppermute | solution.py:56
  378.8 21.3 %collective-permute-start.64 = (bf16[256,1536]{1,0:T(8,128)(2,1)S(1)}, bf16[256,1536]{1,0:T(8,128)(2,1)S(1)}, u32[]{:S(2)}, u32[]{:S(2)}) collective-permute-start(bf16[256,1536]{1,0:T(8,128)(2,1)S(1)} %pad_maximum_fusion.3), channel_id=1, source_target_pairs={{0,1},{8,40},{1,16},{9,41},{16,17},{24,56},{17,0},{25,57},{32,33},... | collective-permute-start | bytes 2359304 | tf_op jit(solution)/shard_map/ppermute | solution.py:56
  403.1 13.3 %collective-permute-start.70 = (bf16[256,1536]{1,0:T(8,128)(2,1)S(1)}, bf16[256,1536]{1,0:T(8,128)(2,1)S(1)}, u32[]{:S(2)}, u32[]{:S(2)}) collective-permute-start(bf16[256,1536]{1,0:T(8,128)(2,1)S(1)} %pad_maximum_fusion.6), channel_id=1, source_target_pairs={{0,16},{8,72},{1,17},{9,73},{16,0},{24,88},{17,1},{25,89},{32,48},... | collective-permute-start | bytes 2359304 | tf_op jit(solution)/shard_map/ppermute | solution.py:56
  410.7 12.2 %collective-permute-start.66 = (bf16[144,1024]{1,0:T(8,128)(2,1)}, bf16[144,1024]{1,0:T(8,128)(2,1)}, u32[]{:S(2)}, u32[]{:S(2)}) collective-permute-start(bf16[144,1024]{1,0:T(8,128)(2,1)} %get-tuple-element.486), channel_id=1, source_target_pairs={{0,1},{8,40},{1,16},{9,41},{16,17},{24,56},{17,0},{25,57},{32,33},... | collective-permute-start | bytes 884744 | tf_op jit(solution)/shard_map/ppermute | solution.py:56
  411.1 11.9 %collective-permute-start.67 = (bf16[144,1024]{1,0:T(8,128)(2,1)}, bf16[144,1024]{1,0:T(8,128)(2,1)}, u32[]{:S(2)}, u32[]{:S(2)}) collective-permute-start(bf16[144,1024]{1,0:T(8,128)(2,1)} %get-tuple-element.485), channel_id=1, source_target_pairs={{0,16},{8,72},{1,17},{9,73},{16,0},{24,88},{17,1},{25,89},{32,48},... | collective-permute-start | bytes 884744 | tf_op jit(solution)/shard_map/ppermute | solution.py:56
  (113 other events, 903.9 us)
Sparse Core Ops, SparseCore 0:
  317.9 26.5 reduce-scatter.1
  368.2 26.3 all-gather.1

commit v2 on v1

--- a/solution.py
+++ b/solution.py
@@ -809,7 +809,7 @@
     came = core_swap(mix(mixed, 1, mixes, LOW))
     mix_parts = settle(mix(mixed, 0, mixes, F32), came)
     mix_parts = lax.optimization_barrier(mix_parts)
-    far = [*far, *fetch(*after(near[2:4], mix_parts))]
+    far = [*far, *fetch(*after(near[2:4], mixed))]
     attn_sum = scatter_z(mix_parts).astype(LOW)
     attn_sum, far = lax.optimization_barrier((attn_sum, far))
     far = [*far, *fetch(*after(near[4:6], attn_sum))]

time: 442 us -> 438 us (level)
    unnamed x174 -> x168, local copies, waits for them, and re-layouts: 24.2 us -> 23.3 us
  transfers between devices with their start and end apart: 74 -> 74, of which waited for: 45 -> 44; matrix products, arithmetic and copies ran while one was open for 7% -> 7% of each run, Pallas kernels for 18% -> 18%
where the time goes in v2:
time: 438 us; the launch traced here: 432 us
  waiting for transfers between devices  165 us (38%)
  Pallas kernels  102 us (23%)
  starting transfers between devices  93.5 us (21%)
  local copies, waits for them, and re-layouts  36.9 us (8%)
  other arithmetic  17.5 us (4%)
  between operations  16.4 us (4%)
    ppermute x24, waiting for transfers between devices, ring_shift(): return lax.ppermute(a, axes, [(i, (i + step) % RING) for i in range(RING)])  89.4 us
    pallas_call x34, Pallas kernels, call(): pl.pallas_call(kernel, in_specs=[pl.BlockSpec(memory_space=pltpu.SMEM if...  86.8 us
    ppermute x17, waiting for transfers between devices, plane_shift(): return lax.ppermute(a, ('y', 'xh', 'core', 'xl'), pairs)  32.1 us
    ppermute x17, starting transfers between devices, plane_shift(): return lax.ppermute(a, ('y', 'xh', 'core', 'xl'), pairs)  24.9 us
    ppermute x24, starting transfers between devices, ring_shift(): return lax.ppermute(a, axes, [(i, (i + step) % RING) for i in range(RING)])  24.6 us
    unnamed x168, local copies, waits for them, and re-layouts  23.3 us
    ppermute x12, starting transfers between devices, core_swap(): return lax.ppermute(a, 'core', [(0, 1), (1, 0)])  14.8 us
    ppermute x4, starting transfers between devices, shuffle(): lax.ppermute(sent[k], ('core', 'xl'), [p for p in perm if p[0] != p[1]])  12.7 us
  transfers between devices with their start and end apart: 74, of which 44 were waited for; matrix products, arithmetic and copies ran while one was open for 7% of the time, Pallas kernels for 18%

profile of v2, /device:TPU:1, one launch (start us, length us, event | category | flops | bytes accessed | tf_op | source)
XLA Modules:
  0.0 431.6 jit_solution(16638246880816806479)
XLA Ops:
  11.5 2.5 shard_map.237
  18.5 5.9 %shard_map.238 = (bf16[384,1024]{1,0:T(8,128)(2,1)}, bf16[384,1024]{1,0:T(8,128)(2,1)}, bf16[512,1024]{1,0:T(8,128)(2,1)}, bf16[512,1024]{1,0:T(8,128)(2,1)}, bf...) custom-call(s32[1]{0:T(128)} %bitcast.table.core_ref.core, ...), custom_call_target="tpu_custom_call" | custom-call | tf_op jit(solution)/shard_map/pallas_call | solution.py:109
  27.3 3.2 multiply_sine_fusion
  34.5 2.4 concatenate.81.table_ref
  39.6 3.2 collective-permute-done.3.refs_2_.refs_3_
  54.4 2.8 shard_map.240
  58.5 4.0 collective-permute-start.9
  66.4 3.5 collective-permute-done.7
  70.1 5.7 %shard_map.241 = (bf16[768,256]{1,0:T(8,128)(2,1)S(1)}, bf16[768,768]{1,0:T(8,128)(2,1)S(1)}, f32[768,8]{1,0:T(8,128)S(1)}) custom-call(f32[768,768]{1,0:T(8,128)S(1)} %get-tuple-element.264.qkv_ref, f32[8,768]{1,0:T(8,128)S(1)} %fusion.3.sums_ref, f32[2,256]{1,0:T(2,128)S(1)} %copy-done.55, f32[768,384]{1,0:T(8,128)S(1)} %copy-done.9, f32[1,768]{1,0:T(1,128)S(1)} %copy-done.54), custom_call_target="tpu_custom_call" | custom-call | tf_op jit(solution)/shard_map/pallas_call | solution.py:355
  75.9 5.3 %collective-permute-done.10.refs_3_.refs_4_.refs_6_.far0 = bf16[384,1024]{1,0:T(8,128)(2,1)S(1)} collective-permute-done((bf16[384,1024]{1,0:T(8,128)(2,1)S(1)}, bf16[384,1024]{1,0:T(8,128)(2,1)S(1)}, u32[]{:S(2)}, u32[]{:S(2)}) %collective-permute-start.10) | collective-permute-done | bytes 786464 | tf_op jit(solution)/shard_map/ppermute | solution.py:64
  90.3 8.5 %collective-permute-done.13 = bf16[96,2048]{1,0:T(8,128)(2,1)S(1)} collective-permute-done((bf16[96,2048]{1,0:T(8,128)(2,1)S(1)}, bf16[96,2048]{1,0:T(8,128)(2,1)S(1)}, u32[]{:S(2)}, u32[]{:S(2)}) %collective-permute-start.13) | collective-permute-done | bytes 393248 | tf_op jit(solution)/shard_map/ppermute | solution.py:40
  100.1 9.8 %collective-permute-done.15 = bf16[96,2048]{1,0:T(8,128)(2,1)S(1)} collective-permute-done((bf16[96,2048]{1,0:T(8,128)(2,1)S(1)}, bf16[96,2048]{1,0:T(8,128)(2,1)S(1)}, u32[]{:S(2)}, u32[]{:S(2)}) %collective-permute-start.15) | collective-permute-done | bytes 393248 | tf_op jit(solution)/shard_map/ppermute | solution.py:40
  116.0 8.4 %collective-permute-done.18.b1.a1 = bf16[96,2048]{1,0:T(8,128)(2,1)S(1)} collective-permute-done((bf16[96,2048]{1,0:T(8,128)(2,1)S(1)}, bf16[96,2048]{1,0:T(8,128)(2,1)S(1)}, u32[]{:S(2)}, u32[]{:S(2)}) %collective-permute-start.18) | collective-permute-done | bytes 393248 | tf_op jit(solution)/shard_map/ppermute | solution.py:40
  124.4 5.8 %collective-permute-done.19.b2.a2 = bf16[96,2048]{1,0:T(8,128)(2,1)S(1)} collective-permute-done((bf16[96,2048]{1,0:T(8,128)(2,1)S(1)}, bf16[96,2048]{1,0:T(8,128)(2,1)S(1)}, u32[]{:S(2)}, u32[]{:S(2)}) %collective-permute-start.19) | collective-permute-done | bytes 393248 | tf_op jit(solution)/shard_map/ppermute | solution.py:40
  130.2 2.5 collective-permute-done.20.b3.a3
  136.8 2.4 collective-permute-start.23
  141.5 3.4 shard_map.246
  145.8 3.4 shard_map.247
  149.3 3.4 collective-permute-done.24.refs_7_.refs_6_
  162.1 8.9 %collective-permute-done.27 = bf16[96,2048]{1,0:T(8,128)(2,1)S(1)} collective-permute-done((bf16[96,2048]{1,0:T(8,128)(2,1)S(1)}, bf16[96,2048]{1,0:T(8,128)(2,1)S(1)}, u32[]{:S(2)}, u32[]{:S(2)}) %collective-permute-start.27) | collective-permute-done | bytes 393248 | tf_op jit(solution)/shard_map/ppermute | solution.py:40
  172.4 9.4 %collective-permute-done.29 = bf16[96,2048]{1,0:T(8,128)(2,1)S(1)} collective-permute-done((bf16[96,2048]{1,0:T(8,128)(2,1)S(1)}, bf16[96,2048]{1,0:T(8,128)(2,1)S(1)}, u32[]{:S(2)}, u32[]{:S(2)}) %collective-permute-start.29) | collective-permute-done | bytes 393248 | tf_op jit(solution)/shard_map/ppermute | solution.py:40
  188.4 7.0 %collective-permute-done.31.b1 = bf16[96,2048]{1,0:T(8,128)(2,1)S(1)} collective-permute-done((bf16[96,2048]{1,0:T(8,128)(2,1)S(1)}, bf16[96,2048]{1,0:T(8,128)(2,1)S(1)}, u32[]{:S(2)}, u32[]{:S(2)}) %collective-permute-start.31) | collective-permute-done | bytes 393248 | tf_op jit(solution)/shard_map/ppermute | solution.py:40
  195.4 5.5 %collective-permute-done.32.b2 = bf16[96,2048]{1,0:T(8,128)(2,1)S(1)} collective-permute-done((bf16[96,2048]{1,0:T(8,128)(2,1)S(1)}, bf16[96,2048]{1,0:T(8,128)(2,1)S(1)}, u32[]{:S(2)}, u32[]{:S(2)}) %collective-permute-start.32) | collective-permute-done | bytes 393248 | tf_op jit(solution)/shard_map/ppermute | solution.py:40
  209.7 2.3 shard_map.254
  215.4 3.4 shard_map.257
  219.4 3.4 shard_map.256.own_ref
  227.4 4.3 %collective-permute-start.40 = (bf16[384,1024]{1,0:T(8,128)(2,1)}, bf16[384,1024]{1,0:T(8,128)(2,1)S(1)}, u32[]{:S(2)}, u32[]{:S(2)}) collective-permute-start(bf16[384,1024]{1,0:T(8,128)(2,1)} %get-tuple-element.355), channel_id=1, source_target_pairs={{8,1},{1,9},{9,8},{10,3},{3,11},{11,10},{12,5},{5,13},{13,12},{14,... | collective-permute-start | bytes 2359304 | tf_op jit(solution)/shard_map/ppermute | solution.py:750
  233.7 8.5 %shard_map.259 = (bf16[512,1536]{1,0:T(8,128)(2,1)S(1)}, bf16[512,1536]{1,0:T(8,128)(2,1)S(1)}, bf16[512,1536]{1,0:T(8,128)(2,1)S(1)}, bf16[512,1536]{1,0:T(8,128)(2,1)}) custom-call(s32[16]{0:T(128)S(1)} %copy-done.58, bf16[384,2048]{1,0:T(8,128)(2,1)S(1)} %get-tuple-element.367.rows_ref.refs_1_, ...), custom_call_target="tpu_custom_call" | custom-call | tf_op jit(solution)/shard_map/pallas_call | solution.py:355
  243.3 3.7 collective-permute-done.39
  254.9 7.3 %shard_map.260 = (bf16[512,1536]{1,0:T(8,128)(2,1)S(1)}, bf16[512,768]{1,0:T(8,128)(2,1)S(1)}, bf16[512,768]{1,0:T(8,128)(2,1)S(1)}, bf16[512,1536]{1,0:T(8,128)...) custom-call(s32[16]{0:T(128)S(1)} %copy-done.58, ...), custom_call_target="tpu_custom_call" | custom-call | tf_op jit(solution)/shard_map/pallas_call | solution.py:355
  263.4 5.3 %collective-permute-done.43.g2 = bf16[96,2048]{1,0:T(8,128)(2,1)S(1)} collective-permute-done((bf16[96,2048]{1,0:T(8,128)(2,1)S(1)}, bf16[96,2048]{1,0:T(8,128)(2,1)S(1)}, u32[]{:S(2)}, u32[]{:S(2)}) %collective-permute-start.43) | collective-permute-done | bytes 393248 | tf_op jit(solution)/shard_map/ppermute | solution.py:40
  273.2 2.9 collective-permute-start.47
  280.4 7.9 %shard_map.262 = (f32[768,512]{1,0:T(8,128)S(1)}, bf16[768,256]{1,0:T(8,128)(2,1)S(1)}, f32[8,768]{1,0:T(8,128)S(1)}, f32[2,256]{1,0:T(2,128)S(1)}) custom-call(f32[768,768]{1,0:T(8,128)S(1)} %get-tuple-element.264.qkv_ref, f32[768,8]{1,0:T(8,128)S(1)} %get-tuple-element.360.scale_ref.rms_ref, f32[2,256]{1,0:T(2,128)S(1)} %copy-done.55, ...), custom_call_target="tpu_custom_call" | custom-call | tf_op jit(solution)/shard_map/pallas_call | solution.py:355
  298.5 4.1 collective-permute-done.51
  302.9 3.2 collective-permute-done.54
  316.6 2.9 collective-permute-start.59
  324.3 6.2 %shard_map.267 = (bf16[576,1024]{1,0:T(8,128)(2,1)S(1)}, bf16[576,1024]{1,0:T(8,128)(2,1)}, bf16[576,1024]{1,0:T(8,128)(2,1)}, bf16[576,1024]{1,0:T(8,128)(2,1)}) custom-call(s32[16]{0:T(128)S(1)} %copy-done.59, bf16[768,2048]{1,0:T(8,128)(2,1)S(1)} %shard_map.239.states_ref.refs_1_, bf16[768,768]{1,0:T(8,128)(2,1)S(1)} %copy-done.7, ...), custom_call_target="tpu_custom_call" | custom-call | tf_op jit(solution)/shard_map/pallas_call | solution.py:355
  331.5 9.2 %reduce-scatter.2.cloned.1.call-done = bf16[96,2048]{1,0:T(8,128)(2,1)} async-done(((bf16[384,2048]{1,0:T(8,128)(2,1)}), bf16[96,2048]{1,0:T(8,128)(2,1)}) %reduce-scatter.2.cloned.1.call-update) | async-done | bytes 393232 | tf_op jit(solution)/shard_map/reduce_scatter | solution.py:918
  342.9 4.5 %collective-permute-start.57 = (bf16[96,1024]{1,0:T(8,128)(2,1)S(1)}, bf16[96,1024]{1,0:T(8,128)(2,1)S(1)}, u32[]{:S(2)}, u32[]{:S(2)}) collective-permute-start(bf16[96,1024]{1,0:T(8,128)(2,1)S(1)} %get-tuple-element.487), channel_id=1, source_target_pairs={{8,1},{1,9},{9,8},{10,3},{3,11},{11,10},{12,5},{5,13},{13,12},{14,... | collective-permute-start | bytes 589832 | tf_op jit(solution)/shard_map/ppermute | solution.py:750
  350.3 3.8 shard_map.268
  354.1 6.1 %collective-permute-done.57 = bf16[96,1024]{1,0:T(8,128)(2,1)S(1)} collective-permute-done((bf16[96,1024]{1,0:T(8,128)(2,1)S(1)}, bf16[96,1024]{1,0:T(8,128)(2,1)S(1)}, u32[]{:S(2)}, u32[]{:S(2)}) %collective-permute-start.57) | collective-permute-done | bytes 196640 | tf_op jit(solution)/shard_map/ppermute | solution.py:750
  372.2 2.7 collective-permute-start.65
  375.1 17.2 %collective-permute-done.65.p3 = bf16[256,1536]{1,0:T(8,128)(2,1)S(1)} collective-permute-done((bf16[256,1536]{1,0:T(8,128)(2,1)S(1)}, bf16[256,1536]{1,0:T(8,128)(2,1)S(1)}, u32[]{:S(2)}, u32[]{:S(2)}) %collective-permute-start.65) | collective-permute-done | bytes 786464 | tf_op jit(solution)/shard_map/ppermute | solution.py:56
  392.3 3.8 collective-permute-done.64.p1
  399.3 3.6 collective-permute-start.70
  402.8 3.0 add_convert_fusion
  409.7 2.8 collective-permute-done.70.p2
  416.7 2.4 shard_map.271
  (390 shorter events, 173.7 us)
Async XLA Ops:
  7.2 333.5 %reduce-scatter.2.cloned.1.call-start = ((), (), s32[]{:S(2)}) async-start(), calls=%async_computation.1 | async-start | bytes 1966080 | tf_op jit(solution)/shard_map/reduce_scatter | solution.py:918
  7.2 17.2 %collective-permute-start = (s32[768]{0:T(1024)}, s32[768]{0:T(1024)S(1)}, u32[]{:S(2)}, u32[]{:S(2)}) collective-permute-start(s32[768]{0:T(1024)} %param.15), channel_id=1, source_target_pairs={{0,8},{8,0},{1,9},{9,1},{2,10},{10,2},{3,11},{11,3},{4,12},{12,4},... | collective-permute-start | bytes 9224 | tf_op jit(solution)/shard_map/ppermute | solution.py:60
  10.1 26.9 %collective-permute-start.1 = (f32[2560]{0:T(1024)}, f32[2560]{0:T(1024)}, u32[]{:S(2)}, u32[]{:S(2)}) collective-permute-start(f32[2560]{0:T(1024)} %pad_maximum_fusion.8), channel_id=1, source_target_pairs={{0,1},{1,0},{2,3},{3,2},{4,5},{5,4},{6,7},{7,6},{8,9},{9,8},{10,11... | collective-permute-start | bytes 30728 | tf_op jit(solution)/shard_map/ppermute | solution.py:64
  11.4 28.3 %collective-permute-start.2 = (bf16[768,1024]{1,0:T(8,128)(2,1)}, bf16[768,1024]{1,0:T(8,128)(2,1)S(1)}, u32[]{:S(2)}, u32[]{:S(2)}) collective-permute-start(bf16[768,1024]{1,0:T(8,128)(2,1)} %a_ref.2), channel_id=1, source_target_pairs={{0,8},{9,1},{8,9},{1,0},{2,10},{11,3},{10,11},{3,2},{4,12},{13,5},... | collective-permute-start | bytes 4718600 | tf_op jit(solution)/shard_map/ppermute | solution.py:126
  14.1 28.7 %collective-permute-start.3 = (bf16[768,768]{1,0:T(8,128)(2,1)}, bf16[768,768]{1,0:T(8,128)(2,1)S(1)}, u32[]{:S(2)}, u32[]{:S(2)}) collective-permute-start(bf16[768,768]{1,0:T(8,128)(2,1)} %get-tuple-element.247.refs_0_.refs_1_), channel_id=1, source_target_pairs={{0,17},{17,0},{1,16},{16,1},{2,19},{19,2},{3,18},{18,3},{4,21},{21... | collective-permute-start | bytes 3538952 | tf_op jit(solution)/shard_map/ppermute | solution.py:68
  16.1 23.5 %collective-permute-start.4 = (bf16[256,768]{1,0:T(8,128)(2,1)}, bf16[256,768]{1,0:T(8,128)(2,1)S(1)}, u32[]{:S(2)}, u32[]{:S(2)}) collective-permute-start(bf16[256,768]{1,0:T(8,128)(2,1)} %get-tuple-element.248.refs_1_.refs_2_), channel_id=1, source_target_pairs={{0,1},{1,0},{2,3},{3,2},{4,5},{5,4},{6,7},{7,6},{8,9},{9,8},{10,11... | collective-permute-start | bytes 1179656 | tf_op jit(solution)/shard_map/ppermute | solution.py:64
  62.5 18.7 %collective-permute-start.10 = (bf16[384,1024]{1,0:T(8,128)(2,1)S(1)}, bf16[384,1024]{1,0:T(8,128)(2,1)S(1)}, u32[]{:S(2)}, u32[]{:S(2)}) collective-permute-start(bf16[384,1024]{1,0:T(8,128)(2,1)S(1)} %copy-done.4), channel_id=1, source_target_pairs={{0,1},{1,0},{2,3},{3,2},{4,5},{5,4},{6,7},{7,6},{8,9},{9,8},{10,11... | collective-permute-start | bytes 2359304 | tf_op jit(solution)/shard_map/ppermute | solution.py:64
  62.9 19.3 %collective-permute-start.11 = (bf16[384,1024]{1,0:T(8,128)(2,1)S(1)}, bf16[384,1024]{1,0:T(8,128)(2,1)S(1)}, u32[]{:S(2)}, u32[]{:S(2)}) collective-permute-start(bf16[384,1024]{1,0:T(8,128)(2,1)S(1)} %copy-done.5), channel_id=1, source_target_pairs={{0,17},{17,0},{1,16},{16,1},{2,19},{19,2},{3,18},{18,3},{4,21},{21... | collective-permute-start | bytes 2359304 | tf_op jit(solution)/shard_map/ppermute | solution.py:68
  85.1 25.0 %collective-permute-start.16 = (bf16[512,1024]{1,0:T(8,128)(2,1)S(1)}, bf16[512,1024]{1,0:T(8,128)(2,1)S(1)}, u32[]{:S(2)}, u32[]{:S(2)}) collective-permute-start(bf16[512,1024]{1,0:T(8,128)(2,1)S(1)} %copy-done), channel_id=1, source_target_pairs={{0,1},{1,0},{2,3},{3,2},{4,5},{5,4},{6,7},{7,6},{8,9},{9,8},{10,11... | collective-permute-start | bytes 3145736 | tf_op jit(solution)/shard_map/ppermute | solution.py:64
  85.4 25.5 %collective-permute-start.17 = (bf16[512,1024]{1,0:T(8,128)(2,1)S(1)}, bf16[512,1024]{1,0:T(8,128)(2,1)S(1)}, u32[]{:S(2)}, u32[]{:S(2)}) collective-permute-start(bf16[512,1024]{1,0:T(8,128)(2,1)S(1)} %copy-done.1), channel_id=1, source_target_pairs={{0,17},{17,0},{1,16},{16,1},{2,19},{19,2},{3,18},{18,3},{4,21},{21... | collective-permute-start | bytes 3145736 | tf_op jit(solution)/shard_map/ppermute | solution.py:68
  89.0 21.0 %collective-permute-start.15 = (bf16[96,2048]{1,0:T(8,128)(2,1)S(1)}, bf16[96,2048]{1,0:T(8,128)(2,1)S(1)}, u32[]{:S(2)}, u32[]{:S(2)}) collective-permute-start(bf16[96,2048]{1,0:T(8,128)(2,1)S(1)} %get-tuple-element.280), channel_id=1, source_target_pairs={{0,2},{2,4},{4,6},{6,0},{1,3},{3,5},{5,7},{7,1},{8,10},{10,12},{12... | collective-permute-start | bytes 1179656 | tf_op jit(solution)/shard_map/ppermute | solution.py:40
  110.9 23.4 %collective-permute-start.21 = (bf16[512,1024]{1,0:T(8,128)(2,1)S(1)}, bf16[512,1024]{1,0:T(8,128)(2,1)S(1)}, u32[]{:S(2)}, u32[]{:S(2)}) collective-permute-start(bf16[512,1024]{1,0:T(8,128)(2,1)S(1)} %copy-done.2), channel_id=1, source_target_pairs={{0,1},{1,0},{2,3},{3,2},{4,5},{5,4},{6,7},{7,6},{8,9},{9,8},{10,11... | collective-permute-start | bytes 3145736 | tf_op jit(solution)/shard_map/ppermute | solution.py:64
  111.2 24.4 %collective-permute-start.22 = (bf16[512,1024]{1,0:T(8,128)(2,1)S(1)}, bf16[512,1024]{1,0:T(8,128)(2,1)S(1)}, u32[]{:S(2)}, u32[]{:S(2)}) collective-permute-start(bf16[512,1024]{1,0:T(8,128)(2,1)S(1)} %copy-done.3), channel_id=1, source_target_pairs={{0,17},{17,0},{1,16},{16,1},{2,19},{19,2},{3,18},{18,3},{4,21},{21... | collective-permute-start | bytes 3145736 | tf_op jit(solution)/shard_map/ppermute | solution.py:68
  113.1 17.1 %collective-permute-start.19 = (bf16[96,2048]{1,0:T(8,128)(2,1)S(1)}, bf16[96,2048]{1,0:T(8,128)(2,1)S(1)}, u32[]{:S(2)}, u32[]{:S(2)}) collective-permute-start(bf16[96,2048]{1,0:T(8,128)(2,1)S(1)} %add_convert_fusion.3.b0.a0), channel_id=1, source_target_pairs={{0,4},{2,6},{4,0},{6,2},{1,5},{3,7},{5,1},{7,3},{8,12},{10,14},{12... | collective-permute-start | bytes 1179656 | tf_op jit(solution)/shard_map/ppermute | solution.py:40
  114.4 18.3 %collective-permute-start.20 = (bf16[96,2048]{1,0:T(8,128)(2,1)S(1)}, bf16[96,2048]{1,0:T(8,128)(2,1)S(1)}, u32[]{:S(2)}, u32[]{:S(2)}) collective-permute-start(bf16[96,2048]{1,0:T(8,128)(2,1)S(1)} %add_convert_fusion.3.b0.a0), channel_id=1, source_target_pairs={{0,6},{2,0},{4,2},{6,4},{1,7},{3,1},{5,3},{7,5},{8,14},{10,8},{12,... | collective-permute-start | bytes 1179656 | tf_op jit(solution)/shard_map/ppermute | solution.py:40
  139.2 13.5 %collective-permute-start.24 = (bf16[256,1024]{1,0:T(8,128)(2,1)S(1)}, bf16[256,1024]{1,0:T(8,128)(2,1)S(1)}, u32[]{:S(2)}, u32[]{:S(2)}) collective-permute-start(bf16[256,1024]{1,0:T(8,128)(2,1)S(1)} %copy-done.13), channel_id=1, source_target_pairs={{0,1},{1,0},{2,3},{3,2},{4,5},{5,4},{6,7},{7,6},{8,9},{9,8},{10,11... | collective-permute-start | bytes 1572872 | tf_op jit(solution)/shard_map/ppermute | solution.py:64
  139.3 14.6 %collective-permute-start.25 = (bf16[256,1024]{1,0:T(8,128)(2,1)S(1)}, bf16[256,1024]{1,0:T(8,128)(2,1)S(1)}, u32[]{:S(2)}, u32[]{:S(2)}) collective-permute-start(bf16[256,1024]{1,0:T(8,128)(2,1)S(1)} %copy-done.14), channel_id=1, source_target_pairs={{0,17},{17,0},{1,16},{16,1},{2,19},{19,2},{3,18},{18,3},{4,21},{21... | collective-permute-start | bytes 1572872 | tf_op jit(solution)/shard_map/ppermute | solution.py:68
  160.4 21.6 %collective-permute-start.30 = (bf16[768,1024]{1,0:T(8,128)(2,1)S(1)}, bf16[768,1024]{1,0:T(8,128)(2,1)S(1)}, u32[]{:S(2)}, u32[]{:S(2)}) collective-permute-start(bf16[768,1024]{1,0:T(8,128)(2,1)S(1)} %copy-done.29), channel_id=1, source_target_pairs={{0,8},{9,1},{8,9},{1,0},{2,10},{11,3},{10,11},{3,2},{4,12},{13,5},... | collective-permute-start | bytes 4718600 | tf_op jit(solution)/shard_map/ppermute | solution.py:126
  160.8 11.6 %collective-permute-start.28 = (bf16[96,2048]{1,0:T(8,128)(2,1)S(1)}, bf16[96,2048]{1,0:T(8,128)(2,1)S(1)}, u32[]{:S(2)}, u32[]{:S(2)}) collective-permute-start(bf16[96,2048]{1,0:T(8,128)(2,1)S(1)} %get-tuple-element.318), channel_id=1, source_target_pairs={{0,4},{2,6},{4,0},{6,2},{1,5},{3,7},{5,1},{7,3},{8,12},{10,14},{12... | collective-permute-start | bytes 1179656 | tf_op jit(solution)/shard_map/ppermute | solution.py:40
  160.8 21.0 %collective-permute-start.29 = (bf16[96,2048]{1,0:T(8,128)(2,1)S(1)}, bf16[96,2048]{1,0:T(8,128)(2,1)S(1)}, u32[]{:S(2)}, u32[]{:S(2)}) collective-permute-start(bf16[96,2048]{1,0:T(8,128)(2,1)S(1)} %get-tuple-element.319), channel_id=1, source_target_pairs={{0,2},{2,4},{4,6},{6,0},{1,3},{3,5},{5,7},{7,1},{8,10},{10,12},{12... | collective-permute-start | bytes 1179656 | tf_op jit(solution)/shard_map/ppermute | solution.py:40
  183.3 12.1 %collective-permute-start.31 = (bf16[96,2048]{1,0:T(8,128)(2,1)S(1)}, bf16[96,2048]{1,0:T(8,128)(2,1)S(1)}, u32[]{:S(2)}, u32[]{:S(2)}) collective-permute-start(bf16[96,2048]{1,0:T(8,128)(2,1)S(1)} %add_convert_fusion.2.b0), channel_id=1, source_target_pairs={{0,2},{2,4},{4,6},{6,0},{1,3},{3,5},{5,7},{7,1},{8,10},{10,12},{12... | collective-permute-start | bytes 1179656 | tf_op jit(solution)/shard_map/ppermute | solution.py:40
  183.4 17.6 %collective-permute-start.32 = (bf16[96,2048]{1,0:T(8,128)(2,1)S(1)}, bf16[96,2048]{1,0:T(8,128)(2,1)S(1)}, u32[]{:S(2)}, u32[]{:S(2)}) collective-permute-start(bf16[96,2048]{1,0:T(8,128)(2,1)S(1)} %add_convert_fusion.2.b0), channel_id=1, source_target_pairs={{0,4},{2,6},{4,0},{6,2},{1,5},{3,7},{5,1},{7,3},{8,12},{10,14},{12... | collective-permute-start | bytes 1179656 | tf_op jit(solution)/shard_map/ppermute | solution.py:40
  184.6 18.3 %collective-permute-start.33 = (bf16[96,2048]{1,0:T(8,128)(2,1)S(1)}, bf16[96,2048]{1,0:T(8,128)(2,1)S(1)}, u32[]{:S(2)}, u32[]{:S(2)}) collective-permute-start(bf16[96,2048]{1,0:T(8,128)(2,1)S(1)} %add_convert_fusion.2.b0), channel_id=1, source_target_pairs={{0,6},{2,0},{4,2},{6,4},{1,7},{3,1},{5,3},{7,5},{8,14},{10,8},{12,... | collective-permute-start | bytes 1179656 | tf_op jit(solution)/shard_map/ppermute | solution.py:40
  224.6 18.7 %collective-permute-start.37 = (bf16[96,2048]{1,0:T(8,128)(2,1)S(1)}, bf16[96,2048]{1,0:T(8,128)(2,1)S(1)}, u32[]{:S(2)}, u32[]{:S(2)}) collective-permute-start(bf16[96,2048]{1,0:T(8,128)(2,1)S(1)} %get-tuple-element.346), channel_id=1, source_target_pairs={{0,6},{2,0},{4,2},{6,4},{1,7},{3,1},{5,3},{7,5},{8,14},{10,8},{12,... | collective-permute-start | bytes 1179656 | tf_op jit(solution)/shard_map/ppermute | solution.py:40
  226.7 16.6 %collective-permute-start.38 = (bf16[96,2048]{1,0:T(8,128)(2,1)S(1)}, bf16[96,2048]{1,0:T(8,128)(2,1)S(1)}, u32[]{:S(2)}, u32[]{:S(2)}) collective-permute-start(bf16[96,2048]{1,0:T(8,128)(2,1)S(1)} %get-tuple-element.347), channel_id=1, source_target_pairs={{0,4},{2,6},{4,0},{6,2},{1,5},{3,7},{5,1},{7,3},{8,12},{10,14},{12... | collective-permute-start | bytes 1179656 | tf_op jit(solution)/shard_map/ppermute | solution.py:40
  226.7 20.4 %collective-permute-start.39 = (bf16[96,2048]{1,0:T(8,128)(2,1)S(1)}, bf16[96,2048]{1,0:T(8,128)(2,1)S(1)}, u32[]{:S(2)}, u32[]{:S(2)}) collective-permute-start(bf16[96,2048]{1,0:T(8,128)(2,1)S(1)} %get-tuple-element.348), channel_id=1, source_target_pairs={{0,2},{2,4},{4,6},{6,0},{1,3},{3,5},{5,7},{7,1},{8,10},{10,12},{12... | collective-permute-start | bytes 1179656 | tf_op jit(solution)/shard_map/ppermute | solution.py:40
  227.4 19.9 %collective-permute-start.40 = (bf16[384,1024]{1,0:T(8,128)(2,1)}, bf16[384,1024]{1,0:T(8,128)(2,1)S(1)}, u32[]{:S(2)}, u32[]{:S(2)}) collective-permute-start(bf16[384,1024]{1,0:T(8,128)(2,1)} %get-tuple-element.355), channel_id=1, source_target_pairs={{8,1},{1,9},{9,8},{10,3},{3,11},{11,10},{12,5},{5,13},{13,12},{14,... | collective-permute-start | bytes 2359304 | tf_op jit(solution)/shard_map/ppermute | solution.py:750
  231.7 17.1 %collective-permute-start.41 = (bf16[384,1024]{1,0:T(8,128)(2,1)}, bf16[384,1024]{1,0:T(8,128)(2,1)S(1)}, u32[]{:S(2)}, u32[]{:S(2)}) collective-permute-start(bf16[384,1024]{1,0:T(8,128)(2,1)} %get-tuple-element.356), channel_id=1, source_target_pairs={{0,1},{8,0},{1,8},{2,3},{10,2},{3,10},{4,5},{12,4},{5,12},{6,7},{1... | collective-permute-start | bytes 2359304 | tf_op jit(solution)/shard_map/ppermute | solution.py:750
  248.8 22.2 %collective-permute-start.46 = (bf16[512,1536]{1,0:T(8,128)(2,1)}, bf16[512,1536]{1,0:T(8,128)(2,1)S(1)}, u32[]{:S(2)}, u32[]{:S(2)}) collective-permute-start(bf16[512,1536]{1,0:T(8,128)(2,1)} %get-tuple-element.366), channel_id=1, source_target_pairs={{0,96},{8,25},{1,97},{9,8},{16,112},{24,9},{17,113},{25,24},{32,0}... | collective-permute-start | bytes 4718600 | tf_op jit(solution)/shard_map/ppermute | solution.py:56
  250.8 20.8 %collective-permute-start.45 = (bf16[512,1536]{1,0:T(8,128)(2,1)S(1)}, bf16[512,1536]{1,0:T(8,128)(2,1)S(1)}, u32[]{:S(2)}, u32[]{:S(2)}) collective-permute-start(bf16[512,1536]{1,0:T(8,128)(2,1)S(1)} %get-tuple-element.364), channel_id=1, source_target_pairs={{0,32},{8,9},{1,33},{9,24},{16,48},{24,25},{17,49},{25,8},{32,64},... | collective-permute-start | bytes 4718600 | tf_op jit(solution)/shard_map/ppermute | solution.py:56
  250.8 12.6 %collective-permute-start.42 = (bf16[96,2048]{1,0:T(8,128)(2,1)S(1)}, bf16[96,2048]{1,0:T(8,128)(2,1)S(1)}, u32[]{:S(2)}, u32[]{:S(2)}) collective-permute-start(bf16[96,2048]{1,0:T(8,128)(2,1)S(1)} %fusion.1.g0), channel_id=1, source_target_pairs={{0,2},{2,4},{4,6},{6,0},{1,3},{3,5},{5,7},{7,1},{8,10},{10,12},{12... | collective-permute-start | bytes 1179656 | tf_op jit(solution)/shard_map/ppermute | solution.py:40
  252.4 16.4 %collective-permute-start.43 = (bf16[96,2048]{1,0:T(8,128)(2,1)S(1)}, bf16[96,2048]{1,0:T(8,128)(2,1)S(1)}, u32[]{:S(2)}, u32[]{:S(2)}) collective-permute-start(bf16[96,2048]{1,0:T(8,128)(2,1)S(1)} %fusion.1.g0), channel_id=1, source_target_pairs={{0,4},{2,6},{4,0},{6,2},{1,5},{3,7},{5,1},{7,3},{8,12},{10,14},{12... | collective-permute-start | bytes 1179656 | tf_op jit(solution)/shard_map/ppermute | solution.py:40
  253.6 17.4 %collective-permute-start.44 = (bf16[96,2048]{1,0:T(8,128)(2,1)S(1)}, bf16[96,2048]{1,0:T(8,128)(2,1)S(1)}, u32[]{:S(2)}, u32[]{:S(2)}) collective-permute-start(bf16[96,2048]{1,0:T(8,128)(2,1)S(1)} %fusion.1.g0), channel_id=1, source_target_pairs={{0,6},{2,0},{4,2},{6,4},{1,7},{3,1},{5,3},{7,5},{8,14},{10,8},{12,... | collective-permute-start | bytes 1179656 | tf_op jit(solution)/shard_map/ppermute | solution.py:40
  276.2 13.4 %collective-permute-start.48 = (bf16[512,768]{1,0:T(8,128)(2,1)S(1)}, bf16[512,768]{1,0:T(8,128)(2,1)S(1)}, u32[]{:S(2)}, u32[]{:S(2)}) collective-permute-start(bf16[512,768]{1,0:T(8,128)(2,1)S(1)} %get-tuple-element.394), channel_id=1, source_target_pairs={{0,32},{8,9},{1,33},{9,24},{16,48},{24,25},{17,49},{25,8},{32,64},... | collective-permute-start | bytes 2359304 | tf_op jit(solution)/shard_map/ppermute | solution.py:56
  292.9 13.2 %collective-permute-start.54 = (bf16[512,768]{1,0:T(8,128)(2,1)S(1)}, bf16[512,768]{1,0:T(8,128)(2,1)S(1)}, u32[]{:S(2)}, u32[]{:S(2)}) collective-permute-start(bf16[512,768]{1,0:T(8,128)(2,1)S(1)} %get-tuple-element.400), channel_id=1, source_target_pairs={{0,32},{8,9},{1,33},{9,24},{16,48},{24,25},{17,49},{25,8},{32,64},... | collective-permute-start | bytes 2359304 | tf_op jit(solution)/shard_map/ppermute | solution.py:56
  314.0 101.3 %all-gather.2.cloned.1.call-start = ((), (), s32[]{:S(2)}) async-start(), calls=%async_computation.2 | async-start | bytes 1966080 | tf_op jit(solution)/shard_map/all_gather | solution.py:934
  316.6 44.4 %collective-permute-start.59 = (bf16[512,1536]{1,0:T(8,128)(2,1)}, bf16[512,1536]{1,0:T(8,128)(2,1)}, u32[]{:S(2)}, u32[]{:S(2)}) collective-permute-start(bf16[512,1536]{1,0:T(8,128)(2,1)} %copy-done.62), channel_id=1, source_target_pairs={{0,64},{8,24},{1,65},{9,25},{16,80},{24,8},{17,81},{25,9},{32,96},... | collective-permute-start | bytes 4718600 | tf_op jit(solution)/shard_map/ppermute | solution.py:56
  319.5 41.5 %collective-permute-start.60 = (bf16[512,1536]{1,0:T(8,128)(2,1)}, bf16[512,1536]{1,0:T(8,128)(2,1)}, u32[]{:S(2)}, u32[]{:S(2)}) collective-permute-start(bf16[512,1536]{1,0:T(8,128)(2,1)} %copy-done.63), channel_id=1, source_target_pairs={{0,64},{8,24},{1,65},{9,25},{16,80},{24,8},{17,81},{25,9},{32,96},... | collective-permute-start | bytes 4718600 | tf_op jit(solution)/shard_map/ppermute | solution.py:56
  342.9 17.3 %collective-permute-start.57 = (bf16[96,1024]{1,0:T(8,128)(2,1)S(1)}, bf16[96,1024]{1,0:T(8,128)(2,1)S(1)}, u32[]{:S(2)}, u32[]{:S(2)}) collective-permute-start(bf16[96,1024]{1,0:T(8,128)(2,1)S(1)} %get-tuple-element.487), channel_id=1, source_target_pairs={{8,1},{1,9},{9,8},{10,3},{3,11},{11,10},{12,5},{5,13},{13,12},{14,... | collective-permute-start | bytes 589832 | tf_op jit(solution)/shard_map/ppermute | solution.py:750
  347.4 12.8 %collective-permute-start.58 = (bf16[96,1024]{1,0:T(8,128)(2,1)S(1)}, bf16[96,1024]{1,0:T(8,128)(2,1)S(1)}, u32[]{:S(2)}, u32[]{:S(2)}) collective-permute-start(bf16[96,1024]{1,0:T(8,128)(2,1)S(1)} %get-tuple-element.488), channel_id=1, source_target_pairs={{0,1},{8,0},{1,8},{2,3},{10,2},{3,10},{4,5},{12,4},{5,12},{6,7},{1... | collective-permute-start | bytes 589832 | tf_op jit(solution)/shard_map/ppermute | solution.py:750
  361.0 35.2 %collective-permute-start.61 = (bf16[576,1024]{1,0:T(8,128)(2,1)}, bf16[576,1024]{1,0:T(8,128)(2,1)}, u32[]{:S(2)}, u32[]{:S(2)}) collective-permute-start(bf16[576,1024]{1,0:T(8,128)(2,1)} %get-tuple-element.436), channel_id=1, source_target_pairs={{0,32},{8,9},{1,33},{9,24},{16,48},{24,25},{17,49},{25,8},{32,64},... | collective-permute-start | bytes 3538952 | tf_op jit(solution)/shard_map/ppermute | solution.py:56
  361.0 36.2 %collective-permute-start.62 = (bf16[576,1024]{1,0:T(8,128)(2,1)}, bf16[576,1024]{1,0:T(8,128)(2,1)}, u32[]{:S(2)}, u32[]{:S(2)}) collective-permute-start(bf16[576,1024]{1,0:T(8,128)(2,1)} %get-tuple-element.437), channel_id=1, source_target_pairs={{0,64},{8,24},{1,65},{9,25},{16,80},{24,8},{17,81},{25,9},{32,96},... | collective-permute-start | bytes 3538952 | tf_op jit(solution)/shard_map/ppermute | solution.py:56
  362.2 37.0 %collective-permute-start.63 = (bf16[576,1024]{1,0:T(8,128)(2,1)}, bf16[576,1024]{1,0:T(8,128)(2,1)}, u32[]{:S(2)}, u32[]{:S(2)}) collective-permute-start(bf16[576,1024]{1,0:T(8,128)(2,1)} %get-tuple-element.438), channel_id=1, source_target_pairs={{0,96},{8,25},{1,97},{9,8},{16,112},{24,9},{17,113},{25,24},{32,0}... | collective-permute-start | bytes 3538952 | tf_op jit(solution)/shard_map/ppermute | solution.py:56
  372.2 20.1 %collective-permute-start.65 = (bf16[256,1536]{1,0:T(8,128)(2,1)S(1)}, bf16[256,1536]{1,0:T(8,128)(2,1)S(1)}, u32[]{:S(2)}, u32[]{:S(2)}) collective-permute-start(bf16[256,1536]{1,0:T(8,128)(2,1)S(1)} %pad_maximum_fusion.4), channel_id=1, source_target_pairs={{0,17},{8,104},{1,0},{9,105},{16,1},{24,120},{17,16},{25,121},{32,... | collective-permute-start | bytes 2359304 | tf_op jit(solution)/shard_map/ppermute | solution.py:56
  375.0 21.2 %collective-permute-start.64 = (bf16[256,1536]{1,0:T(8,128)(2,1)S(1)}, bf16[256,1536]{1,0:T(8,128)(2,1)S(1)}, u32[]{:S(2)}, u32[]{:S(2)}) collective-permute-start(bf16[256,1536]{1,0:T(8,128)(2,1)S(1)} %pad_maximum_fusion.3), channel_id=1, source_target_pairs={{0,1},{8,40},{1,16},{9,41},{16,17},{24,56},{17,0},{25,57},{32,33},... | collective-permute-start | bytes 2359304 | tf_op jit(solution)/shard_map/ppermute | solution.py:56
  399.3 13.2 %collective-permute-start.70 = (bf16[256,1536]{1,0:T(8,128)(2,1)S(1)}, bf16[256,1536]{1,0:T(8,128)(2,1)S(1)}, u32[]{:S(2)}, u32[]{:S(2)}) collective-permute-start(bf16[256,1536]{1,0:T(8,128)(2,1)S(1)} %pad_maximum_fusion.6), channel_id=1, source_target_pairs={{0,16},{8,72},{1,17},{9,73},{16,0},{24,88},{17,1},{25,89},{32,48},... | collective-permute-start | bytes 2359304 | tf_op jit(solution)/shard_map/ppermute | solution.py:56
  406.9 12.2 %collective-permute-start.66 = (bf16[144,1024]{1,0:T(8,128)(2,1)}, bf16[144,1024]{1,0:T(8,128)(2,1)}, u32[]{:S(2)}, u32[]{:S(2)}) collective-permute-start(bf16[144,1024]{1,0:T(8,128)(2,1)} %get-tuple-element.486), channel_id=1, source_target_pairs={{0,1},{8,40},{1,16},{9,41},{16,17},{24,56},{17,0},{25,57},{32,33},... | collective-permute-start | bytes 884744 | tf_op jit(solution)/shard_map/ppermute | solution.py:56
  407.2 11.9 %collective-permute-start.67 = (bf16[144,1024]{1,0:T(8,128)(2,1)}, bf16[144,1024]{1,0:T(8,128)(2,1)}, u32[]{:S(2)}, u32[]{:S(2)}) collective-permute-start(bf16[144,1024]{1,0:T(8,128)(2,1)} %get-tuple-element.485), channel_id=1, source_target_pairs={{0,16},{8,72},{1,17},{9,73},{16,0},{24,88},{17,1},{25,89},{32,48},... | collective-permute-start | bytes 884744 | tf_op jit(solution)/shard_map/ppermute | solution.py:56
  (110 other events, 883.7 us)
Sparse Core Ops, SparseCore 0:
  314.1 26.5 reduce-scatter.1
  364.4 26.3 all-gather.1

commit v3 on v2

--- a/solution.py
+++ b/solution.py
@@ -811,8 +811,9 @@
     mix_parts = lax.optimization_barrier(mix_parts)
     far = [*far, *fetch(*after(near[2:4], mixed))]
     attn_sum = scatter_z(mix_parts).astype(LOW)
+    next_pieces = after(near[4:6], far)
     attn_sum, far = lax.optimization_barrier((attn_sum, far))
-    far = [*far, *fetch(*after(near[4:6], attn_sum))]
+    far = [*far, *fetch(*next_pieces)]
     attn_blocks = gather_z(attn_sum)
     own_states = after(states, attn_sum)[:OWN]
     attn_blocks, far, own_states = lax.optimization_barrier((attn_blocks, far, own_states))

time: 438 us -> 438 us (level)
    ppermute x24, waiting for transfers between devices: 89.4 us -> 53.1 us  [ring_shift(): return lax.ppermute(a, axes, [(i, (i + step) % RING) for i in range(RING)])]
    ppermute x6, waiting for transfers between devices: 10.4 us -> 46.3 us  [pair_swap(): return lax.ppermute(a, 'xl', [(0, 1), (1, 0)])]
  transfers between devices with their start and end apart: 74 -> 74, of which waited for: 44 -> 39; matrix products, arithmetic and copies ran while one was open for 7% -> 7% of each run, Pallas kernels for 18% -> 18%
where the time goes in v3:
time: 438 us; the launch traced here: 432 us
  waiting for transfers between devices  165 us (38%)
  Pallas kernels  102 us (23%)
  starting transfers between devices  93.5 us (21%)
  local copies, waits for them, and re-layouts  36.9 us (8%)
  other arithmetic  17.5 us (4%)
  between operations  16.4 us (4%)
    pallas_call x34, Pallas kernels, call(): pl.pallas_call(kernel, in_specs=[pl.BlockSpec(memory_space=pltpu.SMEM if...  86.8 us
    ppermute x24, waiting for transfers between devices, ring_shift(): return lax.ppermute(a, axes, [(i, (i + step) % RING) for i in range(RING)])  53.1 us
    ppermute x6, waiting for transfers between devices, pair_swap(): return lax.ppermute(a, 'xl', [(0, 1), (1, 0)])  46.3 us
    ppermute x17, waiting for transfers between devices, plane_shift(): return lax.ppermute(a, ('y', 'xh', 'core', 'xl'), pairs)  32.1 us
    ppermute x17, starting transfers between devices, plane_shift(): return lax.ppermute(a, ('y', 'xh', 'core', 'xl'), pairs)  24.9 us
    ppermute x24, starting transfers between devices, ring_shift(): return lax.ppermute(a, axes, [(i, (i + step) % RING) for i in range(RING)])  24.7 us
    unnamed x168, local copies, waits for them, and re-layouts  23.3 us
    ppermute x12, starting transfers between devices, core_swap(): return lax.ppermute(a, 'core', [(0, 1), (1, 0)])  14.8 us
  transfers between devices with their start and end apart: 74, of which 39 were waited for; matrix products, arithmetic and copies ran while one was open for 7% of the time, Pallas kernels for 18%

profile of v3, /device:TPU:1, one launch (start us, length us, event | category | flops | bytes accessed | tf_op | source)
XLA Modules:
  0.0 431.6 jit_solution(2314600590842217248)
XLA Ops:
  11.5 2.5 shard_map.237
  18.5 5.9 %shard_map.238 = (bf16[384,1024]{1,0:T(8,128)(2,1)}, bf16[384,1024]{1,0:T(8,128)(2,1)}, bf16[512,1024]{1,0:T(8,128)(2,1)}, bf16[512,1024]{1,0:T(8,128)(2,1)}, bf...) custom-call(s32[1]{0:T(128)} %bitcast.table.core_ref.core, ...), custom_call_target="tpu_custom_call" | custom-call | tf_op jit(solution)/shard_map/pallas_call | solution.py:109
  27.3 3.2 multiply_sine_fusion
  34.5 2.4 concatenate.81.table_ref
  39.6 3.2 collective-permute-done.3.refs_2_.refs_3_
  47.0 2.3 collective-permute-done.5.second_ref
  54.4 2.8 shard_map.240
  58.5 4.0 collective-permute-start.9
  66.4 3.5 collective-permute-done.7
  70.1 5.7 %shard_map.241 = (bf16[768,256]{1,0:T(8,128)(2,1)S(1)}, bf16[768,768]{1,0:T(8,128)(2,1)S(1)}, f32[768,8]{1,0:T(8,128)S(1)}) custom-call(f32[768,768]{1,0:T(8,128)S(1)} %get-tuple-element.264.qkv_ref, f32[8,768]{1,0:T(8,128)S(1)} %fusion.3.sums_ref, f32[2,256]{1,0:T(2,128)S(1)} %copy-done.55, f32[768,384]{1,0:T(8,128)S(1)} %copy-done.9, f32[1,768]{1,0:T(1,128)S(1)} %copy-done.54), custom_call_target="tpu_custom_call" | custom-call | tf_op jit(solution)/shard_map/pallas_call | solution.py:355
  75.9 5.3 %collective-permute-done.10.refs_3_.refs_4_.refs_6_.far0 = bf16[384,1024]{1,0:T(8,128)(2,1)S(1)} collective-permute-done((bf16[384,1024]{1,0:T(8,128)(2,1)S(1)}, bf16[384,1024]{1,0:T(8,128)(2,1)S(1)}, u32[]{:S(2)}, u32[]{:S(2)}) %collective-permute-start.10) | collective-permute-done | bytes 786464 | tf_op jit(solution)/shard_map/ppermute | solution.py:64
  90.3 19.4 %collective-permute-done.16.refs_6_.refs_12_.refs_8_.refs_14_ = bf16[512,1024]{1,0:T(8,128)(2,1)S(1)} collective-permute-done((bf16[512,1024]{1,0:T(8,128)(2,1)S(1)}, bf16[512,1024]{1,0:T(8,128)(2,1)S(1)}, u32[]{:S(2)}, u32[]{:S(2)}) %collective-permute-start.16) | collective-permute-done | bytes 1048608 | tf_op jit(solution)/shard_map/ppermute | solution.py:64
  116.3 18.1 %collective-permute-done.21.refs_14_.refs_5_.refs_4_.refs_16_ = bf16[512,1024]{1,0:T(8,128)(2,1)S(1)} collective-permute-done((bf16[512,1024]{1,0:T(8,128)(2,1)S(1)}, bf16[512,1024]{1,0:T(8,128)(2,1)S(1)}, u32[]{:S(2)}, u32[]{:S(2)}) %collective-permute-start.21) | collective-permute-done | bytes 1048608 | tf_op jit(solution)/shard_map/ppermute | solution.py:64
  136.8 2.4 collective-permute-start.23
  141.5 3.4 shard_map.246
  145.8 3.4 shard_map.247
  149.3 3.4 collective-permute-done.24.refs_7_.refs_6_
  162.1 8.9 %collective-permute-done.27 = bf16[96,2048]{1,0:T(8,128)(2,1)S(1)} collective-permute-done((bf16[96,2048]{1,0:T(8,128)(2,1)S(1)}, bf16[96,2048]{1,0:T(8,128)(2,1)S(1)}, u32[]{:S(2)}, u32[]{:S(2)}) %collective-permute-start.27) | collective-permute-done | bytes 393248 | tf_op jit(solution)/shard_map/ppermute | solution.py:40
  172.4 9.4 %collective-permute-done.29 = bf16[96,2048]{1,0:T(8,128)(2,1)S(1)} collective-permute-done((bf16[96,2048]{1,0:T(8,128)(2,1)S(1)}, bf16[96,2048]{1,0:T(8,128)(2,1)S(1)}, u32[]{:S(2)}, u32[]{:S(2)}) %collective-permute-start.29) | collective-permute-done | bytes 393248 | tf_op jit(solution)/shard_map/ppermute | solution.py:40
  188.4 7.0 %collective-permute-done.31.b1 = bf16[96,2048]{1,0:T(8,128)(2,1)S(1)} collective-permute-done((bf16[96,2048]{1,0:T(8,128)(2,1)S(1)}, bf16[96,2048]{1,0:T(8,128)(2,1)S(1)}, u32[]{:S(2)}, u32[]{:S(2)}) %collective-permute-start.31) | collective-permute-done | bytes 393248 | tf_op jit(solution)/shard_map/ppermute | solution.py:40
  195.4 5.5 %collective-permute-done.32.b2 = bf16[96,2048]{1,0:T(8,128)(2,1)S(1)} collective-permute-done((bf16[96,2048]{1,0:T(8,128)(2,1)S(1)}, bf16[96,2048]{1,0:T(8,128)(2,1)S(1)}, u32[]{:S(2)}, u32[]{:S(2)}) %collective-permute-start.32) | collective-permute-done | bytes 393248 | tf_op jit(solution)/shard_map/ppermute | solution.py:40
  209.7 2.3 shard_map.254
  215.4 3.4 shard_map.257
  219.4 3.4 shard_map.256.own_ref
  227.4 4.4 %collective-permute-start.40 = (bf16[384,1024]{1,0:T(8,128)(2,1)}, bf16[384,1024]{1,0:T(8,128)(2,1)S(1)}, u32[]{:S(2)}, u32[]{:S(2)}) collective-permute-start(bf16[384,1024]{1,0:T(8,128)(2,1)} %get-tuple-element.355), channel_id=1, source_target_pairs={{8,1},{1,9},{9,8},{10,3},{3,11},{11,10},{12,5},{5,13},{13,12},{14,... | collective-permute-start | bytes 2359304 | tf_op jit(solution)/shard_map/ppermute | solution.py:750
  233.7 8.5 %shard_map.259 = (bf16[512,1536]{1,0:T(8,128)(2,1)S(1)}, bf16[512,1536]{1,0:T(8,128)(2,1)S(1)}, bf16[512,1536]{1,0:T(8,128)(2,1)S(1)}, bf16[512,1536]{1,0:T(8,128)(2,1)}) custom-call(s32[16]{0:T(128)S(1)} %copy-done.58, bf16[384,2048]{1,0:T(8,128)(2,1)S(1)} %get-tuple-element.367.rows_ref.refs_1_, ...), custom_call_target="tpu_custom_call" | custom-call | tf_op jit(solution)/shard_map/pallas_call | solution.py:355
  243.4 3.7 collective-permute-done.39
  255.0 7.3 %shard_map.260 = (bf16[512,1536]{1,0:T(8,128)(2,1)S(1)}, bf16[512,768]{1,0:T(8,128)(2,1)S(1)}, bf16[512,768]{1,0:T(8,128)(2,1)S(1)}, bf16[512,1536]{1,0:T(8,128)...) custom-call(s32[16]{0:T(128)S(1)} %copy-done.58, ...), custom_call_target="tpu_custom_call" | custom-call | tf_op jit(solution)/shard_map/pallas_call | solution.py:355
  263.4 5.3 %collective-permute-done.43.g2 = bf16[96,2048]{1,0:T(8,128)(2,1)S(1)} collective-permute-done((bf16[96,2048]{1,0:T(8,128)(2,1)S(1)}, bf16[96,2048]{1,0:T(8,128)(2,1)S(1)}, u32[]{:S(2)}, u32[]{:S(2)}) %collective-permute-start.43) | collective-permute-done | bytes 393248 | tf_op jit(solution)/shard_map/ppermute | solution.py:40
  268.8 2.3 collective-permute-done.44.g3
  273.3 2.9 collective-permute-start.47
  280.4 7.9 %shard_map.262 = (f32[768,512]{1,0:T(8,128)S(1)}, bf16[768,256]{1,0:T(8,128)(2,1)S(1)}, f32[8,768]{1,0:T(8,128)S(1)}, f32[2,256]{1,0:T(2,128)S(1)}) custom-call(f32[768,768]{1,0:T(8,128)S(1)} %get-tuple-element.264.qkv_ref, f32[768,8]{1,0:T(8,128)S(1)} %get-tuple-element.360.scale_ref.rms_ref, f32[2,256]{1,0:T(2,128)S(1)} %copy-done.55, ...), custom_call_target="tpu_custom_call" | custom-call | tf_op jit(solution)/shard_map/pallas_call | solution.py:355
  298.6 4.1 collective-permute-done.51
  302.9 3.2 collective-permute-done.54
  316.6 2.9 collective-permute-start.59
  324.4 6.2 %shard_map.267 = (bf16[576,1024]{1,0:T(8,128)(2,1)S(1)}, bf16[576,1024]{1,0:T(8,128)(2,1)}, bf16[576,1024]{1,0:T(8,128)(2,1)}, bf16[576,1024]{1,0:T(8,128)(2,1)}) custom-call(s32[16]{0:T(128)S(1)} %copy-done.59, bf16[768,2048]{1,0:T(8,128)(2,1)S(1)} %shard_map.239.states_ref.refs_1_, bf16[768,768]{1,0:T(8,128)(2,1)S(1)} %copy-done.7, ...), custom_call_target="tpu_custom_call" | custom-call | tf_op jit(solution)/shard_map/pallas_call | solution.py:355
  331.6 9.2 %reduce-scatter.2.cloned.1.call-done = bf16[96,2048]{1,0:T(8,128)(2,1)} async-done(((bf16[384,2048]{1,0:T(8,128)(2,1)}), bf16[96,2048]{1,0:T(8,128)(2,1)}) %reduce-scatter.2.cloned.1.call-update) | async-done | bytes 393232 | tf_op jit(solution)/shard_map/reduce_scatter | solution.py:919
  342.9 4.5 %collective-permute-start.57 = (bf16[96,1024]{1,0:T(8,128)(2,1)S(1)}, bf16[96,1024]{1,0:T(8,128)(2,1)S(1)}, u32[]{:S(2)}, u32[]{:S(2)}) collective-permute-start(bf16[96,1024]{1,0:T(8,128)(2,1)S(1)} %get-tuple-element.487), channel_id=1, source_target_pairs={{8,1},{1,9},{9,8},{10,3},{3,11},{11,10},{12,5},{5,13},{13,12},{14,... | collective-permute-start | bytes 589832 | tf_op jit(solution)/shard_map/ppermute | solution.py:750
  350.2 3.8 shard_map.268
  354.1 6.1 %collective-permute-done.57 = bf16[96,1024]{1,0:T(8,128)(2,1)S(1)} collective-permute-done((bf16[96,1024]{1,0:T(8,128)(2,1)S(1)}, bf16[96,1024]{1,0:T(8,128)(2,1)S(1)}, u32[]{:S(2)}, u32[]{:S(2)}) %collective-permute-start.57) | collective-permute-done | bytes 196640 | tf_op jit(solution)/shard_map/ppermute | solution.py:750
  367.7 2.3 shard_map.269
  372.2 2.7 collective-permute-start.65
  375.1 17.2 %collective-permute-done.65.p3 = bf16[256,1536]{1,0:T(8,128)(2,1)S(1)} collective-permute-done((bf16[256,1536]{1,0:T(8,128)(2,1)S(1)}, bf16[256,1536]{1,0:T(8,128)(2,1)S(1)}, u32[]{:S(2)}, u32[]{:S(2)}) %collective-permute-start.65) | collective-permute-done | bytes 786464 | tf_op jit(solution)/shard_map/ppermute | solution.py:56
  392.3 3.8 collective-permute-done.64.p1
  399.3 3.6 collective-permute-start.70
  402.9 3.0 add_convert_fusion
  409.7 2.8 collective-permute-done.70.p2
  416.7 2.4 shard_map.271
  (390 shorter events, 164.3 us)
Async XLA Ops:
  7.2 333.5 %reduce-scatter.2.cloned.1.call-start = ((), (), s32[]{:S(2)}) async-start(), calls=%async_computation.1 | async-start | bytes 1966080 | tf_op jit(solution)/shard_map/reduce_scatter | solution.py:919
  7.2 17.2 %collective-permute-start = (s32[768]{0:T(1024)}, s32[768]{0:T(1024)S(1)}, u32[]{:S(2)}, u32[]{:S(2)}) collective-permute-start(s32[768]{0:T(1024)} %param.15), channel_id=1, source_target_pairs={{0,8},{8,0},{1,9},{9,1},{2,10},{10,2},{3,11},{11,3},{4,12},{12,4},... | collective-permute-start | bytes 9224 | tf_op jit(solution)/shard_map/ppermute | solution.py:60
  10.1 26.9 %collective-permute-start.1 = (f32[2560]{0:T(1024)}, f32[2560]{0:T(1024)}, u32[]{:S(2)}, u32[]{:S(2)}) collective-permute-start(f32[2560]{0:T(1024)} %pad_maximum_fusion.8), channel_id=1, source_target_pairs={{0,1},{1,0},{2,3},{3,2},{4,5},{5,4},{6,7},{7,6},{8,9},{9,8},{10,11... | collective-permute-start | bytes 30728 | tf_op jit(solution)/shard_map/ppermute | solution.py:64
  11.4 28.3 %collective-permute-start.2 = (bf16[768,1024]{1,0:T(8,128)(2,1)}, bf16[768,1024]{1,0:T(8,128)(2,1)S(1)}, u32[]{:S(2)}, u32[]{:S(2)}) collective-permute-start(bf16[768,1024]{1,0:T(8,128)(2,1)} %a_ref.2), channel_id=1, source_target_pairs={{0,8},{9,1},{8,9},{1,0},{2,10},{11,3},{10,11},{3,2},{4,12},{13,5},... | collective-permute-start | bytes 4718600 | tf_op jit(solution)/shard_map/ppermute | solution.py:126
  14.1 28.7 %collective-permute-start.3 = (bf16[768,768]{1,0:T(8,128)(2,1)}, bf16[768,768]{1,0:T(8,128)(2,1)S(1)}, u32[]{:S(2)}, u32[]{:S(2)}) collective-permute-start(bf16[768,768]{1,0:T(8,128)(2,1)} %get-tuple-element.247.refs_0_.refs_1_), channel_id=1, source_target_pairs={{0,17},{17,0},{1,16},{16,1},{2,19},{19,2},{3,18},{18,3},{4,21},{21... | collective-permute-start | bytes 3538952 | tf_op jit(solution)/shard_map/ppermute | solution.py:68
  16.1 23.5 %collective-permute-start.4 = (bf16[256,768]{1,0:T(8,128)(2,1)}, bf16[256,768]{1,0:T(8,128)(2,1)S(1)}, u32[]{:S(2)}, u32[]{:S(2)}) collective-permute-start(bf16[256,768]{1,0:T(8,128)(2,1)} %get-tuple-element.248.refs_1_.refs_2_), channel_id=1, source_target_pairs={{0,1},{1,0},{2,3},{3,2},{4,5},{5,4},{6,7},{7,6},{8,9},{9,8},{10,11... | collective-permute-start | bytes 1179656 | tf_op jit(solution)/shard_map/ppermute | solution.py:64
  62.5 18.7 %collective-permute-start.10 = (bf16[384,1024]{1,0:T(8,128)(2,1)S(1)}, bf16[384,1024]{1,0:T(8,128)(2,1)S(1)}, u32[]{:S(2)}, u32[]{:S(2)}) collective-permute-start(bf16[384,1024]{1,0:T(8,128)(2,1)S(1)} %copy-done.4), channel_id=1, source_target_pairs={{0,1},{1,0},{2,3},{3,2},{4,5},{5,4},{6,7},{7,6},{8,9},{9,8},{10,11... | collective-permute-start | bytes 2359304 | tf_op jit(solution)/shard_map/ppermute | solution.py:64
  62.9 19.3 %collective-permute-start.11 = (bf16[384,1024]{1,0:T(8,128)(2,1)S(1)}, bf16[384,1024]{1,0:T(8,128)(2,1)S(1)}, u32[]{:S(2)}, u32[]{:S(2)}) collective-permute-start(bf16[384,1024]{1,0:T(8,128)(2,1)S(1)} %copy-done.5), channel_id=1, source_target_pairs={{0,17},{17,0},{1,16},{16,1},{2,19},{19,2},{3,18},{18,3},{4,21},{21... | collective-permute-start | bytes 2359304 | tf_op jit(solution)/shard_map/ppermute | solution.py:68
  85.1 24.6 %collective-permute-start.16 = (bf16[512,1024]{1,0:T(8,128)(2,1)S(1)}, bf16[512,1024]{1,0:T(8,128)(2,1)S(1)}, u32[]{:S(2)}, u32[]{:S(2)}) collective-permute-start(bf16[512,1024]{1,0:T(8,128)(2,1)S(1)} %copy-done), channel_id=1, source_target_pairs={{0,1},{1,0},{2,3},{3,2},{4,5},{5,4},{6,7},{7,6},{8,9},{9,8},{10,11... | collective-permute-start | bytes 3145736 | tf_op jit(solution)/shard_map/ppermute | solution.py:64
  85.4 25.5 %collective-permute-start.17 = (bf16[512,1024]{1,0:T(8,128)(2,1)S(1)}, bf16[512,1024]{1,0:T(8,128)(2,1)S(1)}, u32[]{:S(2)}, u32[]{:S(2)}) collective-permute-start(bf16[512,1024]{1,0:T(8,128)(2,1)S(1)} %copy-done.1), channel_id=1, source_target_pairs={{0,17},{17,0},{1,16},{16,1},{2,19},{19,2},{3,18},{18,3},{4,21},{21... | collective-permute-start | bytes 3145736 | tf_op jit(solution)/shard_map/ppermute | solution.py:68
  88.8 24.3 %collective-permute-start.13 = (bf16[96,2048]{1,0:T(8,128)(2,1)S(1)}, bf16[96,2048]{1,0:T(8,128)(2,1)S(1)}, u32[]{:S(2)}, u32[]{:S(2)}) collective-permute-start(bf16[96,2048]{1,0:T(8,128)(2,1)S(1)} %get-tuple-element.278), channel_id=1, source_target_pairs={{0,6},{2,0},{4,2},{6,4},{1,7},{3,1},{5,3},{7,5},{8,14},{10,8},{12,... | collective-permute-start | bytes 1179656 | tf_op jit(solution)/shard_map/ppermute | solution.py:40
  89.0 24.1 %collective-permute-start.14 = (bf16[96,2048]{1,0:T(8,128)(2,1)S(1)}, bf16[96,2048]{1,0:T(8,128)(2,1)S(1)}, u32[]{:S(2)}, u32[]{:S(2)}) collective-permute-start(bf16[96,2048]{1,0:T(8,128)(2,1)S(1)} %get-tuple-element.279), channel_id=1, source_target_pairs={{0,4},{2,6},{4,0},{6,2},{1,5},{3,7},{5,1},{7,3},{8,12},{10,14},{12... | collective-permute-start | bytes 1179656 | tf_op jit(solution)/shard_map/ppermute | solution.py:40
  89.0 24.1 %collective-permute-start.15 = (bf16[96,2048]{1,0:T(8,128)(2,1)S(1)}, bf16[96,2048]{1,0:T(8,128)(2,1)S(1)}, u32[]{:S(2)}, u32[]{:S(2)}) collective-permute-start(bf16[96,2048]{1,0:T(8,128)(2,1)S(1)} %get-tuple-element.280), channel_id=1, source_target_pairs={{0,2},{2,4},{4,6},{6,0},{1,3},{3,5},{5,7},{7,1},{8,10},{10,12},{12... | collective-permute-start | bytes 1179656 | tf_op jit(solution)/shard_map/ppermute | solution.py:40
  110.9 23.4 %collective-permute-start.21 = (bf16[512,1024]{1,0:T(8,128)(2,1)S(1)}, bf16[512,1024]{1,0:T(8,128)(2,1)S(1)}, u32[]{:S(2)}, u32[]{:S(2)}) collective-permute-start(bf16[512,1024]{1,0:T(8,128)(2,1)S(1)} %copy-done.2), channel_id=1, source_target_pairs={{0,1},{1,0},{2,3},{3,2},{4,5},{5,4},{6,7},{7,6},{8,9},{9,8},{10,11... | collective-permute-start | bytes 3145736 | tf_op jit(solution)/shard_map/ppermute | solution.py:64
  111.2 24.4 %collective-permute-start.22 = (bf16[512,1024]{1,0:T(8,128)(2,1)S(1)}, bf16[512,1024]{1,0:T(8,128)(2,1)S(1)}, u32[]{:S(2)}, u32[]{:S(2)}) collective-permute-start(bf16[512,1024]{1,0:T(8,128)(2,1)S(1)} %copy-done.3), channel_id=1, source_target_pairs={{0,17},{17,0},{1,16},{16,1},{2,19},{19,2},{3,18},{18,3},{4,21},{21... | collective-permute-start | bytes 3145736 | tf_op jit(solution)/shard_map/ppermute | solution.py:68
  113.3 22.3 %collective-permute-start.18 = (bf16[96,2048]{1,0:T(8,128)(2,1)S(1)}, bf16[96,2048]{1,0:T(8,128)(2,1)S(1)}, u32[]{:S(2)}, u32[]{:S(2)}) collective-permute-start(bf16[96,2048]{1,0:T(8,128)(2,1)S(1)} %add_convert_fusion.3.b0.a0), channel_id=1, source_target_pairs={{0,2},{2,4},{4,6},{6,0},{1,3},{3,5},{5,7},{7,1},{8,10},{10,12},{12... | collective-permute-start | bytes 1179656 | tf_op jit(solution)/shard_map/ppermute | solution.py:40
  113.4 22.2 %collective-permute-start.19 = (bf16[96,2048]{1,0:T(8,128)(2,1)S(1)}, bf16[96,2048]{1,0:T(8,128)(2,1)S(1)}, u32[]{:S(2)}, u32[]{:S(2)}) collective-permute-start(bf16[96,2048]{1,0:T(8,128)(2,1)S(1)} %add_convert_fusion.3.b0.a0), channel_id=1, source_target_pairs={{0,4},{2,6},{4,0},{6,2},{1,5},{3,7},{5,1},{7,3},{8,12},{10,14},{12... | collective-permute-start | bytes 1179656 | tf_op jit(solution)/shard_map/ppermute | solution.py:40
  114.7 20.9 %collective-permute-start.20 = (bf16[96,2048]{1,0:T(8,128)(2,1)S(1)}, bf16[96,2048]{1,0:T(8,128)(2,1)S(1)}, u32[]{:S(2)}, u32[]{:S(2)}) collective-permute-start(bf16[96,2048]{1,0:T(8,128)(2,1)S(1)} %add_convert_fusion.3.b0.a0), channel_id=1, source_target_pairs={{0,6},{2,0},{4,2},{6,4},{1,7},{3,1},{5,3},{7,5},{8,14},{10,8},{12,... | collective-permute-start | bytes 1179656 | tf_op jit(solution)/shard_map/ppermute | solution.py:40
  139.3 13.5 %collective-permute-start.24 = (bf16[256,1024]{1,0:T(8,128)(2,1)S(1)}, bf16[256,1024]{1,0:T(8,128)(2,1)S(1)}, u32[]{:S(2)}, u32[]{:S(2)}) collective-permute-start(bf16[256,1024]{1,0:T(8,128)(2,1)S(1)} %copy-done.13), channel_id=1, source_target_pairs={{0,1},{1,0},{2,3},{3,2},{4,5},{5,4},{6,7},{7,6},{8,9},{9,8},{10,11... | collective-permute-start | bytes 1572872 | tf_op jit(solution)/shard_map/ppermute | solution.py:64
  139.3 14.6 %collective-permute-start.25 = (bf16[256,1024]{1,0:T(8,128)(2,1)S(1)}, bf16[256,1024]{1,0:T(8,128)(2,1)S(1)}, u32[]{:S(2)}, u32[]{:S(2)}) collective-permute-start(bf16[256,1024]{1,0:T(8,128)(2,1)S(1)} %copy-done.14), channel_id=1, source_target_pairs={{0,17},{17,0},{1,16},{16,1},{2,19},{19,2},{3,18},{18,3},{4,21},{21... | collective-permute-start | bytes 1572872 | tf_op jit(solution)/shard_map/ppermute | solution.py:68
  160.4 21.6 %collective-permute-start.30 = (bf16[768,1024]{1,0:T(8,128)(2,1)S(1)}, bf16[768,1024]{1,0:T(8,128)(2,1)S(1)}, u32[]{:S(2)}, u32[]{:S(2)}) collective-permute-start(bf16[768,1024]{1,0:T(8,128)(2,1)S(1)} %copy-done.29), channel_id=1, source_target_pairs={{0,8},{9,1},{8,9},{1,0},{2,10},{11,3},{10,11},{3,2},{4,12},{13,5},... | collective-permute-start | bytes 4718600 | tf_op jit(solution)/shard_map/ppermute | solution.py:126
  160.8 21.0 %collective-permute-start.29 = (bf16[96,2048]{1,0:T(8,128)(2,1)S(1)}, bf16[96,2048]{1,0:T(8,128)(2,1)S(1)}, u32[]{:S(2)}, u32[]{:S(2)}) collective-permute-start(bf16[96,2048]{1,0:T(8,128)(2,1)S(1)} %get-tuple-element.319), channel_id=1, source_target_pairs={{0,2},{2,4},{4,6},{6,0},{1,3},{3,5},{5,7},{7,1},{8,10},{10,12},{12... | collective-permute-start | bytes 1179656 | tf_op jit(solution)/shard_map/ppermute | solution.py:40
  183.4 17.6 %collective-permute-start.32 = (bf16[96,2048]{1,0:T(8,128)(2,1)S(1)}, bf16[96,2048]{1,0:T(8,128)(2,1)S(1)}, u32[]{:S(2)}, u32[]{:S(2)}) collective-permute-start(bf16[96,2048]{1,0:T(8,128)(2,1)S(1)} %add_convert_fusion.2.b0), channel_id=1, source_target_pairs={{0,4},{2,6},{4,0},{6,2},{1,5},{3,7},{5,1},{7,3},{8,12},{10,14},{12... | collective-permute-start | bytes 1179656 | tf_op jit(solution)/shard_map/ppermute | solution.py:40
  184.6 18.3 %collective-permute-start.33 = (bf16[96,2048]{1,0:T(8,128)(2,1)S(1)}, bf16[96,2048]{1,0:T(8,128)(2,1)S(1)}, u32[]{:S(2)}, u32[]{:S(2)}) collective-permute-start(bf16[96,2048]{1,0:T(8,128)(2,1)S(1)} %add_convert_fusion.2.b0), channel_id=1, source_target_pairs={{0,6},{2,0},{4,2},{6,4},{1,7},{3,1},{5,3},{7,5},{8,14},{10,8},{12,... | collective-permute-start | bytes 1179656 | tf_op jit(solution)/shard_map/ppermute | solution.py:40
  224.6 18.8 %collective-permute-start.37 = (bf16[96,2048]{1,0:T(8,128)(2,1)S(1)}, bf16[96,2048]{1,0:T(8,128)(2,1)S(1)}, u32[]{:S(2)}, u32[]{:S(2)}) collective-permute-start(bf16[96,2048]{1,0:T(8,128)(2,1)S(1)} %get-tuple-element.346), channel_id=1, source_target_pairs={{0,6},{2,0},{4,2},{6,4},{1,7},{3,1},{5,3},{7,5},{8,14},{10,8},{12,... | collective-permute-start | bytes 1179656 | tf_op jit(solution)/shard_map/ppermute | solution.py:40
  226.7 16.6 %collective-permute-start.38 = (bf16[96,2048]{1,0:T(8,128)(2,1)S(1)}, bf16[96,2048]{1,0:T(8,128)(2,1)S(1)}, u32[]{:S(2)}, u32[]{:S(2)}) collective-permute-start(bf16[96,2048]{1,0:T(8,128)(2,1)S(1)} %get-tuple-element.347), channel_id=1, source_target_pairs={{0,4},{2,6},{4,0},{6,2},{1,5},{3,7},{5,1},{7,3},{8,12},{10,14},{12... | collective-permute-start | bytes 1179656 | tf_op jit(solution)/shard_map/ppermute | solution.py:40
  226.7 20.4 %collective-permute-start.39 = (bf16[96,2048]{1,0:T(8,128)(2,1)S(1)}, bf16[96,2048]{1,0:T(8,128)(2,1)S(1)}, u32[]{:S(2)}, u32[]{:S(2)}) collective-permute-start(bf16[96,2048]{1,0:T(8,128)(2,1)S(1)} %get-tuple-element.348), channel_id=1, source_target_pairs={{0,2},{2,4},{4,6},{6,0},{1,3},{3,5},{5,7},{7,1},{8,10},{10,12},{12... | collective-permute-start | bytes 1179656 | tf_op jit(solution)/shard_map/ppermute | solution.py:40
  227.4 19.9 %collective-permute-start.40 = (bf16[384,1024]{1,0:T(8,128)(2,1)}, bf16[384,1024]{1,0:T(8,128)(2,1)S(1)}, u32[]{:S(2)}, u32[]{:S(2)}) collective-permute-start(bf16[384,1024]{1,0:T(8,128)(2,1)} %get-tuple-element.355), channel_id=1, source_target_pairs={{8,1},{1,9},{9,8},{10,3},{3,11},{11,10},{12,5},{5,13},{13,12},{14,... | collective-permute-start | bytes 2359304 | tf_op jit(solution)/shard_map/ppermute | solution.py:750
  231.7 17.1 %collective-permute-start.41 = (bf16[384,1024]{1,0:T(8,128)(2,1)}, bf16[384,1024]{1,0:T(8,128)(2,1)S(1)}, u32[]{:S(2)}, u32[]{:S(2)}) collective-permute-start(bf16[384,1024]{1,0:T(8,128)(2,1)} %get-tuple-element.356), channel_id=1, source_target_pairs={{0,1},{8,0},{1,8},{2,3},{10,2},{3,10},{4,5},{12,4},{5,12},{6,7},{1... | collective-permute-start | bytes 2359304 | tf_op jit(solution)/shard_map/ppermute | solution.py:750
  248.9 22.2 %collective-permute-start.46 = (bf16[512,1536]{1,0:T(8,128)(2,1)}, bf16[512,1536]{1,0:T(8,128)(2,1)S(1)}, u32[]{:S(2)}, u32[]{:S(2)}) collective-permute-start(bf16[512,1536]{1,0:T(8,128)(2,1)} %get-tuple-element.366), channel_id=1, source_target_pairs={{0,96},{8,25},{1,97},{9,8},{16,112},{24,9},{17,113},{25,24},{32,0}... | collective-permute-start | bytes 4718600 | tf_op jit(solution)/shard_map/ppermute | solution.py:56
  250.8 20.8 %collective-permute-start.45 = (bf16[512,1536]{1,0:T(8,128)(2,1)S(1)}, bf16[512,1536]{1,0:T(8,128)(2,1)S(1)}, u32[]{:S(2)}, u32[]{:S(2)}) collective-permute-start(bf16[512,1536]{1,0:T(8,128)(2,1)S(1)} %get-tuple-element.364), channel_id=1, source_target_pairs={{0,32},{8,9},{1,33},{9,24},{16,48},{24,25},{17,49},{25,8},{32,64},... | collective-permute-start | bytes 4718600 | tf_op jit(solution)/shard_map/ppermute | solution.py:56
  250.8 12.6 %collective-permute-start.42 = (bf16[96,2048]{1,0:T(8,128)(2,1)S(1)}, bf16[96,2048]{1,0:T(8,128)(2,1)S(1)}, u32[]{:S(2)}, u32[]{:S(2)}) collective-permute-start(bf16[96,2048]{1,0:T(8,128)(2,1)S(1)} %fusion.1.g0), channel_id=1, source_target_pairs={{0,2},{2,4},{4,6},{6,0},{1,3},{3,5},{5,7},{7,1},{8,10},{10,12},{12... | collective-permute-start | bytes 1179656 | tf_op jit(solution)/shard_map/ppermute | solution.py:40
  252.4 16.4 %collective-permute-start.43 = (bf16[96,2048]{1,0:T(8,128)(2,1)S(1)}, bf16[96,2048]{1,0:T(8,128)(2,1)S(1)}, u32[]{:S(2)}, u32[]{:S(2)}) collective-permute-start(bf16[96,2048]{1,0:T(8,128)(2,1)S(1)} %fusion.1.g0), channel_id=1, source_target_pairs={{0,4},{2,6},{4,0},{6,2},{1,5},{3,7},{5,1},{7,3},{8,12},{10,14},{12... | collective-permute-start | bytes 1179656 | tf_op jit(solution)/shard_map/ppermute | solution.py:40
  253.6 17.5 %collective-permute-start.44 = (bf16[96,2048]{1,0:T(8,128)(2,1)S(1)}, bf16[96,2048]{1,0:T(8,128)(2,1)S(1)}, u32[]{:S(2)}, u32[]{:S(2)}) collective-permute-start(bf16[96,2048]{1,0:T(8,128)(2,1)S(1)} %fusion.1.g0), channel_id=1, source_target_pairs={{0,6},{2,0},{4,2},{6,4},{1,7},{3,1},{5,3},{7,5},{8,14},{10,8},{12,... | collective-permute-start | bytes 1179656 | tf_op jit(solution)/shard_map/ppermute | solution.py:40
  276.2 13.4 %collective-permute-start.48 = (bf16[512,768]{1,0:T(8,128)(2,1)S(1)}, bf16[512,768]{1,0:T(8,128)(2,1)S(1)}, u32[]{:S(2)}, u32[]{:S(2)}) collective-permute-start(bf16[512,768]{1,0:T(8,128)(2,1)S(1)} %get-tuple-element.394), channel_id=1, source_target_pairs={{0,32},{8,9},{1,33},{9,24},{16,48},{24,25},{17,49},{25,8},{32,64},... | collective-permute-start | bytes 2359304 | tf_op jit(solution)/shard_map/ppermute | solution.py:56
  292.9 13.2 %collective-permute-start.54 = (bf16[512,768]{1,0:T(8,128)(2,1)S(1)}, bf16[512,768]{1,0:T(8,128)(2,1)S(1)}, u32[]{:S(2)}, u32[]{:S(2)}) collective-permute-start(bf16[512,768]{1,0:T(8,128)(2,1)S(1)} %get-tuple-element.400), channel_id=1, source_target_pairs={{0,32},{8,9},{1,33},{9,24},{16,48},{24,25},{17,49},{25,8},{32,64},... | collective-permute-start | bytes 2359304 | tf_op jit(solution)/shard_map/ppermute | solution.py:56
  314.0 101.3 %all-gather.2.cloned.1.call-start = ((), (), s32[]{:S(2)}) async-start(), calls=%async_computation.2 | async-start | bytes 1966080 | tf_op jit(solution)/shard_map/all_gather | solution.py:935
  316.6 44.4 %collective-permute-start.59 = (bf16[512,1536]{1,0:T(8,128)(2,1)}, bf16[512,1536]{1,0:T(8,128)(2,1)}, u32[]{:S(2)}, u32[]{:S(2)}) collective-permute-start(bf16[512,1536]{1,0:T(8,128)(2,1)} %copy-done.62), channel_id=1, source_target_pairs={{0,64},{8,24},{1,65},{9,25},{16,80},{24,8},{17,81},{25,9},{32,96},... | collective-permute-start | bytes 4718600 | tf_op jit(solution)/shard_map/ppermute | solution.py:56
  319.5 41.5 %collective-permute-start.60 = (bf16[512,1536]{1,0:T(8,128)(2,1)}, bf16[512,1536]{1,0:T(8,128)(2,1)}, u32[]{:S(2)}, u32[]{:S(2)}) collective-permute-start(bf16[512,1536]{1,0:T(8,128)(2,1)} %copy-done.63), channel_id=1, source_target_pairs={{0,64},{8,24},{1,65},{9,25},{16,80},{24,8},{17,81},{25,9},{32,96},... | collective-permute-start | bytes 4718600 | tf_op jit(solution)/shard_map/ppermute | solution.py:56
  342.9 17.3 %collective-permute-start.57 = (bf16[96,1024]{1,0:T(8,128)(2,1)S(1)}, bf16[96,1024]{1,0:T(8,128)(2,1)S(1)}, u32[]{:S(2)}, u32[]{:S(2)}) collective-permute-start(bf16[96,1024]{1,0:T(8,128)(2,1)S(1)} %get-tuple-element.487), channel_id=1, source_target_pairs={{8,1},{1,9},{9,8},{10,3},{3,11},{11,10},{12,5},{5,13},{13,12},{14,... | collective-permute-start | bytes 589832 | tf_op jit(solution)/shard_map/ppermute | solution.py:750
  347.4 12.8 %collective-permute-start.58 = (bf16[96,1024]{1,0:T(8,128)(2,1)S(1)}, bf16[96,1024]{1,0:T(8,128)(2,1)S(1)}, u32[]{:S(2)}, u32[]{:S(2)}) collective-permute-start(bf16[96,1024]{1,0:T(8,128)(2,1)S(1)} %get-tuple-element.488), channel_id=1, source_target_pairs={{0,1},{8,0},{1,8},{2,3},{10,2},{3,10},{4,5},{12,4},{5,12},{6,7},{1... | collective-permute-start | bytes 589832 | tf_op jit(solution)/shard_map/ppermute | solution.py:750
  361.0 35.2 %collective-permute-start.61 = (bf16[576,1024]{1,0:T(8,128)(2,1)}, bf16[576,1024]{1,0:T(8,128)(2,1)}, u32[]{:S(2)}, u32[]{:S(2)}) collective-permute-start(bf16[576,1024]{1,0:T(8,128)(2,1)} %get-tuple-element.436), channel_id=1, source_target_pairs={{0,32},{8,9},{1,33},{9,24},{16,48},{24,25},{17,49},{25,8},{32,64},... | collective-permute-start | bytes 3538952 | tf_op jit(solution)/shard_map/ppermute | solution.py:56
  361.0 36.2 %collective-permute-start.62 = (bf16[576,1024]{1,0:T(8,128)(2,1)}, bf16[576,1024]{1,0:T(8,128)(2,1)}, u32[]{:S(2)}, u32[]{:S(2)}) collective-permute-start(bf16[576,1024]{1,0:T(8,128)(2,1)} %get-tuple-element.437), channel_id=1, source_target_pairs={{0,64},{8,24},{1,65},{9,25},{16,80},{24,8},{17,81},{25,9},{32,96},... | collective-permute-start | bytes 3538952 | tf_op jit(solution)/shard_map/ppermute | solution.py:56
  362.3 37.0 %collective-permute-start.63 = (bf16[576,1024]{1,0:T(8,128)(2,1)}, bf16[576,1024]{1,0:T(8,128)(2,1)}, u32[]{:S(2)}, u32[]{:S(2)}) collective-permute-start(bf16[576,1024]{1,0:T(8,128)(2,1)} %get-tuple-element.438), channel_id=1, source_target_pairs={{0,96},{8,25},{1,97},{9,8},{16,112},{24,9},{17,113},{25,24},{32,0}... | collective-permute-start | bytes 3538952 | tf_op jit(solution)/shard_map/ppermute | solution.py:56
  372.2 20.1 %collective-permute-start.65 = (bf16[256,1536]{1,0:T(8,128)(2,1)S(1)}, bf16[256,1536]{1,0:T(8,128)(2,1)S(1)}, u32[]{:S(2)}, u32[]{:S(2)}) collective-permute-start(bf16[256,1536]{1,0:T(8,128)(2,1)S(1)} %pad_maximum_fusion.4), channel_id=1, source_target_pairs={{0,17},{8,104},{1,0},{9,105},{16,1},{24,120},{17,16},{25,121},{32,... | collective-permute-start | bytes 2359304 | tf_op jit(solution)/shard_map/ppermute | solution.py:56
  375.0 21.2 %collective-permute-start.64 = (bf16[256,1536]{1,0:T(8,128)(2,1)S(1)}, bf16[256,1536]{1,0:T(8,128)(2,1)S(1)}, u32[]{:S(2)}, u32[]{:S(2)}) collective-permute-start(bf16[256,1536]{1,0:T(8,128)(2,1)S(1)} %pad_maximum_fusion.3), channel_id=1, source_target_pairs={{0,1},{8,40},{1,16},{9,41},{16,17},{24,56},{17,0},{25,57},{32,33},... | collective-permute-start | bytes 2359304 | tf_op jit(solution)/shard_map/ppermute | solution.py:56
  399.3 13.2 %collective-permute-start.70 = (bf16[256,1536]{1,0:T(8,128)(2,1)S(1)}, bf16[256,1536]{1,0:T(8,128)(2,1)S(1)}, u32[]{:S(2)}, u32[]{:S(2)}) collective-permute-start(bf16[256,1536]{1,0:T(8,128)(2,1)S(1)} %pad_maximum_fusion.6), channel_id=1, source_target_pairs={{0,16},{8,72},{1,17},{9,73},{16,0},{24,88},{17,1},{25,89},{32,48},... | collective-permute-start | bytes 2359304 | tf_op jit(solution)/shard_map/ppermute | solution.py:56
  406.9 12.2 %collective-permute-start.66 = (bf16[144,1024]{1,0:T(8,128)(2,1)}, bf16[144,1024]{1,0:T(8,128)(2,1)}, u32[]{:S(2)}, u32[]{:S(2)}) collective-permute-start(bf16[144,1024]{1,0:T(8,128)(2,1)} %get-tuple-element.486), channel_id=1, source_target_pairs={{0,1},{8,40},{1,16},{9,41},{16,17},{24,56},{17,0},{25,57},{32,33},... | collective-permute-start | bytes 884744 | tf_op jit(solution)/shard_map/ppermute | solution.py:56
  (110 other events, 886.9 us)
Sparse Core Ops, SparseCore 0:
  314.1 26.5 reduce-scatter.1
  364.4 26.3 all-gather.1
